TPU v7x, 128 devices: a whole 4x4x4 slice. The times are simulated.
128 devices in a mesh: lat: 8 (over x, y_hi), lon: 16 (over z, y_lo, core).
Axes of the slice: x: 4, y: 4 (y_hi: 2, y_lo: 2; y = y_hi * 2 + y_lo), z: 4, core: 2. Of those that a mesh axis runs over, the one named last changes fastest.
Arguments:
- stash_input: int32 [48, 32, 7200], P(None, 'lat', 'lon'), may hold values from 0 to 255
- input_low: bfloat16 [3, 32, 7200], P(None, 'lat', 'lon'), as said below
- input_high: bfloat16 [3, 32, 7200], P(None, 'lat', 'lon'), as said below
- stash_hidden: int32 [192, 32, 7200], P(None, 'lat', 'lon'), may hold values from 0 to 255
- hidden_low: bfloat16 [12, 32, 7200], P(None, 'lat', 'lon'), as said below
- hidden_high: bfloat16 [12, 32, 7200], P(None, 'lat', 'lon'), as said below
- grad_out: bfloat16 [192, 32, 7200], P(None, 'lat', 'lon'), may hold values from -6 to 6
- kernel: float32 [192, 7, 7], replicated, may hold values from -0.875 to 0.875
- conv_bias: float32 [192], replicated, may hold values from -3 to 3
- norm_gain: float32 [192], replicated, may hold values from 0.25 to 1.75
- norm_bias: float32 [192], replicated, may hold values from -3 to 3
- w_in: bfloat16 [192, 768], replicated, may hold values from -0.4375 to 0.4375
- w_out: bfloat16 [768, 192], replicated, may hold values from -0.21875 to 0.21875
- out_bias: float32 [192], replicated, may hold values from -4 to 4
- layer_scale: float32 [192], replicated, may hold values from 0.5 to 1.5
Outputs:
- grad_input: bfloat16 [192, 32, 7200], P(None, 'lat', 'lon')
- grad_kernel: float32 [192, 7, 7], replicated
- grad_conv_bias: float32 [192], replicated
- grad_norm_gain: float32 [192], replicated
- grad_norm_bias: float32 [192], replicated
- grad_w_in: float32 [192, 768], replicated
- grad_w_out: float32 [768, 192], replicated
- grad_out_bias: float32 [192], replicated
- grad_layer_scale: float32 [192], replicated
Inputs may be any that keep to these rules, and one draw needn't show every extreme that they name: `stash_input`: each word packs four 2-bit codes in its low eight bits. `stash_hidden`: each word packs four 2-bit codes in its low eight bits. `input_low`: below input_high at every entry. `input_high`: above input_low at every entry. `hidden_low`: below hidden_high at every entry. `hidden_high`: above hidden_low at every entry.
All inputs are finite; a program needn't handle non-finite values.
Results may differ from a plain program's by a relative error of at most 0.008.
Values may be sent and summed in bfloat16 or wider, within the bound.
No kernel may reach another device: no remote copies, remote signals or barrier semaphores. Data moves between devices by JAX's collectives and lax.ppermute only.
A program may use at most 128 MiB of HBM per device.

v0:
```python
import math

import jax
import jax.numpy as jnp
from jax import lax
from jax.sharding import PartitionSpec as P

GROUP = 64
RADIUS = 3


def padded_2(cells, sides, width, closed):
    for axis, dim in sides:
        count = lax.axis_size(axis)
        ends = count if closed else count - 1
        head = lax.slice_in_dim(cells, 0, width, axis=dim)
        tail = lax.slice_in_dim(cells, cells.shape[dim] - width, cells.shape[dim], axis=dim)
        cells = jnp.concatenate(
            [
                lax.ppermute(tail, axis, [(i, (i + 1) % count) for i in range(ends)]),
                cells,
                lax.ppermute(head, axis, [((i + 1) % count, i) for i in range(ends)]),
            ],
            axis=dim,
        )
    return cells


def restore(packed, lowest, highest):
    pieces = [jnp.bitwise_and(jnp.right_shift(packed, 2 * bit_pair), 3) for bit_pair in range(4)]
    symbols = (
        jnp.stack(pieces, axis=1)
        .reshape((packed.shape[0] * 4,) + packed.shape[1:])
        .astype(jnp.float32)
    )
    bottom = jnp.repeat(lowest.astype(jnp.float32), GROUP, axis=0)
    summit = jnp.repeat(highest.astype(jnp.float32), GROUP, axis=0)
    return bottom + symbols * (summit - bottom) / 3.0


def extend(field):
    wider = padded_2(field, (("lon", 2),), RADIUS, True)
    return padded_2(wider, (("lat", 1),), RADIUS, False)


def forward_taps(padded, kernel, rows, cols):
    total = jnp.zeros((padded.shape[0], rows, cols), jnp.float32)
    for row_tap in range(2 * RADIUS + 1):
        for col_tap in range(2 * RADIUS + 1):
            total = (
                total
                + kernel[:, row_tap, col_tap][:, None, None]
                * padded[:, row_tap : row_tap + rows, col_tap : col_tap + cols]
            )
    return total


def backward_taps(padded, kernel, rows, cols):
    total = jnp.zeros((padded.shape[0], rows, cols), jnp.float32)
    for row_tap in range(2 * RADIUS + 1):
        for col_tap in range(2 * RADIUS + 1):
            row_start = 2 * RADIUS - row_tap
            col_start = 2 * RADIUS - col_tap
            total = (
                total
                + kernel[:, row_tap, col_tap][:, None, None]
                * padded[:, row_start : row_start + rows, col_start : col_start + cols]
            )
    return total


def tap_products(grad_field, padded, rows, cols):
    outer = []
    for row_tap in range(2 * RADIUS + 1):
        inner = [
            jnp.sum(
                grad_field * padded[:, row_tap : row_tap + rows, col_tap : col_tap + cols],
                axis=(1, 2),
            )
            for col_tap in range(2 * RADIUS + 1)
        ]
        outer.append(jnp.stack(inner, axis=1))
    return jnp.stack(outer, axis=1)


def block_backward(
    conv_out, hidden_pre, grad_block, norm_gain, norm_bias, w_in, w_out, out_bias, layer_scale
):
    channels, rows, cols = conv_out.shape
    count = rows * cols
    flat_conv = conv_out.reshape(channels, count)
    mean_val = jnp.mean(flat_conv, axis=0)
    centered = flat_conv - mean_val
    variance = jnp.mean(centered * centered, axis=0)
    inv_std = lax.rsqrt(variance + 1e-06)
    normed = centered * inv_std
    normed_in = (normed * norm_gain[:, None] + norm_bias[:, None]).astype(jnp.bfloat16)
    hidden = hidden_pre.reshape(hidden_pre.shape[0], count)
    cdf = 0.5 * (1.0 + jax.scipy.special.erf(hidden * 0.7071067811865476))
    density = jnp.exp(-0.5 * hidden * hidden) * 0.3989422804014327
    active = (hidden * cdf).astype(jnp.bfloat16)
    grad_flat = grad_block.reshape(channels, count).astype(jnp.float32)
    scaled = layer_scale[:, None] * grad_flat
    scaled_in = scaled.astype(jnp.bfloat16)
    contract_cells = (((1,), (1,)), ((), ()))
    grad_w_out = lax.dot_general(
        active, scaled_in, contract_cells, preferred_element_type=jnp.float32
    )
    grad_active = jnp.dot(w_out, scaled_in, preferred_element_type=jnp.float32)
    grad_hidden = (grad_active * (cdf + hidden * density)).astype(jnp.bfloat16)
    grad_w_in = lax.dot_general(
        normed_in, grad_hidden, contract_cells, preferred_element_type=jnp.float32
    )
    grad_normed = jnp.dot(w_in, grad_hidden, preferred_element_type=jnp.float32)
    recomputed = (
        lax.dot_general(w_out, active, (((0,), (0,)), ((), ())), preferred_element_type=jnp.float32)
        + out_bias[:, None]
    )
    grad_scale = jnp.sum(grad_flat * recomputed, axis=1)
    grad_obias = jnp.sum(scaled, axis=1)
    grad_gain = jnp.sum(grad_normed * normed, axis=1)
    grad_nbias = jnp.sum(grad_normed, axis=1)
    grad_dn = grad_normed * norm_gain[:, None]
    grad_conv = inv_std * (
        grad_dn - jnp.mean(grad_dn, axis=0) - normed * jnp.mean(grad_dn * normed, axis=0)
    )
    grad_conv = grad_conv.astype(jnp.bfloat16).reshape(channels, rows, cols)
    return (grad_conv, (grad_w_in, grad_w_out, grad_obias, grad_scale, grad_gain, grad_nbias))


def local(
    stash_input,
    input_low,
    input_high,
    stash_hidden,
    hidden_low,
    hidden_high,
    grad_out,
    kernel,
    conv_bias,
    norm_gain,
    norm_bias,
    w_in,
    w_out,
    out_bias,
    layer_scale,
):
    channels, rows, cols = grad_out.shape
    restored = restore(stash_input, input_low, input_high).astype(jnp.bfloat16)
    padded_in = extend(restored).astype(jnp.float32)
    conv_out = forward_taps(padded_in, kernel, rows, cols) + conv_bias[:, None, None]
    hidden_pre = restore(stash_hidden, hidden_low, hidden_high)
    grad_conv, parts = block_backward(
        conv_out, hidden_pre, grad_out, norm_gain, norm_bias, w_in, w_out, out_bias, layer_scale
    )
    grad_w_in, grad_w_out, grad_obias, grad_scale, grad_gain, grad_nbias = parts
    padded_grad = extend(grad_conv).astype(jnp.float32)
    grad_input = (
        grad_out.astype(jnp.float32) + backward_taps(padded_grad, kernel, rows, cols)
    ).astype(jnp.bfloat16)
    own_grad = grad_conv.astype(jnp.float32)
    grad_kernel = tap_products(own_grad, padded_in, rows, cols)
    grad_cbias = jnp.sum(own_grad, axis=(1, 2))
    (
        grad_w_in,
        grad_w_out,
        grad_obias,
        grad_scale,
        grad_gain,
        grad_nbias,
        grad_kernel,
        grad_cbias,
    ) = lax.psum(
        (
            grad_w_in,
            grad_w_out,
            grad_obias,
            grad_scale,
            grad_gain,
            grad_nbias,
            grad_kernel,
            grad_cbias,
        ),
        ("lat", "lon"),
    )
    factor = 1.0 / math.sqrt(rows * lax.axis_size("lat") * cols * lax.axis_size("lon"))
    return (
        grad_input,
        grad_kernel * factor,
        grad_cbias * factor,
        grad_gain * factor,
        grad_nbias * factor,
        grad_w_in * factor,
        grad_w_out * factor,
        grad_obias * factor,
        grad_scale * factor,
    )


def solution(mesh):
    in_specs = (
        P(None, "lat", "lon"),
        P(None, "lat", "lon"),
        P(None, "lat", "lon"),
        P(None, "lat", "lon"),
        P(None, "lat", "lon"),
        P(None, "lat", "lon"),
        P(None, "lat", "lon"),
        P(),
        P(),
        P(),
        P(),
        P(),
        P(),
        P(),
        P(),
    )
    out_specs = (P(None, "lat", "lon"), P(), P(), P(), P(), P(), P(), P(), P())
    return jax.shard_map(local, mesh=mesh, in_specs=in_specs, out_specs=out_specs, check_vma=False)
```

profile of v0, /device:TPU:1, one launch (start us, length us, event | category | flops | bytes accessed | tf_op | source)
XLA Modules:
  0.0 656.0 jit_solution(1695157089477517917)
XLA Ops:
  25.9 8.8 %reshape.116 = f32[768,1800]{1,0:T(8,128)} reshape(f32[12,64,4,450]{3,2,1,0:T(4,128)} %broadcast_in_dim.13) | data formatting | bytes 11059200 | tf_op jit(solution)/shard_map/reshape | solution.py:37
  34.6 6.3 copy.110
  44.4 8.6 %reshape.115 = f32[768,1800]{1,0:T(8,128)} reshape(f32[12,64,4,450]{3,2,1,0:T(4,128)} %broadcast_in_dim.12) | data formatting | bytes 11059200 | tf_op jit(solution)/shard_map/reshape | solution.py:36
  53.0 6.4 copy.113
  61.6 6.7 %copy.109 = f32[192,4,4,450]{3,2,1,0:T(4,128)} copy(f32[192,4,4,450]{3,0,2,1:T(8,128)S(1)} %add_convert_fusion) | data formatting | bytes 11059200 | tf_op jit(solution)/shard_map/convert_element_type | solution.py:34
  68.3 8.6 %convert_element_type.107 = f32[768,1800]{1,0:T(8,128)} reshape(f32[192,4,4,450]{3,2,1,0:T(4,128)} %copy.109) | data formatting | bytes 11059200 | tf_op jit(solution)/shard_map/convert_element_type | solution.py:34
  76.9 6.4 copy.112
  83.4 11.3 %fusion.7 = bf16[768,1800]{0,1:T(8,128)(2,1)} fusion(bf16[768,192]{0,1:T(8,128)(2,1)S(1)} %copy-done, f32[192,1800]{1,0:T(8,128)} %reshape.119, f32[192]{0:T(256)} %param.29, f32[768,1800]{0,1:T(8,128)} %copy.113, f32[768,1800]{0,1:T(8,128)} %copy.112, f32[768,1800]{0,1:T(8,128)} %copy.110), kind=kOutput, calls=%fused_computation.60 | convolution fusion | flops 550886400 | bytes 21031680 | tf_op jit(solution)/shard_map/dot_general | solution.py:109
  94.7 6.7 %fusion.116 = f32[192]{0:T(256)} fusion(f32[192,1800]{1,0:T(8,128)S(1)} %copy-done.9, bf16[768,192]{0,1:T(8,128)(2,1)S(1)} %copy-done, f32[192]{0:T(256)S(1)} %copy-done.41, f32[768,1800]{0,1:T(8,128)} %copy.113, f32[768,1800]{0,1:T(8,128)S(1)} %copy-done.2, f32[768,1800]{0,1:T(8,128)} %copy.110), kind=kOutput, calls=%fused_computation.242 | convolution fusion | flops 544319808 | bytes 18267648 | tf_op jit(solution)/shard_map/dot_general | solution.py:116
  108.7 7.3 %convert_element_type.118 = bf16[768,1800]{1,0:T(8,128)(2,1)} reshape(bf16[12,64,4,450]{3,2,1,0:T(4,128)(2,1)} %multiply_convert_fusion) | data formatting | bytes 5529600 | tf_op jit(solution)/shard_map/convert_element_type | solution.py:101
  127.6 6.1 collective-permute-done.3
  134.3 15.7 %collective-permute-done.2 = bf16[192,3,456]{2,0,1:T(8,128)(2,1)S(1)} collective-permute-done((bf16[192,3,456]{2,0,1:T(8,128)(2,1)S(1)}, bf16[192,3,456]{2,0,1:T(8,128)(2,1)S(1)}, u32[]{:S(2)}, u32[]{:S(2)}) %collective-permute-start.2) | collective-permute-done | bytes 525344 | tf_op jit(solution)/shard_map/ppermute | solution.py:20
  150.6 7.7 %maximum_convert_fusion = f32[192,10,456]{2,1,0:T(8,128)} fusion(bf16[192,3,456]{2,1,0:T(4,128)(2,1)S(1)} %copy.104, bf16[192,4,3]{2,1,0:T(4,128)(2,1)} %collective-permute-done.1, bf16[192,4,450]{2,1,0:T(4,128)(2,1)S(1)} %fusion.14, bf16[192,4,3]{2,1,0:T(4,128)(2,1)S(1)} %collective-permute-done, bf16[192,3,456]{2,1,0:T(4,128)(2,1)S(1)} %copy.103), kind=kLoop, calls=%fused_computation.64 | loop fusion | flops 8755200 | bytes 5253120 | tf_op jit(solution)/shard_map/convert_element_type | solution.py:150
  158.4 127.9 %fusion.123 = (f32[4,450]{1,0:T(4,128)S(1)}, f32[192,4,450]{2,1,0:T(4,128)S(1)}) fusion(f32[192]{0:T(256)S(1)} %copy-done.42, f32[192,10,456]{2,1,0:T(8,128)} %maximum_convert_fusion, f32[192]{0:T(256)S(1)} %bitcast.284, f32[192]{0:T(256)S(1)} %bitcast.286, f32[192]{0:T(256)S(1)} %bitcast.192, f32[192]{0:T(256)S(1)} %bitcast.194, f32[192]{0:T(256)S(1)} %bitcast.196, ...), kind=kLoop, calls=%fused_computation.275 | loop fusion | flops 34212600 | bytes 69165600 | tf_op jit(solution)/shard_map/reduce_sum | solution.py:92
  294.1 41.9 %fusion.61 = (f32[192]{0:T(256)S(1)}, f32[192]{0:T(256)S(1)}, f32[192]{0:T(256)S(1)}, f32[192]{0:T(256)S(1)}, f32[192]{0:T(256)S(1)}, /*index=5*/f32[192]{0:T(25...) fusion(bf16[192,4,450]{2,1,0:T(4,128)(2,1)S(1)} %reshape.118, ...), kind=kLoop, calls=%fused_computation.121 | loop fusion | flops 9328704 | bytes 18672384 | tf_op jit(solution)/shard_map/reduce_sum | solution.py:76
  336.0 39.4 %fusion.63 = (f32[192]{0:T(256)S(1)}, f32[192]{0:T(256)S(1)}, f32[192]{0:T(256)S(1)}, f32[192]{0:T(256)S(1)}, f32[192]{0:T(256)S(1)}, /*index=5*/f32[192]{0:T(25...) fusion(bf16[192,4,450]{2,1,0:T(4,128)(2,1)S(1)} %reshape.118, ...), kind=kLoop, calls=%fused_computation.123 | loop fusion | flops 12783744 | bytes 25588224 | tf_op jit(solution)/shard_map/reduce_sum | solution.py:76
  375.4 27.0 %fusion.62 = (f32[192]{0:T(256)S(1)}, f32[192]{0:T(256)S(1)}, f32[192]{0:T(256)S(1)}, f32[192]{0:T(256)S(1)}, f32[192]{0:T(256)S(1)}, /*index=5*/f32[192]{0:T(25...) fusion(bf16[192,4,450]{2,1,0:T(4,128)(2,1)S(1)} %reshape.118, ...), kind=kLoop, calls=%fused_computation.122 | loop fusion | flops 12783744 | bytes 25588224 | tf_op jit(solution)/shard_map/reduce_sum | solution.py:76
  406.9 67.9 %all-reduce = (f32[192,7,7]{0,2,1:T(8,128)S(1)}, f32[192]{0:T(256)S(1)}, f32[192]{0:T(256)S(1)}, f32[192]{0:T(256)S(1)}, f32[192]{0:T(256)S(1)}, /*index=5*/f32[192]{0:T(256)S(1)}) all-reduce(f32[192,7,7]{0,2,1:T(8,128)S(1)} %constant_dynamic-update-slice_fusion, ...), channel_id=1, replica_groups=mesh['lat'=8,'lon'=16] {'lat','lon'}, use_global_device_ids=true, to_apply=%region_53.0 | all-reduce | flops 10368 | bytes 82944 | tf_op jit(solution)/shard_map/psum | solution.py:173
  486.7 6.3 collective-permute-start.6
  494.7 6.8 %collective-permute-done.7 = bf16[192,3,456]{2,0,1:T(8,128)(2,1)} collective-permute-done((bf16[192,3,456]{2,0,1:T(8,128)(2,1)S(1)}, bf16[192,3,456]{2,0,1:T(8,128)(2,1)}, u32[]{:S(2)}, u32[]{:S(2)}) %collective-permute-start.7) | collective-permute-done | bytes 525344 | tf_op jit(solution)/shard_map/ppermute | solution.py:22
  503.1 12.9 %collective-permute-done.6 = bf16[192,3,456]{2,0,1:T(8,128)(2,1)} collective-permute-done((bf16[192,3,456]{2,0,1:T(8,128)(2,1)S(1)}, bf16[192,3,456]{2,0,1:T(8,128)(2,1)}, u32[]{:S(2)}, u32[]{:S(2)}) %collective-permute-start.6) | collective-permute-done | bytes 525344 | tf_op jit(solution)/shard_map/ppermute | solution.py:20
  517.7 6.4 maximum_convert_fusion.1
  524.2 98.7 %fusion.66 = bf16[192,4,450]{2,1,0:T(4,128)(2,1)} fusion(f32[192,10,456]{2,1,0:T(8,128)} %maximum_convert_fusion.1, bf16[192,4,450]{2,1,0:T(4,128)(2,1)S(1)} %copy-done.4, f32[192]{0:T(256)S(1)} %bitcast.285, f32[192]{0:T(256)S(1)} %bitcast.287, f32[192]{0:T(256)S(1)} %bitcast.193, f32[192]{0:T(256)S(1)} %bitcast.195, f32[192]{0:T(256)S(1)} %bitcast.197, ...), kind=kLoop, calls=%fused_computation.127 | loop fusion | flops 34560000 | bytes 69157632 | tf_op jit(solution)/shard_map/convert_element_type | solution.py:160
  622.9 23.3 %all-reduce.4.cloned.1.call-done = (f32[192,768]{1,0:T(8,128)}, f32[768,192]{0,1:T(8,128)}) async-done(((f32[192,768]{1,0:T(8,128)}, f32[768,192]{0,1:T(8,128)}), (f32[192,768]{1,0:T(8,128)}, f32[768,192]{0,1:T(8,128)})) %all-reduce.4.cloned.1.call-update) | async-done | bytes 1179664 | tf_op jit(solution)/shard_map/psum | solution.py:173
  (181 shorter events, 75.8 us)
Async XLA Ops:
  7.2 76.2 %copy-start = (bf16[768,192]{0,1:T(8,128)(2,1)S(1)}, bf16[768,192]{0,1:T(8,128)(2,1)}, u32[]{:S(2)}) copy-start(bf16[768,192]{0,1:T(8,128)(2,1)} %param.27) | copy-start | bytes 884740
  7.2 638.9 %all-reduce.4.cloned.1.call-start = ((), (), s32[]{:S(2)}) async-start(), calls=%async_computation | async-start | bytes 2359296 | tf_op jit(solution)/shard_map/psum | solution.py:173
  12.6 103.4 %collective-permute-start = (bf16[192,4,3]{2,1,0:T(4,128)(2,1)}, bf16[192,4,3]{2,1,0:T(4,128)(2,1)S(1)}, u32[]{:S(2)}, u32[]{:S(2)}) collective-permute-start(bf16[192,4,3]{2,1,0:T(4,128)(2,1)} %get-tuple-element.112), channel_id=1, source_target_pairs={{0,1},{1,2},{2,3},{3,4},{4,5},{5,6},{6,7},{7,8},{8,9},{9,10},{10,1... | collective-permute-start | bytes 13832 | tf_op jit(solution)/shard_map/ppermute | solution.py:20
  15.3 100.8 %collective-permute-start.1 = (bf16[192,4,3]{2,1,0:T(4,128)(2,1)}, bf16[192,4,3]{2,1,0:T(4,128)(2,1)}, u32[]{:S(2)}, u32[]{:S(2)}) collective-permute-start(bf16[192,4,3]{2,1,0:T(4,128)(2,1)} %get-tuple-element.113), channel_id=1, source_target_pairs={{1,0},{2,1},{3,2},{4,3},{5,4},{6,5},{7,6},{8,7},{9,8},{10,9},{11,1... | collective-permute-start | bytes 13832 | tf_op jit(solution)/shard_map/ppermute | solution.py:22
  76.9 24.6 %slice-start.2 = ((s8[6291456]{0:T(1024)(128)(4,1)}), s8[2097152]{0:T(1024)(128)(4,1)S(1)}, s32[]{:S(2)}) async-start(s8[6291456]{0:T(1024)(128)(4,1)} %bitcast.184), calls=%async_computation.3 | async-start | bytes 4194304
  83.4 11.4 %copy-start.9 = (f32[192,1800]{1,0:T(8,128)S(1)}, f32[192,1800]{1,0:T(8,128)}, u32[]{:S(2)}) copy-start(f32[192,1800]{1,0:T(8,128)} %reshape.119) | copy-start | bytes 4147204
  83.4 11.4 %copy-start.41 = (f32[192]{0:T(256)S(1)}, f32[192]{0:T(256)}, u32[]{:S(2)}) copy-start(f32[192]{0:T(256)} %param.28) | copy-start | bytes 2308
  83.4 18.1 %slice-start.3 = ((s8[6291456]{0:T(1024)(128)(4,1)}), s8[4194304]{0:T(1024)(128)(4,1)S(1)}, s32[]{:S(2)}) async-start(s8[6291456]{0:T(1024)(128)(4,1)} %bitcast.184), calls=%async_computation.4 | async-start | bytes 8388608
  118.7 15.0 %collective-permute-start.3 = (bf16[192,3,456]{2,0,1:T(8,128)(2,1)S(1)}, bf16[192,3,456]{2,0,1:T(8,128)(2,1)S(1)}, u32[]{:S(2)}, u32[]{:S(2)}) collective-permute-start(bf16[192,3,456]{2,0,1:T(8,128)(2,1)S(1)} %copy.102), channel_id=1, source_target_pairs={{16,0},{32,16},{48,32},{64,48},{80,64},{96,80},{112,96},{17,1},{33... | collective-permute-start | bytes 1575944 | tf_op jit(solution)/shard_map/ppermute | solution.py:22
  120.1 29.8 %collective-permute-start.2 = (bf16[192,3,456]{2,0,1:T(8,128)(2,1)S(1)}, bf16[192,3,456]{2,0,1:T(8,128)(2,1)S(1)}, u32[]{:S(2)}, u32[]{:S(2)}) collective-permute-start(bf16[192,3,456]{2,0,1:T(8,128)(2,1)S(1)} %copy.101), channel_id=1, source_target_pairs={{0,16},{16,32},{32,48},{48,64},{64,80},{80,96},{96,112},{1,17},{17... | collective-permute-start | bytes 1575944 | tf_op jit(solution)/shard_map/ppermute | solution.py:20
  125.7 32.5 %copy-start.28 = (f32[192,1,1]{0,2,1:T(1,128)}, f32[192,1,1]{0,2,1:T(1,128)S(1)}, u32[]{:S(2)}) copy-start(f32[192,1,1]{0,2,1:T(1,128)S(1)} %get-tuple-element.162) | copy-start | bytes 2308
  125.7 32.5 %copy-start.30 = (f32[192,1,1]{0,2,1:T(1,128)}, f32[192,1,1]{0,2,1:T(1,128)S(1)}, u32[]{:S(2)}) copy-start(f32[192,1,1]{0,2,1:T(1,128)S(1)} %get-tuple-element.163) | copy-start | bytes 2308
  125.7 32.5 %copy-start.32 = (f32[192,1,1]{0,2,1:T(1,128)}, f32[192,1,1]{0,2,1:T(1,128)S(1)}, u32[]{:S(2)}) copy-start(f32[192,1,1]{0,2,1:T(1,128)S(1)} %get-tuple-element.164) | copy-start | bytes 2308
  125.7 32.5 %copy-start.34 = (f32[192,1,1]{0,2,1:T(1,128)}, f32[192,1,1]{0,2,1:T(1,128)S(1)}, u32[]{:S(2)}) copy-start(f32[192,1,1]{0,2,1:T(1,128)S(1)} %get-tuple-element.165) | copy-start | bytes 2308
  125.8 32.5 %copy-start.36 = (f32[192,1,1]{0,2,1:T(1,128)}, f32[192,1,1]{0,2,1:T(1,128)S(1)}, u32[]{:S(2)}) copy-start(f32[192,1,1]{0,2,1:T(1,128)S(1)} %get-tuple-element.166) | copy-start | bytes 2308
  294.1 81.3 %slice-start = ((s8[6291456]{0:T(1024)(128)(4,1)}), s8[2097152]{0:T(1024)(128)(4,1)S(1)}, s32[]{:S(2)}) async-start(s8[6291456]{0:T(1024)(128)(4,1)} %bitcast.182), calls=%async_computation.1 | async-start | bytes 4194304
  336.0 39.4 %slice-start.1 = ((s8[6291456]{0:T(1024)(128)(4,1)}), s8[4194304]{0:T(1024)(128)(4,1)S(1)}, s32[]{:S(2)}) async-start(s8[6291456]{0:T(1024)(128)(4,1)} %bitcast.182), calls=%async_computation.2 | async-start | bytes 8388608
  375.4 27.2 %copy-start.6 = (f32[192,1800]{1,0:T(8,128)S(1)}, f32[192,1800]{1,0:T(8,128)}, u32[]{:S(2)}) copy-start(f32[192,1800]{1,0:T(8,128)} %copy-done.5) | copy-start | bytes 4147204
  375.4 27.2 %copy-start.44 = (f32[192]{0:T(256)S(1)}, f32[192]{0:T(256)}, u32[]{:S(2)}) copy-start(f32[192]{0:T(256)} %param.25) | copy-start | bytes 2308
  476.0 3.4 collective-permute-start.4
  476.7 6.9 %collective-permute-start.5 = (bf16[192,4,3]{2,1,0:T(4,128)(2,1)S(1)}, bf16[192,4,3]{2,1,0:T(4,128)(2,1)S(1)}, u32[]{:S(2)}, u32[]{:S(2)}) collective-permute-start(bf16[192,4,3]{2,1,0:T(4,128)(2,1)S(1)} %get-tuple-element.109), channel_id=1, source_target_pairs={{1,0},{2,1},{3,2},{4,3},{5,4},{6,5},{7,6},{8,7},{9,8},{10,9},{11,1... | collective-permute-start | bytes 13832 | tf_op jit(solution)/shard_map/ppermute | solution.py:22
  485.4 16.2 %collective-permute-start.7 = (bf16[192,3,456]{2,0,1:T(8,128)(2,1)S(1)}, bf16[192,3,456]{2,0,1:T(8,128)(2,1)}, u32[]{:S(2)}, u32[]{:S(2)}) collective-permute-start(bf16[192,3,456]{2,0,1:T(8,128)(2,1)S(1)} %copy.115), channel_id=1, source_target_pairs={{16,0},{32,16},{48,32},{64,48},{80,64},{96,80},{112,96},{17,1},{33... | collective-permute-start | bytes 1575944 | tf_op jit(solution)/shard_map/ppermute | solution.py:22
  486.7 29.4 %collective-permute-start.6 = (bf16[192,3,456]{2,0,1:T(8,128)(2,1)S(1)}, bf16[192,3,456]{2,0,1:T(8,128)(2,1)}, u32[]{:S(2)}, u32[]{:S(2)}) collective-permute-start(bf16[192,3,456]{2,0,1:T(8,128)(2,1)S(1)} %copy.114), channel_id=1, source_target_pairs={{0,16},{16,32},{32,48},{48,64},{64,80},{80,96},{96,112},{1,17},{17... | collective-permute-start | bytes 1575944 | tf_op jit(solution)/shard_map/ppermute | solution.py:20
  524.1 124.8 %copy-start.1 = (bf16[768,192]{0,1:T(8,128)(2,1)S(1)}, bf16[768,192]{0,1:T(8,128)(2,1)}, u32[]{:S(2)}) copy-start(bf16[768,192]{0,1:T(8,128)(2,1)} %param.27) | copy-start | bytes 884740
  (34 other events, 207.7 us)
Sparse Core Ops, SparseCore 0:
  493.7 152.4 all-reduce.3
where the time goes:
time: 662 us; the launch traced here: 656 us
  other arithmetic  373 us (56%)
  local copies, waits for them, and re-layouts  83.8 us (13%)
  waiting for transfers between devices  71.2 us (11%)
  blocking collectives  67.9 us (10%)
  matrix products  27.1 us (4%)
  starting transfers between devices  18 us (3%)
  between operations  15.1 us (2%)
    reduce_sum x1, other arithmetic, block_backward(): mean_val = jnp.mean(flat_conv, axis=0)  128 us
    reduce_sum x3, other arithmetic, tap_products(): jnp.sum(grad_field * padded[:, row_tap:row_tap + rows, col_tap:col_tap +...  108 us
    convert_element_type x1, other arithmetic, local(): grad_input = (grad_out.astype(jnp.float32) + backward_taps(padded_grad, k...  98.7 us
    psum x1, blocking collectives, local(): lax.psum((grad_w_in, grad_w_out, grad_obias, grad_scale, grad_gain, grad_...  67.9 us
    ppermute x4, waiting for transfers between devices, padded_2(): lax.ppermute(tail, axis, [(i, (i + 1) % count) for i in range(ends)])  30.7 us
    psum x1, waiting for transfers between devices, local(): lax.psum((grad_w_in, grad_w_out, grad_obias, grad_scale, grad_gain, grad_...  23.3 us
    convert_element_type x4, local copies, waits for them, and re-layouts, restore(): symbols = jnp.stack(pieces, axis=1).reshape((packed.shape[0] * 4,) + pack...  22.8 us
    ppermute x4, waiting for transfers between devices, padded_2(): lax.ppermute(head, axis, [((i + 1) % count, i) for i in range(ends)])  17.2 us
  transfers between devices with their start and end apart: 9, of which 7 were waited for; matrix products, arithmetic and copies ran while one was open for 33% of the time, Pallas kernels for 0%

commit v1 on v0

v1 whole, which is shorter than its diff:
```python
import functools
import math

import jax
import jax.numpy as jnp
from jax import lax
from jax.experimental import pallas as pl
from jax.experimental.pallas import tpu as pltpu
from jax.sharding import PartitionSpec as P

C = 192
FF = 768
WORDS = FF // 4
GROUP = 64
RADIUS = 3
TAPS = 2 * RADIUS + 1
ROWS = 4
COLS = 450
WIDE = COLS + 2 * RADIUS
LANES = 512
MAIN = 384
TAIL = COLS + RADIUS - MAIN
PACK = 1408
RIM = MAIN * RADIUS + TAIL * RADIUS - (PACK - 128)
CH = 16
TIE = 3
F32 = jnp.float32
BF16 = jnp.bfloat16
VMEM_LIMIT = 20 * 1024 * 1024


def params():
    return pltpu.CompilerParams(vmem_limit_bytes=VMEM_LIMIT)


def resident(kernel, name, out_shape, *args, scratch=()):
    spec = pl.BlockSpec(memory_space=pltpu.VMEM)
    return pl.pallas_call(
        kernel,
        out_shape=out_shape,
        in_specs=[spec] * len(args),
        out_specs=jax.tree.map(lambda _: spec, out_shape),
        scratch_shapes=list(scratch),
        compiler_params=params(),
        name=name,
    )(*args)


def lane_iota(shape):
    return lax.broadcasted_iota(jnp.int32, shape, len(shape) - 1)


def nt_dot(a, b):
    return lax.dot_general(a, b, (((1,), (1,)), ((), ())), preferred_element_type=F32)


def nn_dot(a, b):
    return jnp.dot(a, b, preferred_element_type=F32)


def rims_of(rows, head):
    first = RADIUS if head else COLS
    base = RIM + (RADIUS * ROWS if head else 0)
    lane = lane_iota((C, 128))
    total = jnp.zeros((C, 128), F32)
    for r, row in enumerate(rows):
        start = base + RADIUS * r
        moved = pltpu.roll(row, (start - first) % LANES, 1)[:, :128]
        keep = (lane >= start) & (lane < start + RADIUS)
        total = jnp.where(keep, moved, total)
    return total.astype(BF16)


def pack(rows, ref):
    lane = lane_iota((C, 256))
    tails = jnp.zeros((C, 256), F32)
    for k, value in enumerate(rows):
        ref[:, MAIN * k : MAIN * (k + 1)] = value[:, :MAIN].astype(BF16)
        wide = jnp.concatenate([value[:, MAIN:], jnp.zeros((C, 128), F32)], axis=1)
        moved = pltpu.roll(wide, TAIL * k, 1) if k else wide
        keep = (lane >= TAIL * k) & (lane < TAIL * (k + 1))
        tails = jnp.where(keep, moved, tails)
    ref[:, MAIN * RADIUS :] = tails.astype(BF16)


def send_rows(rows, head_ref, tail_ref, up_ref, down_ref):
    pack(rows[:RADIUS], up_ref)
    pack(rows[ROWS - RADIUS :], down_ref)
    head_ref[...] = rims_of(rows, True)
    tail_ref[...] = rims_of(rows, False)


def with_rims(first_tile, last_tile, rims, r):
    lane = lane_iota((C, 128))
    left = pltpu.roll(rims, (-RIM - RADIUS * r) % 128, 1)
    spot = RADIUS + COLS - MAIN
    right = pltpu.roll(rims, (spot - RIM - RADIUS * (ROWS + r)) % 128, 1)
    first_tile = jnp.where(lane < RADIUS, left, first_tile)
    last_tile = jnp.where((lane >= spot) & (lane < spot + RADIUS), right, last_tile)
    return first_tile.astype(BF16), last_tile.astype(BF16)


def fill_own(field_ref, own_ref, rims_ref):
    rims = rims_ref[...].astype(F32)
    for r in range(ROWS):
        first, last = with_rims(
            own_ref[r, :, :128].astype(F32), own_ref[r, :, MAIN:].astype(F32), rims, r
        )
        field_ref[RADIUS + r, :, :128] = first
        field_ref[RADIUS + r, :, 128:MAIN] = own_ref[r, :, 128:MAIN]
        field_ref[RADIUS + r, :, MAIN:] = last


def fill_halo(field_ref, ref, first_row, source_row):
    rims = ref[:, PACK - 128 :].astype(F32)
    tails = ref[:, MAIN * RADIUS :].astype(F32)
    lane = lane_iota((C, 128))
    for k in range(RADIUS):
        moved = pltpu.roll(tails, (-TAIL * k) % 256, 1) if k else tails
        last = jnp.where(lane < TAIL, moved[:, :128], 0.0)
        first, last = with_rims(
            ref[:, MAIN * k : MAIN * k + 128].astype(F32), last, rims, source_row + k
        )
        field_ref[first_row + k, :, :128] = first
        field_ref[first_row + k, :, 128:MAIN] = ref[:, MAIN * k + 128 : MAIN * (k + 1)]
        field_ref[first_row + k, :, MAIN:] = last


def restore_kernel(
    words_ref, low_ref, high_ref, own_ref, head_ref, tail_ref, up_ref, down_ref, bounds
):
    nwords = C // 4
    bounds[...] = jnp.zeros(bounds.shape, F32)
    for g in range(C // GROUP):
        low = low_ref[g].astype(F32)
        bounds[0, g, :, :COLS] = low
        bounds[1, g, :, :COLS] = high_ref[g].astype(F32) - low
    per = GROUP // 4
    row_id = lax.broadcasted_iota(jnp.int32, (C, C), 0)
    col_id = lax.broadcasted_iota(jnp.int32, (C, C), 1)
    place = (row_id == 4 * (col_id % nwords) + col_id // nwords).astype(F32).astype(BF16)
    lane = lane_iota((C, LANES))
    rows = []
    for r in range(ROWS):
        pieces = []
        words = words_ref[:, r, :]
        words = jnp.concatenate([words, jnp.zeros((nwords, LANES - COLS), jnp.int32)], axis=1)
        for j in range(4):
            code = (jnp.right_shift(words, 2 * j) & 3).astype(F32)
            for g in range(C // GROUP):
                low = bounds[0, g, r : r + 1, :]
                span = bounds[1, g, r : r + 1, :]
                value = low + code[g * per : (g + 1) * per] * span / 3.0
                pieces.append(value.astype(BF16))
        mixed = jnp.concatenate(pieces, axis=0)
        value = nn_dot(place, mixed)
        value = pltpu.roll(value, RADIUS, 1)
        value = jnp.where((lane >= RADIUS) & (lane < RADIUS + COLS), value, 0.0)
        rows.append(value)
        own_ref[r] = value.astype(BF16)
    send_rows(rows, head_ref, tail_ref, up_ref, down_ref)


def mlp_kernel(
    words_ref, low_ref, high_ref, grad_ref, scale_ref, w_out_ref, w_in_ref,
    hidden_ref, normed_ref, g_ref, sums_ref,
    order, w_out_p, w_in_p, table, lifted, active,
):
    step = pl.program_id(0)

    @pl.when(step == 0)
    def _():
        row_id = lax.broadcasted_iota(jnp.int32, (FF, FF), 0)
        col_id = lax.broadcasted_iota(jnp.int32, (FF, FF), 1)
        order[...] = (col_id == 4 * (row_id % WORDS) + row_id // WORDS).astype(F32).astype(BF16)
        w_out_p[...] = nt_dot(order[...], w_out_ref[...]).astype(BF16)
        w_in_p[...] = nt_dot(w_in_ref[...], order[...]).astype(BF16)
        g_ref[...] = jnp.zeros((C, FF), F32)
        sums_ref[...] = jnp.zeros((C, 128), F32)

    grad = grad_ref[0].astype(F32)
    scaled = (scale_ref[:, :1] * grad).astype(BF16)
    lifted[...] = nn_dot(w_out_p[...], scaled)
    low = low_ref[0].astype(F32)
    span = high_ref[0].astype(F32) - low
    for k in range(4):
        hidden = low + float(k) * span / 3.0
        cdf = 0.5 * (1.0 + lax.erf(hidden * 0.7071067811865476))
        density = jnp.exp(-0.5 * hidden * hidden) * 0.3989422804014327
        table[k] = hidden * cdf
        table[4 + k] = cdf + hidden * density
    for g in range(FF // GROUP):
        words = words_ref[0, CH * g : CH * (g + 1), :]
        values = [jnp.broadcast_to(table[k, g : g + 1, :], (CH, LANES)) for k in range(8)]
        for j in range(4):
            odd = (words & (1 << (2 * j))) != 0
            upper = (words & (2 << (2 * j))) != 0
            act = jnp.where(
                upper, jnp.where(odd, values[3], values[2]), jnp.where(odd, values[1], values[0])
            )
            slope = jnp.where(
                upper, jnp.where(odd, values[7], values[6]), jnp.where(odd, values[5], values[4])
            )
            place = slice(WORDS * j + CH * g, WORDS * j + CH * (g + 1))
            active[place, :] = act.astype(BF16)
            hidden_ref[0, place, :] = (lifted[place, :] * slope).astype(BF16)
    normed_ref[0] = nn_dot(w_in_p[...], hidden_ref[0])
    g_ref[...] += nt_dot(grad_ref[0], active[...])
    lane = lane_iota((C, 128))
    total = jnp.sum(grad, axis=1, keepdims=True)
    sums_ref[...] += jnp.where(lane == 52, total, 0.0)

    @pl.when(step == ROWS - 1)
    def _():
        value = g_ref[...]
        high = value.astype(BF16)
        rest = (value - high.astype(F32)).astype(BF16)
        g_ref[...] = nn_dot(high, order[...]) + nn_dot(rest, order[...])


def stencil(field_ref, taps_ref, wide_taps, partial, emit, flip):
    def body(block, carry):
        chans = pl.ds(pl.multiple_of(block * CH, CH), CH)
        taps = taps_ref[chans, :]
        for t in range(TAPS * TAPS):
            source = TAPS * TAPS - 1 - t if flip else t
            wide_taps[t] = jnp.broadcast_to(taps[:, source : source + 1], (CH, 128))
        for tile in range(LANES // 128):
            lanes = slice(128 * tile, 128 * (tile + 1))
            cells = [field_ref[r, chans, lanes].astype(F32) for r in range(ROWS + 2 * RADIUS)]
            for q in range(TAPS):
                sums = [None] * ROWS
                for p in range(TAPS):
                    tap = wide_taps[TAPS * p + q]
                    for i in range(ROWS):
                        term = tap * cells[i + p]
                        sums[i] = term if sums[i] is None else sums[i] + term
                for i in range(ROWS):
                    partial[q, i, :, lanes] = sums[i]
        for i in range(ROWS):
            total = partial[0, i]
            for q in range(1, TAPS):
                total = total + pltpu.roll(partial[q, i], LANES - q, 1)
            emit(chans, i, total)
        return carry

    lax.fori_loop(0, C // CH, body, 0)


def conv_kernel(
    own_ref, rims_ref, above_ref, below_ref,
    taps_ref, chan_ref, normed_ref,
    field_ref, grad_ref, head_ref, tail_ref, up_ref, down_ref, normed_in_ref, sums_ref,
    conv, wide_taps, partial,
):
    fill_own(field_ref, own_ref, rims_ref)
    fill_halo(field_ref, above_ref, 0, ROWS - RADIUS)
    fill_halo(field_ref, below_ref, RADIUS + ROWS, 0)

    def emit(chans, i, total):
        conv[i, chans, :] = total + chan_ref[chans, 0:1]

    stencil(field_ref, taps_ref, wide_taps, partial, emit, False)
    gain = chan_ref[:, 1:2]
    bias = chan_ref[:, 2:3]
    lane = lane_iota((C, LANES))
    rows = []
    sum_gain = jnp.zeros((C, LANES), F32)
    sum_bias = jnp.zeros((C, LANES), F32)
    sum_conv = jnp.zeros((C, LANES), F32)
    for r in range(ROWS):
        value = conv[r]
        centered = value - jnp.sum(value, axis=0, keepdims=True) * (1.0 / C)
        variance = jnp.sum(centered * centered, axis=0, keepdims=True) * (1.0 / C)
        inv_std = lax.rsqrt(variance + 1e-06)
        normed = centered * inv_std
        normed_in_ref[r] = (normed * gain + bias).astype(BF16)
        back = normed_ref[r]
        sum_gain = sum_gain + back * normed
        sum_bias = sum_bias + back
        dn = back * gain
        mean_dn = jnp.sum(dn, axis=0, keepdims=True) * (1.0 / C)
        mean_dx = jnp.sum(dn * normed, axis=0, keepdims=True) * (1.0 / C)
        grad = inv_std * (dn - mean_dn - normed * mean_dx)
        grad = jnp.where(lane < COLS, grad, 0.0).astype(BF16).astype(F32)
        sum_conv = sum_conv + grad
        grad = pltpu.roll(grad, RADIUS, 1)
        rows.append(grad)
        grad_ref[r] = grad.astype(BF16)
    send_rows(rows, head_ref, tail_ref, up_ref, down_ref)
    lane = lane_iota((C, 128))
    sums = jnp.where(lane == 49, jnp.sum(sum_gain, axis=1, keepdims=True), 0.0)
    sums = jnp.where(lane == 50, jnp.sum(sum_bias, axis=1, keepdims=True), sums)
    sums_ref[...] = jnp.where(lane == 51, jnp.sum(sum_conv, axis=1, keepdims=True), sums)


def taps_kernel(field_ref, grad_ref, normed_in_ref, hidden_ref, sums_ref, h_ref, order):
    row = lax.broadcasted_iota(jnp.int32, (CH, 256), 0)
    diagonal = lane_iota((CH, 256)) % CH == row
    row = lax.broadcasted_iota(jnp.int32, (128, 128), 0)
    pick = (row // CH == lane_iota((128, 128))).astype(F32).astype(BF16)
    cells = (ROWS + 2 * RADIUS) * CH
    lane = lane_iota((CH, 128))

    def body(block, carry):
        chans = pl.ds(pl.multiple_of(block * CH, CH), CH)
        field = field_ref[:, chans, :].reshape(cells, LANES)
        grads = [grad_ref[i, chans, :] for i in range(ROWS)]
        moved = [
            pltpu.roll(grads[i], (q - RADIUS) % LANES, 1) if q != RADIUS else grads[i]
            for q in range(TAPS)
            for i in range(ROWS)
        ]
        product = nt_dot(jnp.concatenate(moved, axis=0), field)
        product = jnp.concatenate(
            [product, jnp.zeros((TAPS * ROWS * CH, 256 - cells), F32)], axis=1
        )
        totals = []
        for q in range(TAPS):
            total = None
            for i in range(ROWS):
                start = (q * ROWS + i) * CH
                value = jnp.where(diagonal, product[start : start + CH], 0.0)
                value = (pltpu.roll(value, 256 - CH * i, 1) if i else value)[:, :128]
                total = value if total is None else total + value
            totals.append(jnp.where(lane < TAPS * CH, total, 0.0))
        total = jnp.concatenate(totals, axis=0)
        high = total.astype(BF16)
        rest = (total - high.astype(F32)).astype(BF16)
        result = nn_dot(high, pick) + nn_dot(rest, pick)
        sums = jnp.zeros((CH, 128), F32)
        for q in range(TAPS):
            value = result[q * CH : (q + 1) * CH]
            value = pltpu.roll(value, TAPS * q, 1) if q else value
            sums = jnp.where((lane >= TAPS * q) & (lane < TAPS * (q + 1)), value, sums)
        sums_ref[chans, :] = sums
        return carry

    lax.fori_loop(0, C // CH, body, 0, unroll=2)
    h_sum = jnp.zeros((C, FF), F32)
    for r in range(ROWS):
        h_sum = h_sum + nt_dot(normed_in_ref[r], hidden_ref[r])
    row_id = lax.broadcasted_iota(jnp.int32, (FF, FF), 0)
    col_id = lax.broadcasted_iota(jnp.int32, (FF, FF), 1)
    order[...] = (col_id == 4 * (row_id % WORDS) + row_id // WORDS).astype(F32).astype(BF16)
    high = h_sum.astype(BF16)
    rest = (h_sum - high.astype(F32)).astype(BF16)
    h_ref[...] = nn_dot(high, order[...]) + nn_dot(rest, order[...])


def input_kernel(
    own_ref, rims_ref, above_ref, below_ref, taps_ref, grad_ref,
    out_ref, field, wide_taps, partial,
):
    fill_own(field, own_ref, rims_ref)
    fill_halo(field, above_ref, 0, ROWS - RADIUS)
    fill_halo(field, below_ref, RADIUS + ROWS, 0)

    def emit(chans, i, total):
        out_ref[i, chans, :] = (grad_ref[i, chans, :].astype(F32) + total).astype(BF16)

    stencil(field, taps_ref, wide_taps, partial, emit, True)


def ring(axis, count):
    ahead = [(i, (i + 1) % count) for i in range(count)]
    return functools.partial(lax.ppermute, axis_name=axis, perm=ahead), functools.partial(
        lax.ppermute, axis_name=axis, perm=[(b, a) for a, b in ahead]
    )


def extend(head, tail, up, down):
    ahead, behind = ring("lon", lax.axis_size("lon"))
    rims = ahead(tail) + behind(head)
    up = jnp.concatenate([up[:, : PACK - 128], up[:, PACK - 128 :] + rims], axis=1)
    down = jnp.concatenate([down[:, : PACK - 128], down[:, PACK - 128 :] + rims], axis=1)
    count = lax.axis_size("lat")
    above = lax.ppermute(down, "lat", [(i, i + 1) for i in range(count - 1)])
    below = lax.ppermute(up, "lat", [(i + 1, i) for i in range(count - 1)])
    return rims, above, below, up


def swap(value, bit):
    count = lax.axis_size("lat") * lax.axis_size("lon")
    return lax.ppermute(value, ("lat", "lon"), [(i, i ^ bit) for i in range(count)])


def rounded(value):
    return lax.reduce_precision(value, 8, 7)


def all_sum(value, tied, step):
    me = lax.axis_index("lat") * lax.axis_size("lon") + lax.axis_index("lon")
    split = (1, 4, 8)
    whole = (32, 64, 2, 16)
    for count, bit in enumerate(split):
        if count == step:
            value, tied = lax.optimization_barrier((value, tied))
        half = value.shape[0] // 2
        upper = (me & bit) != 0
        low, high = value[:half], value[half:]
        send = jnp.where(upper, low, high)
        keep = jnp.where(upper, high, low)
        value = keep + swap(send.astype(BF16) if bit > 1 else send, bit).astype(F32)
    for count, bit in enumerate(whole):
        if count + len(split) == step:
            value, tied = lax.optimization_barrier((value, tied))
        sent = rounded(value)
        value = sent + swap(sent.astype(BF16), bit).astype(F32)
    value = rounded(value).astype(BF16)
    for bit in reversed(split):
        upper = (me & bit) != 0
        other = swap(value, bit)
        value = jnp.concatenate(
            [jnp.where(upper, other, value), jnp.where(upper, value, other)], axis=0
        )
    return value.astype(F32), tied


def by_row(array):
    moved = jnp.transpose(array, (1, 0, 2))
    return jnp.pad(moved, ((0, 0), (0, 0), (0, LANES - moved.shape[2])))


def local(
    stash_input, input_low, input_high, stash_hidden, hidden_low, hidden_high, grad_out,
    kernel, conv_bias, norm_gain, norm_bias, w_in, w_out, out_bias, layer_scale,
):
    field_shape = jax.ShapeDtypeStruct((ROWS, C, LANES), BF16)
    rim_shape = jax.ShapeDtypeStruct((C, 128), BF16)
    pack_shape = jax.ShapeDtypeStruct((C, PACK), BF16)
    own, *sends = resident(
        restore_kernel,
        "restore",
        (field_shape, rim_shape, rim_shape, pack_shape, pack_shape),
        stash_input,
        input_low,
        input_high,
        scratch=[pltpu.VMEM((2, C // GROUP, ROWS, LANES), F32)],
    )
    *halo, _ = extend(*sends)

    taps = jnp.pad(kernel.reshape(C, TAPS * TAPS), ((0, 0), (0, 128 - TAPS * TAPS)))
    chan = jnp.stack([conv_bias, norm_gain, norm_bias, layer_scale, out_bias], axis=1)
    chan = jnp.pad(chan, ((0, 0), (0, 123)))
    grad_rows = by_row(grad_out)

    def row_spec(count):
        return pl.BlockSpec((1, count, LANES), lambda r: (r, 0, 0))

    def whole_spec(*shape):
        return pl.BlockSpec(shape, lambda r: (0,) * len(shape))

    scale_wide = jnp.broadcast_to(layer_scale[:, None], (C, 128))
    hidden_back, normed_back, g_part, sums_a = pl.pallas_call(
        mlp_kernel,
        grid=(ROWS,),
        in_specs=[
            row_spec(WORDS), row_spec(FF // GROUP), row_spec(FF // GROUP), row_spec(C),
            whole_spec(C, 128), whole_spec(C, FF), whole_spec(C, FF),
        ],
        out_specs=[row_spec(FF), row_spec(C), whole_spec(C, FF), whole_spec(C, 128)],
        out_shape=(
            jax.ShapeDtypeStruct((ROWS, FF, LANES), BF16),
            jax.ShapeDtypeStruct((ROWS, C, LANES), F32),
            jax.ShapeDtypeStruct((C, FF), F32),
            jax.ShapeDtypeStruct((C, 128), F32),
        ),
        scratch_shapes=[
            pltpu.VMEM((FF, FF), BF16),
            pltpu.VMEM((FF, C), BF16),
            pltpu.VMEM((C, FF), BF16),
            pltpu.VMEM((8, FF // GROUP, LANES), F32),
            pltpu.VMEM((FF, LANES), F32),
            pltpu.VMEM((FF, LANES), BF16),
        ],
        compiler_params=params(),
        name="mlp",
    )(
        by_row(stash_hidden), by_row(hidden_low), by_row(hidden_high), grad_rows,
        scale_wide, jnp.transpose(w_out), w_in,
    )

    stencil_scratch = [
        pltpu.VMEM((TAPS * TAPS, CH, 128), F32),
        pltpu.VMEM((TAPS, ROWS, CH, LANES), F32),
    ]
    field, grad_own, *sends, normed_in, sums_b = resident(
        conv_kernel,
        "conv",
        (
            jax.ShapeDtypeStruct((ROWS + 2 * RADIUS, C, LANES), BF16),
            field_shape,
            rim_shape,
            rim_shape,
            pack_shape,
            pack_shape,
            field_shape,
            jax.ShapeDtypeStruct((C, 128), F32),
        ),
        own,
        *halo,
        taps,
        chan,
        normed_back,
        scratch=[pltpu.VMEM((ROWS, C, LANES), F32)] + stencil_scratch,
    )

    *grad_halo, _ = extend(*sends)
    sums_c, h_part = resident(
        taps_kernel,
        "taps",
        (jax.ShapeDtypeStruct((C, 128), F32), jax.ShapeDtypeStruct((C, FF), F32)),
        field,
        grad_own,
        normed_in,
        hidden_back,
        scratch=[pltpu.VMEM((FF, FF), BF16)],
    )
    total, grad_halo = all_sum(
        jnp.concatenate([g_part, h_part, sums_a + sums_b + sums_c], axis=1), grad_halo, TIE
    )
    grad_input = resident(
        input_kernel,
        "input",
        field_shape,
        grad_own,
        *grad_halo,
        taps,
        grad_rows,
        scratch=[pltpu.VMEM((ROWS + 2 * RADIUS, C, LANES), BF16)] + stencil_scratch,
    )
    grad_input = jnp.transpose(grad_input[:, :, :COLS], (1, 0, 2))

    cells = ROWS * lax.axis_size("lat") * COLS * lax.axis_size("lon")
    factor = 1.0 / math.sqrt(cells)
    total = total * factor
    g_sum, h_sum, sums = total[:, :FF], total[:, FF : 2 * FF], total[:, 2 * FF :]
    sum_grad = sums[:, 52]
    grad_scale = jnp.sum(g_sum * jnp.transpose(w_out).astype(F32), axis=1) + out_bias * sum_grad
    return (
        grad_input,
        jnp.transpose(sums[:, : TAPS * TAPS].reshape(C, TAPS, TAPS), (0, 2, 1)),
        sums[:, 51],
        sums[:, 49],
        sums[:, 50],
        h_sum,
        jnp.transpose(g_sum * layer_scale[:, None]),
        sum_grad * layer_scale,
        grad_scale,
    )


def solution(mesh):
    split = P(None, "lat", "lon")
    return jax.shard_map(
        local,
        mesh=mesh,
        in_specs=(split,) * 7 + (P(),) * 8,
        out_specs=(split,) + (P(),) * 8,
        check_vma=False,
    )
```

time: 662 us -> 144 us (0.22)
  other arithmetic: 373 us -> 4.46 us
  local copies, waits for them, and re-layouts: 83.8 us -> 14.2 us
  blocking collectives: 67.9 us -> 0 us
  Pallas kernels: 0 us -> 36.2 us
  waiting for transfers between devices: 71.2 us -> 43.4 us
  matrix products: 27.1 us -> 0 us
  starting transfers between devices: 18 us -> 43.5 us
  between operations: 15.1 us -> 1.15 us
    reduce_sum x7 -> x1, other arithmetic: 237 us -> 1.13 us  [local(): jnp.sum(g_sum * jnp.transpose(w_out).astype(F32), axis=1)]
    convert_element_type x11 -> x7, other arithmetic: 124 us -> 0.26 us  [the longest x4 0.14 us: all_sum(): value = sent + swap(sent.astype(BF16), bit).astype(F32)]
    psum x1 -> x0, blocking collectives: 67.9 us -> none  [local(): lax.psum((grad_w_in, grad_w_out, grad_obias, grad_scale, grad_gain, grad_...]
    pallas_call x0 -> x5, Pallas kernels: none -> 36.2 us  [the longest x4 29.1 us: resident(): pl.pallas_call(kernel, out_shape=out_shape, in_specs=[spec] * len(args),...]
    convert_element_type x7 -> x0, local copies, waits for them, and re-layouts: 34.4 us -> none  [the longest x4 22.8 us: restore(): symbols = jnp.stack(pieces, axis=1).reshape((packed.shape[0] * 4,) + pack...]
    reshape x6 -> x3, local copies, waits for them, and re-layouts: 32.6 us -> 0.13 us  [the longest x2 0.12 us: local(): kernel.reshape(C, TAPS * TAPS)]
    dot_general x5 -> x0, matrix products: 27.1 us -> none  [the longest x1 11.3 us: block_backward(): grad_active = jnp.dot(w_out, scaled_in, preferred_element_type=jnp.float32)]
    ppermute x8 -> x18, starting transfers between devices: 18 us -> 43.5 us  [the longest x10 24.3 us: swap(): lax.ppermute(value, ('lat', 'lon'), [(i, i ^ bit) for i in range(count)])]
  transfers between devices with their start and end apart: 9 -> 18, of which waited for: 7 -> 13; matrix products, arithmetic and copies ran while one was open for 33% -> 6% of each run, Pallas kernels for 0% -> 17%
where the time goes in v1:
time: 144 us; the launch traced here: 143 us
  starting transfers between devices  43.5 us (30%)
  waiting for transfers between devices  43.4 us (30%)
  Pallas kernels  36.2 us (25%)
  local copies, waits for them, and re-layouts  14.2 us (10%)
  other arithmetic  4.46 us (3%)
    pallas_call x4, Pallas kernels, resident(): pl.pallas_call(kernel, out_shape=out_shape, in_specs=[spec] * len(args),...  29.1 us
    ppermute x10, starting transfers between devices, swap(): lax.ppermute(value, ('lat', 'lon'), [(i, i ^ bit) for i in range(count)])  24.3 us
    ppermute x10, waiting for transfers between devices, swap(): lax.ppermute(value, ('lat', 'lon'), [(i, i ^ bit) for i in range(count)])  19.1 us
    ppermute x2, waiting for transfers between devices, extend(): above = lax.ppermute(down, 'lat', [(i, i + 1) for i in range(count - 1)])  15.6 us
    ppermute x2, starting transfers between devices, extend(): above = lax.ppermute(down, 'lat', [(i, i + 1) for i in range(count - 1)])  11.6 us
    unnamed x46, local copies, waits for them, and re-layouts  9.06 us
    pallas_call x1, Pallas kernels, local(): pl.pallas_call(mlp_kernel, grid=(ROWS,), in_specs=[row_spec(WORDS), row_s...  7.06 us
    ppermute x4, starting transfers between devices, extend(): rims = ahead(tail) + behind(head)  5.03 us
  transfers between devices with their start and end apart: 18, of which 13 were waited for; matrix products, arithmetic and copies ran while one was open for 6% of the time, Pallas kernels for 17%

profile of v1, /device:TPU:1, one launch (start us, length us, event | category | flops | bytes accessed | tf_op | source)
XLA Modules:
  0.0 142.9 jit_solution(9984435872828572930)
XLA Ops:
  4.1 2.8 %collective-permute-start = (bf16[192,128]{1,0:T(8,128)(2,1)S(1)}, bf16[192,128]{1,0:T(8,128)(2,1)S(1)}, u32[]{:S(2)}, u32[]{:S(2)}) collective-permute-start(bf16[192,128]{1,0:T(8,128)(2,1)S(1)} %get-tuple-element.33), channel_id=1, source_target_pairs={{0,1},{1,2},{2,3},{3,4},{4,5},{5,6},{6,7},{7,8},{8,9},{9,10},{10,1... | collective-permute-start | bytes 147464 | tf_op jit(solution)/shard_map/ppermute | solution.py:374
  8.0 2.6 %collective-permute-done.1 = bf16[192,128]{1,0:T(8,128)(2,1)S(1)} collective-permute-done((bf16[192,128]{1,0:T(8,128)(2,1)S(1)}, bf16[192,128]{1,0:T(8,128)(2,1)S(1)}, u32[]{:S(2)}, u32[]{:S(2)}) %collective-permute-start.1) | collective-permute-done | bytes 49184 | tf_op jit(solution)/shard_map/ppermute | solution.py:374
  11.5 5.6 %collective-permute-start.2 = (bf16[192,1408]{1,0:T(8,128)(2,1)}, bf16[192,1408]{1,0:T(8,128)(2,1)}, u32[]{:S(2)}, u32[]{:S(2)}) collective-permute-start(bf16[192,1408]{1,0:T(8,128)(2,1)} %pad_maximum_fusion.1), channel_id=1, source_target_pairs={{0,16},{16,32},{32,48},{48,64},{64,80},{80,96},{96,112},{1,17},{17... | collective-permute-start | bytes 1622024 | tf_op jit(solution)/shard_map/ppermute | solution.py:378
  27.9 7.1 %mlp.1 = (bf16[4,768,512]{2,1,0:T(8,128)(2,1)S(1)}, f32[4,192,512]{2,1,0:T(8,128)S(1)}, f32[192,768]{1,0:T(8,128)S(1)}, f32[192,128]{1,0:T(8,128)S(1)}) custom-call(s32[4,192,512]{2,1,0:T(8,128)S(1)} %pad.25.words_ref, bf16[4,12,512]{2,1,0:T(8,128)(2,1)S(1)} %copy-done.6, bf16[4,12,512]{2,1,0:T(8,128)(2,1)S(1)} %copy-done.7, ...), custom_call_target="tpu_custom_call" | custom-call | tf_op jit(solution)/shard_map/mlp/pallas_call | solution.py:455
  35.0 3.8 %collective-permute-done.2.above_ref = bf16[192,1408]{1,0:T(8,128)(2,1)} collective-permute-done((bf16[192,1408]{1,0:T(8,128)(2,1)}, bf16[192,1408]{1,0:T(8,128)(2,1)}, u32[]{:S(2)}, u32[]{:S(2)}) %collective-permute-start.2) | collective-permute-done | bytes 540704 | tf_op jit(solution)/shard_map/ppermute | solution.py:378
  38.8 11.0 %conv.1 = (bf16[10,192,512]{2,1,0:T(8,128)(2,1)S(1)}, bf16[4,192,512]{2,1,0:T(8,128)(2,1)S(1)}, bf16[192,128]{1,0:T(8,128)(2,1)S(1)}, bf16[192,128]{1,0:T(8,128)...) custom-call(bf16[4,192,512]{2,1,0:T(8,128)(2,1)S(1)} %get-tuple-elem, ...), custom_call_target="tpu_custom_call" | custom-call | tf_op jit(solution)/shard_map/conv/pallas_call | solution.py:38
  49.9 2.2 %collective-permute-start.8 = (bf16[192,128]{1,0:T(8,128)(2,1)S(1)}, bf16[192,128]{1,0:T(8,128)(2,1)S(1)}, u32[]{:S(2)}, u32[]{:S(2)}) collective-permute-start(bf16[192,128]{1,0:T(8,128)(2,1)S(1)} %get-tuple-element.48), channel_id=1, source_target_pairs={{1,0},{2,1},{3,2},{4,3},{5,4},{6,5},{7,6},{8,7},{9,8},{10,9},{11,1... | collective-permute-start | bytes 147464 | tf_op jit(solution)/shard_map/ppermute | solution.py:374
  52.1 9.4 %taps.1 = (f32[192,128]{1,0:T(8,128)S(1)}, f32[192,768]{1,0:T(8,128)S(1)}) custom-call(bf16[10,192,512]{2,1,0:T(8,128)(2,1)S(1)} %get-tuple-element.40.field_ref, bf16[4,192,512]{2,1,0:T(8,128)(2,1)S(1)} %get-tuple-element.38.grad_ref.own_ref, bf16[4,192,512]{2,1,0:T(8,128)(2,1)S(1)} %get-tuple-element.41.normed_in_ref, ...), custom_call_target="tpu_custom_call" | custom-call | tf_op jit(solution)/shard_map/taps/pallas_call | solution.py:38
  61.8 3.7 %collective-permute-start.4 = (f32[96,1664]{1,0:T(8,128)S(1)}, f32[96,1664]{1,0:T(8,128)S(1)}, u32[]{:S(2)}, u32[]{:S(2)}) collective-permute-start(f32[96,1664]{1,0:T(8,128)S(1)} %slice_select_fusion), channel_id=1, source_target_pairs={{0,1},{1,0},{2,3},{3,2},{4,5},{5,4},{6,7},{7,6},{8,9},{9,8},{10,11... | collective-permute-start | bytes 1916936 | tf_op jit(solution)/shard_map/ppermute | solution.py:385
  67.5 6.0 %collective-permute-start.9 = (bf16[192,1408]{1,0:T(8,128)(2,1)S(1)}, bf16[192,1408]{1,0:T(8,128)(2,1)S(1)}, u32[]{:S(2)}, u32[]{:S(2)}) collective-permute-start(bf16[192,1408]{1,0:T(8,128)(2,1)S(1)} %pad_maximum_fusion.3), channel_id=1, source_target_pairs={{0,16},{16,32},{32,48},{48,64},{64,80},{80,96},{96,112},{1,17},{17... | collective-permute-start | bytes 1622024 | tf_op jit(solution)/shard_map/ppermute | solution.py:378
  73.6 3.1 %collective-permute-start.6 = (bf16[24,1664]{1,0:T(8,128)(2,1)S(1)}, bf16[24,1664]{1,0:T(8,128)(2,1)S(1)}, u32[]{:S(2)}, u32[]{:S(2)}) collective-permute-start(bf16[24,1664]{1,0:T(8,128)(2,1)S(1)} %select_convert_fusion.1), channel_id=1, source_target_pairs={{0,8},{1,9},{2,10},{3,11},{4,12},{5,13},{6,14},{7,15},{8,0},{9,1},... | collective-permute-start | bytes 239624 | tf_op jit(solution)/shard_map/ppermute | solution.py:385
  76.7 2.1 %collective-permute-done.6 = bf16[24,1664]{1,0:T(8,128)(2,1)S(1)} collective-permute-done((bf16[24,1664]{1,0:T(8,128)(2,1)S(1)}, bf16[24,1664]{1,0:T(8,128)(2,1)S(1)}, u32[]{:S(2)}, u32[]{:S(2)}) %collective-permute-start.6) | collective-permute-done | bytes 79904 | tf_op jit(solution)/shard_map/ppermute | solution.py:385
  78.8 4.9 %collective-permute-done.10.below_ref = bf16[192,1408]{1,0:T(8,128)(2,1)S(1)} collective-permute-done((bf16[192,1408]{1,0:T(8,128)(2,1)S(1)}, bf16[192,1408]{1,0:T(8,128)(2,1)S(1)}, u32[]{:S(2)}, u32[]{:S(2)}) %collective-permute-start.10) | collective-permute-done | bytes 540704 | tf_op jit(solution)/shard_map/ppermute | solution.py:379
  83.7 11.9 %collective-permute-done.9.above_ref = bf16[192,1408]{1,0:T(8,128)(2,1)S(1)} collective-permute-done((bf16[192,1408]{1,0:T(8,128)(2,1)S(1)}, bf16[192,1408]{1,0:T(8,128)(2,1)S(1)}, u32[]{:S(2)}, u32[]{:S(2)}) %collective-permute-start.9) | collective-permute-done | bytes 540704 | tf_op jit(solution)/shard_map/ppermute | solution.py:378
  95.6 1.8 %collective-permute-start.11 = (bf16[24,1664]{1,0:T(8,128)(2,1)S(1)}, bf16[24,1664]{1,0:T(8,128)(2,1)S(1)}, u32[]{:S(2)}, u32[]{:S(2)}) collective-permute-start(bf16[24,1664]{1,0:T(8,128)(2,1)S(1)} %reduce-precision_convert_fusion.1), channel_id=1, source_target_pairs={{0,32},{1,33},{2,34},{3,35},{4,36},{5,37},{6,38},{7,39},{8,40},{9,... | collective-permute-start | bytes 239624 | tf_op jit(solution)/shard_map/ppermute | solution.py:385
  99.3 3.0 %collective-permute-start.12 = (bf16[24,1664]{1,0:T(8,128)(2,1)S(1)}, bf16[24,1664]{1,0:T(8,128)(2,1)S(1)}, u32[]{:S(2)}, u32[]{:S(2)}) collective-permute-start(bf16[24,1664]{1,0:T(8,128)(2,1)S(1)} %fusion.2), channel_id=1, source_target_pairs={{0,64},{1,65},{2,66},{3,67},{4,68},{5,69},{6,70},{7,71},{8,72},{9,... | collective-permute-start | bytes 239624 | tf_op jit(solution)/shard_map/ppermute | solution.py:385
  104.3 3.3 %collective-permute-done.13 = bf16[24,1664]{1,0:T(8,128)(2,1)S(1)} collective-permute-done((bf16[24,1664]{1,0:T(8,128)(2,1)S(1)}, bf16[24,1664]{1,0:T(8,128)(2,1)S(1)}, u32[]{:S(2)}, u32[]{:S(2)}) %collective-permute-start.13) | collective-permute-done | bytes 79904 | tf_op jit(solution)/shard_map/ppermute | solution.py:385
  107.6 3.5 %collective-permute-start.14 = (bf16[24,1664]{1,0:T(8,128)(2,1)S(1)}, bf16[24,1664]{1,0:T(8,128)(2,1)S(1)}, u32[]{:S(2)}, u32[]{:S(2)}) collective-permute-start(bf16[24,1664]{1,0:T(8,128)(2,1)S(1)} %fusion.1), channel_id=1, source_target_pairs={{0,16},{1,17},{2,18},{3,19},{4,20},{5,21},{6,22},{7,23},{8,24},{9,... | collective-permute-start | bytes 239624 | tf_op jit(solution)/shard_map/ppermute | solution.py:385
  111.1 2.2 %collective-permute-done.14 = bf16[24,1664]{1,0:T(8,128)(2,1)S(1)} collective-permute-done((bf16[24,1664]{1,0:T(8,128)(2,1)S(1)}, bf16[24,1664]{1,0:T(8,128)(2,1)S(1)}, u32[]{:S(2)}, u32[]{:S(2)}) %collective-permute-start.14) | collective-permute-done | bytes 79904 | tf_op jit(solution)/shard_map/ppermute | solution.py:385
  113.4 2.0 %collective-permute-start.15 = (bf16[24,1664]{1,0:T(8,128)(2,1)S(1)}, bf16[24,1664]{1,0:T(8,128)(2,1)S(1)}, u32[]{:S(2)}, u32[]{:S(2)}) collective-permute-start(bf16[24,1664]{1,0:T(8,128)(2,1)S(1)} %reduce-precision_convert_fusion), channel_id=1, source_target_pairs={{0,8},{1,9},{2,10},{3,11},{4,12},{5,13},{6,14},{7,15},{8,0},{9,1},... | collective-permute-start | bytes 239624 | tf_op jit(solution)/shard_map/ppermute | solution.py:385
  115.4 2.9 %collective-permute-done.15 = bf16[24,1664]{1,0:T(8,128)(2,1)S(1)} collective-permute-done((bf16[24,1664]{1,0:T(8,128)(2,1)S(1)}, bf16[24,1664]{1,0:T(8,128)(2,1)S(1)}, u32[]{:S(2)}, u32[]{:S(2)}) %collective-permute-start.15) | collective-permute-done | bytes 79904 | tf_op jit(solution)/shard_map/ppermute | solution.py:385
  118.6 4.8 %collective-permute-done.16 = bf16[48,1664]{1,0:T(8,128)(2,1)S(1)} collective-permute-done((bf16[48,1664]{1,0:T(8,128)(2,1)S(1)}, bf16[48,1664]{1,0:T(8,128)(2,1)S(1)}, u32[]{:S(2)}, u32[]{:S(2)}) %collective-permute-start.16) | collective-permute-done | bytes 159776 | tf_op jit(solution)/shard_map/ppermute | solution.py:385
  123.4 6.6 %collective-permute-start.17 = (bf16[96,1664]{1,0:T(8,128)(2,1)S(1)}, bf16[96,1664]{1,0:T(8,128)(2,1)S(1)}, u32[]{:S(2)}, u32[]{:S(2)}) collective-permute-start(bf16[96,1664]{1,0:T(8,128)(2,1)S(1)} %pad_maximum_fusion.5), channel_id=1, source_target_pairs={{0,1},{1,0},{2,3},{3,2},{4,5},{5,4},{6,7},{7,6},{8,9},{9,8},{10,11... | collective-permute-start | bytes 958472 | tf_op jit(solution)/shard_map/ppermute | solution.py:385
  130.0 7.7 %input.1 = bf16[4,192,512]{2,1,0:T(8,128)(2,1)S(1)} custom-call(bf16[4,192,512]{2,1,0:T(8,128)(2,1)S(1)} %get-tuple-element.38.grad_ref.own_ref, bf16[192,128]{1,0:T(8,128)(2,1)S(1)} %get-tuple-element.51.rims_ref, bf16[192,1408]{1,0:T(8,128)(2,1)S(1)} %collective-permute-done.9.above_ref, bf16[192,1408]{1,0:T(8,128)(2,1)S(1)} %collective-permute-done.10.below_ref, ...), custom_call_target="tpu_custom_call" | custom-call | tf_op jit(solution)/shard_map/input/pallas_call | solution.py:38
  (112 shorter events, 28.0 us)
Async XLA Ops:
  4.1 3.9 %collective-permute-start = (bf16[192,128]{1,0:T(8,128)(2,1)S(1)}, bf16[192,128]{1,0:T(8,128)(2,1)S(1)}, u32[]{:S(2)}, u32[]{:S(2)}) collective-permute-start(bf16[192,128]{1,0:T(8,128)(2,1)S(1)} %get-tuple-element.33), channel_id=1, source_target_pairs={{0,1},{1,2},{2,3},{3,4},{4,5},{5,6},{6,7},{7,8},{8,9},{9,10},{10,1... | collective-permute-start | bytes 147464 | tf_op jit(solution)/shard_map/ppermute | solution.py:374
  6.8 3.8 %collective-permute-start.1 = (bf16[192,128]{1,0:T(8,128)(2,1)S(1)}, bf16[192,128]{1,0:T(8,128)(2,1)S(1)}, u32[]{:S(2)}, u32[]{:S(2)}) collective-permute-start(bf16[192,128]{1,0:T(8,128)(2,1)S(1)} %get-tuple-element.34), channel_id=1, source_target_pairs={{1,0},{2,1},{3,2},{4,3},{5,4},{6,5},{7,6},{8,7},{9,8},{10,9},{11,1... | collective-permute-start | bytes 147464 | tf_op jit(solution)/shard_map/ppermute | solution.py:374
  6.9 12.4 %copy-start.11 = (bf16[192,4,450]{2,1,0:T(4,128)(2,1)S(1)}, bf16[192,4,450]{2,1,0:T(4,128)(2,1)}, u32[]{:S(2)}) copy-start(bf16[192,4,450]{2,1,0:T(4,128)(2,1)} %param.21) | copy-start | bytes 2073604
  10.7 8.8 %copy-start.1 = (bf16[192,128]{1,0:T(8,128)(2,1)}, bf16[192,128]{1,0:T(8,128)(2,1)S(1)}, u32[]{:S(2)}) copy-start(bf16[192,128]{1,0:T(8,128)(2,1)S(1)} %get-tuple-element.89.rims_ref) | copy-start | bytes 147460
  11.5 27.2 %collective-permute-start.2 = (bf16[192,1408]{1,0:T(8,128)(2,1)}, bf16[192,1408]{1,0:T(8,128)(2,1)}, u32[]{:S(2)}, u32[]{:S(2)}) collective-permute-start(bf16[192,1408]{1,0:T(8,128)(2,1)} %pad_maximum_fusion.1), channel_id=1, source_target_pairs={{0,16},{16,32},{32,48},{48,64},{64,80},{80,96},{96,112},{1,17},{17... | collective-permute-start | bytes 1622024 | tf_op jit(solution)/shard_map/ppermute | solution.py:378
  17.1 2.3 %copy-start.10 = (s32[192,4,450]{2,1,0:T(4,128)S(1)}, s32[192,4,450]{2,1,0:T(4,128)}, u32[]{:S(2)}) copy-start(s32[192,4,450]{2,1,0:T(4,128)} %param.18) | copy-start | bytes 4147204
  18.0 20.8 %collective-permute-start.3 = (bf16[192,1408]{1,0:T(8,128)(2,1)}, bf16[192,1408]{1,0:T(8,128)(2,1)}, u32[]{:S(2)}, u32[]{:S(2)}) collective-permute-start(bf16[192,1408]{1,0:T(8,128)(2,1)} %pad_maximum_fusion.2), channel_id=1, source_target_pairs={{16,0},{32,16},{48,32},{64,48},{80,64},{96,80},{112,96},{17,1},{33... | collective-permute-start | bytes 1622024 | tf_op jit(solution)/shard_map/ppermute | solution.py:379
  23.6 1.7 %copy-start = (bf16[768,192]{0,1:T(8,128)(2,1)S(1)}, bf16[768,192]{0,1:T(8,128)(2,1)}, u32[]{:S(2)}) copy-start(bf16[768,192]{0,1:T(8,128)(2,1)} %param.27) | copy-start | bytes 884740
  27.9 10.8 %copy-start.2 = (bf16[192,128]{1,0:T(8,128)(2,1)S(1)}, bf16[192,128]{1,0:T(8,128)(2,1)}, u32[]{:S(2)}) copy-start(bf16[192,128]{1,0:T(8,128)(2,1)} %copy-done.1) | copy-start | bytes 147460
  27.9 10.8 %copy-start.4 = (f32[192,128]{1,0:T(8,128)S(1)}, f32[192,128]{1,0:T(8,128)}, u32[]{:S(2)}) copy-start(f32[192,128]{1,0:T(8,128)} %pad.24.chan_ref) | copy-start | bytes 294916
  49.8 15.6 %collective-permute-start.7 = (bf16[192,128]{1,0:T(8,128)(2,1)S(1)}, bf16[192,128]{1,0:T(8,128)(2,1)S(1)}, u32[]{:S(2)}, u32[]{:S(2)}) collective-permute-start(bf16[192,128]{1,0:T(8,128)(2,1)S(1)} %get-tuple-element.47), channel_id=1, source_target_pairs={{0,1},{1,2},{2,3},{3,4},{4,5},{5,6},{6,7},{7,8},{8,9},{9,10},{10,1... | collective-permute-start | bytes 147464 | tf_op jit(solution)/shard_map/ppermute | solution.py:374
  49.9 15.5 %collective-permute-start.8 = (bf16[192,128]{1,0:T(8,128)(2,1)S(1)}, bf16[192,128]{1,0:T(8,128)(2,1)S(1)}, u32[]{:S(2)}, u32[]{:S(2)}) collective-permute-start(bf16[192,128]{1,0:T(8,128)(2,1)S(1)} %get-tuple-element.48), channel_id=1, source_target_pairs={{1,0},{2,1},{3,2},{4,3},{5,4},{6,5},{7,6},{8,7},{9,8},{10,9},{11,1... | collective-permute-start | bytes 147464 | tf_op jit(solution)/shard_map/ppermute | solution.py:374
  61.8 5.4 %collective-permute-start.4 = (f32[96,1664]{1,0:T(8,128)S(1)}, f32[96,1664]{1,0:T(8,128)S(1)}, u32[]{:S(2)}, u32[]{:S(2)}) collective-permute-start(f32[96,1664]{1,0:T(8,128)S(1)} %slice_select_fusion), channel_id=1, source_target_pairs={{0,1},{1,0},{2,3},{3,2},{4,5},{5,4},{6,7},{7,6},{8,9},{9,8},{10,11... | collective-permute-start | bytes 1916936 | tf_op jit(solution)/shard_map/ppermute | solution.py:385
  65.5 18.2 %collective-permute-start.10 = (bf16[192,1408]{1,0:T(8,128)(2,1)S(1)}, bf16[192,1408]{1,0:T(8,128)(2,1)S(1)}, u32[]{:S(2)}, u32[]{:S(2)}) collective-permute-start(bf16[192,1408]{1,0:T(8,128)(2,1)S(1)} %pad_maximum_fusion.4), channel_id=1, source_target_pairs={{16,0},{32,16},{48,32},{64,48},{80,64},{96,80},{112,96},{17,1},{33... | collective-permute-start | bytes 1622024 | tf_op jit(solution)/shard_map/ppermute | solution.py:379
  67.3 6.2 %collective-permute-start.5 = (bf16[48,1664]{1,0:T(8,128)(2,1)S(1)}, bf16[48,1664]{1,0:T(8,128)(2,1)S(1)}, u32[]{:S(2)}, u32[]{:S(2)}) collective-permute-start(bf16[48,1664]{1,0:T(8,128)(2,1)S(1)} %select_convert_fusion), channel_id=1, source_target_pairs={{0,4},{1,5},{2,6},{3,7},{4,0},{5,1},{6,2},{7,3},{8,12},{9,13},{10,... | collective-permute-start | bytes 479240 | tf_op jit(solution)/shard_map/ppermute | solution.py:385
  67.5 28.1 %collective-permute-start.9 = (bf16[192,1408]{1,0:T(8,128)(2,1)S(1)}, bf16[192,1408]{1,0:T(8,128)(2,1)S(1)}, u32[]{:S(2)}, u32[]{:S(2)}) collective-permute-start(bf16[192,1408]{1,0:T(8,128)(2,1)S(1)} %pad_maximum_fusion.3), channel_id=1, source_target_pairs={{0,16},{16,32},{32,48},{48,64},{64,80},{80,96},{96,112},{1,17},{17... | collective-permute-start | bytes 1622024 | tf_op jit(solution)/shard_map/ppermute | solution.py:378
  73.6 5.2 %collective-permute-start.6 = (bf16[24,1664]{1,0:T(8,128)(2,1)S(1)}, bf16[24,1664]{1,0:T(8,128)(2,1)S(1)}, u32[]{:S(2)}, u32[]{:S(2)}) collective-permute-start(bf16[24,1664]{1,0:T(8,128)(2,1)S(1)} %select_convert_fusion.1), channel_id=1, source_target_pairs={{0,8},{1,9},{2,10},{3,11},{4,12},{5,13},{6,14},{7,15},{8,0},{9,1},... | collective-permute-start | bytes 239624 | tf_op jit(solution)/shard_map/ppermute | solution.py:385
  95.6 3.7 %collective-permute-start.11 = (bf16[24,1664]{1,0:T(8,128)(2,1)S(1)}, bf16[24,1664]{1,0:T(8,128)(2,1)S(1)}, u32[]{:S(2)}, u32[]{:S(2)}) collective-permute-start(bf16[24,1664]{1,0:T(8,128)(2,1)S(1)} %reduce-precision_convert_fusion.1), channel_id=1, source_target_pairs={{0,32},{1,33},{2,34},{3,35},{4,36},{5,37},{6,38},{7,39},{8,40},{9,... | collective-permute-start | bytes 239624 | tf_op jit(solution)/shard_map/ppermute | solution.py:385
  99.3 4.9 %collective-permute-start.12 = (bf16[24,1664]{1,0:T(8,128)(2,1)S(1)}, bf16[24,1664]{1,0:T(8,128)(2,1)S(1)}, u32[]{:S(2)}, u32[]{:S(2)}) collective-permute-start(bf16[24,1664]{1,0:T(8,128)(2,1)S(1)} %fusion.2), channel_id=1, source_target_pairs={{0,64},{1,65},{2,66},{3,67},{4,68},{5,69},{6,70},{7,71},{8,72},{9,... | collective-permute-start | bytes 239624 | tf_op jit(solution)/shard_map/ppermute | solution.py:385
  104.2 3.3 %collective-permute-start.13 = (bf16[24,1664]{1,0:T(8,128)(2,1)S(1)}, bf16[24,1664]{1,0:T(8,128)(2,1)S(1)}, u32[]{:S(2)}, u32[]{:S(2)}) collective-permute-start(bf16[24,1664]{1,0:T(8,128)(2,1)S(1)} %fusion), channel_id=1, source_target_pairs={{0,2},{1,3},{2,0},{3,1},{4,6},{5,7},{6,4},{7,5},{8,10},{9,11},{10,... | collective-permute-start | bytes 239624 | tf_op jit(solution)/shard_map/ppermute | solution.py:385
  107.6 5.7 %collective-permute-start.14 = (bf16[24,1664]{1,0:T(8,128)(2,1)S(1)}, bf16[24,1664]{1,0:T(8,128)(2,1)S(1)}, u32[]{:S(2)}, u32[]{:S(2)}) collective-permute-start(bf16[24,1664]{1,0:T(8,128)(2,1)S(1)} %fusion.1), channel_id=1, source_target_pairs={{0,16},{1,17},{2,18},{3,19},{4,20},{5,21},{6,22},{7,23},{8,24},{9,... | collective-permute-start | bytes 239624 | tf_op jit(solution)/shard_map/ppermute | solution.py:385
  113.4 4.9 %collective-permute-start.15 = (bf16[24,1664]{1,0:T(8,128)(2,1)S(1)}, bf16[24,1664]{1,0:T(8,128)(2,1)S(1)}, u32[]{:S(2)}, u32[]{:S(2)}) collective-permute-start(bf16[24,1664]{1,0:T(8,128)(2,1)S(1)} %reduce-precision_convert_fusion), channel_id=1, source_target_pairs={{0,8},{1,9},{2,10},{3,11},{4,12},{5,13},{6,14},{7,15},{8,0},{9,1},... | collective-permute-start | bytes 239624 | tf_op jit(solution)/shard_map/ppermute | solution.py:385
  118.3 5.1 %collective-permute-start.16 = (bf16[48,1664]{1,0:T(8,128)(2,1)S(1)}, bf16[48,1664]{1,0:T(8,128)(2,1)S(1)}, u32[]{:S(2)}, u32[]{:S(2)}) collective-permute-start(bf16[48,1664]{1,0:T(8,128)(2,1)S(1)} %pad_maximum_fusion.6), channel_id=1, source_target_pairs={{0,4},{1,5},{2,6},{3,7},{4,0},{5,1},{6,2},{7,3},{8,12},{9,13},{10,... | collective-permute-start | bytes 479240 | tf_op jit(solution)/shard_map/ppermute | solution.py:385
  123.4 15.8 %collective-permute-start.17 = (bf16[96,1664]{1,0:T(8,128)(2,1)S(1)}, bf16[96,1664]{1,0:T(8,128)(2,1)S(1)}, u32[]{:S(2)}, u32[]{:S(2)}) collective-permute-start(bf16[96,1664]{1,0:T(8,128)(2,1)S(1)} %pad_maximum_fusion.5), channel_id=1, source_target_pairs={{0,1},{1,0},{2,3},{3,2},{4,5},{5,4},{6,7},{7,6},{8,9},{9,8},{10,11... | collective-permute-start | bytes 958472 | tf_op jit(solution)/shard_map/ppermute | solution.py:385
  (14 other events, 16.9 us)

commit v2 on v1

v2 whole, which is shorter than its diff:
```python
import functools
import math

import jax
import jax.numpy as jnp
from jax import lax
from jax.experimental import pallas as pl
from jax.experimental.pallas import tpu as pltpu
from jax.sharding import PartitionSpec as P

C = 192
FF = 768
WORDS = FF // 4
GROUP = 64
RADIUS = 3
TAPS = 2 * RADIUS + 1
ROWS = 4
COLS = 450
WIDE = COLS + 2 * RADIUS
LANES = 512
MAIN = 384
TAIL = COLS + RADIUS - MAIN
PACK = 1408
RIM = MAIN * RADIUS + TAIL * RADIUS - (PACK - 128)
CH = 16
F32 = jnp.float32
BF16 = jnp.bfloat16
VMEM_LIMIT = 18 * 1024 * 1024


def params():
    return pltpu.CompilerParams(vmem_limit_bytes=VMEM_LIMIT)


def resident(kernel, name, out_shape, *args, scratch=(), space=pltpu.VMEM, aliases=()):
    spec = pl.BlockSpec(memory_space=pltpu.VMEM)
    return pl.pallas_call(
        kernel,
        out_shape=out_shape,
        in_specs=[pl.BlockSpec(memory_space=space)] * len(args),
        out_specs=jax.tree.map(lambda _: spec, out_shape),
        scratch_shapes=list(scratch),
        input_output_aliases=dict(aliases),
        cost_estimate=pl.CostEstimate(flops=0, bytes_accessed=0, transcendentals=0),
        compiler_params=params(),
        name=name,
    )(*args)


def lane_iota(shape):
    return lax.broadcasted_iota(jnp.int32, shape, len(shape) - 1)


def nt_dot(a, b):
    return lax.dot_general(a, b, (((1,), (1,)), ((), ())), preferred_element_type=F32)


def nn_dot(a, b):
    return jnp.dot(a, b, preferred_element_type=F32)


def rims_of(rows, head):
    first = RADIUS if head else COLS
    base = RIM + (RADIUS * ROWS if head else 0)
    lane = lane_iota((C, 128))
    total = jnp.zeros((C, 128), F32)
    for r, row in enumerate(rows):
        start = base + RADIUS * r
        moved = pltpu.roll(row, (start - first) % LANES, 1)[:, :128]
        keep = (lane >= start) & (lane < start + RADIUS)
        total = jnp.where(keep, moved, total)
    return total.astype(BF16)


def pack(rows, ref):
    lane = lane_iota((C, 256))
    tails = jnp.zeros((C, 256), F32)
    for k, value in enumerate(rows):
        ref[:, MAIN * k : MAIN * (k + 1)] = value[:, :MAIN].astype(BF16)
        wide = jnp.concatenate([value[:, MAIN:], jnp.zeros((C, 128), F32)], axis=1)
        moved = pltpu.roll(wide, TAIL * k, 1) if k else wide
        keep = (lane >= TAIL * k) & (lane < TAIL * (k + 1))
        tails = jnp.where(keep, moved, tails)
    ref[:, MAIN * RADIUS :] = tails.astype(BF16)


def send_rows(rows, head_ref, tail_ref, up_ref, down_ref):
    pack(rows[:RADIUS], up_ref)
    pack(rows[ROWS - RADIUS :], down_ref)
    head_ref[...] = rims_of(rows, True)
    tail_ref[...] = rims_of(rows, False)


def with_rims(first_tile, last_tile, rims, r):
    lane = lane_iota((C, 128))
    left = pltpu.roll(rims, (-RIM - RADIUS * r) % 128, 1)
    spot = RADIUS + COLS - MAIN
    right = pltpu.roll(rims, (spot - RIM - RADIUS * (ROWS + r)) % 128, 1)
    first_tile = jnp.where(lane < RADIUS, left, first_tile)
    last_tile = jnp.where((lane >= spot) & (lane < spot + RADIUS), right, last_tile)
    return first_tile.astype(BF16), last_tile.astype(BF16)


def fill_halo(field_ref, ref, first_row, source_row):
    rims = ref[:, PACK - 128 :].astype(F32)
    tails = ref[:, MAIN * RADIUS :].astype(F32)
    lane = lane_iota((C, 128))
    for k in range(RADIUS):
        moved = pltpu.roll(tails, (-TAIL * k) % 256, 1) if k else tails
        last = jnp.where(lane < TAIL, moved[:, :128], 0.0)
        first, last = with_rims(
            ref[:, MAIN * k : MAIN * k + 128].astype(F32), last, rims, source_row + k
        )
        field_ref[first_row + k, :, :128] = first
        field_ref[first_row + k, :, 128:MAIN] = ref[:, MAIN * k + 128 : MAIN * (k + 1)]
        field_ref[first_row + k, :, MAIN:] = last


def fetch(sources, targets, sems, meanwhile=None):
    copies = [
        pltpu.make_async_copy(source, target, sems.at[k])
        for k, (source, target) in enumerate(zip(sources, targets))
    ]
    for copy in copies:
        copy.start()
    if meanwhile is not None:
        meanwhile()
    for copy in copies:
        copy.wait()


def restore_kernel(
    words_hbm, low_hbm, high_hbm, own_ref, head_ref, tail_ref, up_ref, down_ref,
    words_ref, low_ref, high_ref, bounds, sems,
):
    fetch((words_hbm, low_hbm, high_hbm), (words_ref, low_ref, high_ref), sems)
    nwords = C // 4
    bounds[...] = jnp.zeros(bounds.shape, F32)
    for g in range(C // GROUP):
        low = low_ref[g].astype(F32)
        bounds[0, g, :, :COLS] = low
        bounds[1, g, :, :COLS] = high_ref[g].astype(F32) - low
    per = GROUP // 4
    row_id = lax.broadcasted_iota(jnp.int32, (C, C), 0)
    col_id = lax.broadcasted_iota(jnp.int32, (C, C), 1)
    place = (row_id == 4 * (col_id % nwords) + col_id // nwords).astype(F32).astype(BF16)
    lane = lane_iota((C, LANES))
    rows = []
    for r in range(ROWS):
        pieces = []
        words = words_ref[:, r, :]
        words = jnp.concatenate([words, jnp.zeros((nwords, LANES - COLS), jnp.int32)], axis=1)
        for j in range(4):
            code = (jnp.right_shift(words, 2 * j) & 3).astype(F32)
            for g in range(C // GROUP):
                low = bounds[0, g, r : r + 1, :]
                span = bounds[1, g, r : r + 1, :]
                value = low + code[g * per : (g + 1) * per] * span / 3.0
                pieces.append(value.astype(BF16))
        mixed = jnp.concatenate(pieces, axis=0)
        value = nn_dot(place, mixed)
        value = pltpu.roll(value, RADIUS, 1)
        value = jnp.where((lane >= RADIUS) & (lane < RADIUS + COLS), value, 0.0)
        rows.append(value)
        own_ref[r] = value.astype(BF16)
    send_rows(rows, head_ref, tail_ref, up_ref, down_ref)


def natural_order(order):
    row_id = lax.broadcasted_iota(jnp.int32, (FF, FF), 0)
    col_id = lax.broadcasted_iota(jnp.int32, (FF, FF), 1)
    order[...] = (col_id == 4 * (row_id % WORDS) + row_id // WORDS).astype(F32).astype(BF16)


def reorder(value, order):
    high = value.astype(BF16)
    rest = (value - high.astype(F32)).astype(BF16)
    return nn_dot(high, order[...]) + nn_dot(rest, order[...])


def mlp_kernel(
    words_hbm, low_hbm, high_hbm, grad_hbm, chan_hbm, w_out_hbm, w_in_hbm,
    hidden_ref, normed_ref, g_ref, sums_ref, rows_ref,
    words_ref, low_ref, high_ref, grad_ref, chan_ref, w_out_ref, w_in_ref, sems,
    order, w_out_p, w_in_p, lifted, active, bounds, grads,
):
    fetch(
        (w_out_hbm, w_in_hbm, low_hbm, high_hbm, grad_hbm, words_hbm, chan_hbm),
        (w_out_ref, w_in_ref, low_ref, high_ref, grad_ref, words_ref, chan_ref),
        sems,
        functools.partial(natural_order, order),
    )
    w_out_p[...] = nt_dot(order[...], w_out_ref[...]).astype(BF16)
    w_in_p[...] = nt_dot(w_in_ref[...], order[...]).astype(BF16)
    groups = FF // GROUP
    bounds[...] = jnp.zeros(bounds.shape, F32)
    grads[...] = grad_ref[...].astype(F32)
    for g in range(groups):
        low = low_ref[g].astype(F32)
        span = high_ref[g].astype(F32) - low
        for k in range(4):
            hidden = low + float(k) * span / 3.0
            cdf = 0.5 * (1.0 + lax.erf(hidden * 0.7071067811865476))
            density = jnp.exp(-0.5 * hidden * hidden) * 0.3989422804014327
            bounds[k, g, :, :COLS] = hidden * cdf
            bounds[4 + k, g, :, :COLS] = cdf + hidden * density
    g_sum = jnp.zeros((C, FF), F32)
    total = jnp.zeros((C, 1), F32)
    for r in range(ROWS):
        grad = grads[:, r, :]
        grad = jnp.concatenate([grad, jnp.zeros((C, LANES - COLS), F32)], axis=1)
        total = total + jnp.sum(grad, axis=1, keepdims=True)
        rows_ref[r] = grad.astype(BF16)
        scaled = (chan_ref[:, 3:4] * grad).astype(BF16)
        lifted[...] = nn_dot(w_out_p[...], scaled)
        words_row = words_ref[:, r, :]
        words_row = jnp.concatenate(
            [words_row, jnp.zeros((WORDS, LANES - COLS), jnp.int32)], axis=1
        )
        for g in range(groups):
            words = words_row[CH * g : CH * (g + 1)]
            values = [
                jnp.broadcast_to(bounds[k, g, r : r + 1, :], (CH, LANES)) for k in range(8)
            ]
            for j in range(4):
                odd = (words & (1 << (2 * j))) != 0
                upper = (words & (2 << (2 * j))) != 0
                act = jnp.where(
                    upper,
                    jnp.where(odd, values[3], values[2]),
                    jnp.where(odd, values[1], values[0]),
                )
                slope = jnp.where(
                    upper,
                    jnp.where(odd, values[7], values[6]),
                    jnp.where(odd, values[5], values[4]),
                )
                place = slice(WORDS * j + CH * g, WORDS * j + CH * (g + 1))
                active[place, :] = act.astype(BF16)
                hidden_ref[r, place, :] = (lifted[place, :] * slope).astype(BF16)
        normed_ref[r] = nn_dot(w_in_p[...], hidden_ref[r])
        g_sum = g_sum + nt_dot(rows_ref[r], active[...])
    sums_ref[...] = jnp.where(lane_iota((C, 128)) == 52, total, 0.0)
    g_ref[...] = reorder(g_sum, order)


OWN = tuple(range(RADIUS, RADIUS + ROWS))
HALO = tuple(range(RADIUS)) + tuple(range(RADIUS + ROWS, 2 * RADIUS + ROWS))


def stencil(cell, used, taps_ref, wide_taps, partial, emit, flip):
    def body(block, carry):
        chans = pl.ds(pl.multiple_of(block * CH, CH), CH)
        taps = taps_ref[chans, :]
        for t in range(TAPS * TAPS):
            source = TAPS * TAPS - 1 - t if flip else t
            wide_taps[t] = jnp.broadcast_to(taps[:, source : source + 1], (CH, 128))
        for tile in range(LANES // 128):
            lanes = slice(128 * tile, 128 * (tile + 1))
            cells = {r: cell(r, chans, lanes).astype(F32) for r in used}
            for q in range(TAPS):
                sums = [None] * ROWS
                for p in range(TAPS):
                    tap = wide_taps[TAPS * p + q]
                    for i in range(ROWS):
                        if i + p in cells:
                            term = tap * cells[i + p]
                            sums[i] = term if sums[i] is None else sums[i] + term
                for i in range(ROWS):
                    partial[q, i, :, lanes] = sums[i]
        for i in range(ROWS):
            total = partial[0, i]
            for q in range(1, TAPS):
                total = total + pltpu.roll(partial[q, i], LANES - q, 1)
            emit(chans, i, total)
        return carry

    lax.fori_loop(0, C // CH, body, 0)


def own_kernel(own_ref, rims_ref, taps_ref, filled_ref, total_ref, wide_taps, partial, *, flip):
    rims = rims_ref[...].astype(F32)
    for r in range(ROWS):
        first, last = with_rims(
            own_ref[r, :, :128].astype(F32), own_ref[r, :, MAIN:].astype(F32), rims, r
        )
        filled_ref[r, :, :128] = first
        filled_ref[r, :, 128:MAIN] = own_ref[r, :, 128:MAIN]
        filled_ref[r, :, MAIN:] = last

    def emit(chans, i, total):
        total_ref[i, chans, :] = total

    def cell(r, chans, lanes):
        return filled_ref[r - RADIUS, chans, lanes]

    stencil(cell, OWN, taps_ref, wide_taps, partial, emit, flip)


def conv_kernel(
    filled_ref, total_ref, above_ref, below_ref, taps_ref, chan_ref, normed_ref,
    field_ref, grad_ref, head_ref, tail_ref, up_ref, down_ref, normed_in_ref, sums_ref,
    conv, sums, wide_taps, partial,
):
    fill_halo(field_ref, above_ref, 0, ROWS - RADIUS)
    fill_halo(field_ref, below_ref, RADIUS + ROWS, 0)
    field_ref[RADIUS : RADIUS + ROWS] = filled_ref[...]

    def emit(chans, i, total):
        conv[i, chans, :] = total_ref[i, chans, :] + (total + chan_ref[chans, 0:1])

    def cell(r, chans, lanes):
        return field_ref[r, chans, lanes]

    stencil(cell, HALO, taps_ref, wide_taps, partial, emit, False)
    gain = jnp.broadcast_to(chan_ref[:, 1:2], (C, 128))
    bias = jnp.broadcast_to(chan_ref[:, 2:3], (C, 128))
    sums[...] = jnp.zeros(sums.shape, F32)
    rows = []
    for r in range(ROWS):
        for tile in range(LANES // 128):
            lanes = slice(128 * tile, 128 * (tile + 1))
            value = conv[r, :, lanes]
            centered = value - jnp.sum(value, axis=0, keepdims=True) * (1.0 / C)
            variance = jnp.sum(centered * centered, axis=0, keepdims=True) * (1.0 / C)
            inv_std = lax.rsqrt(variance + 1e-06)
            normed = centered * inv_std
            normed_in_ref[r, :, lanes] = (normed * gain + bias).astype(BF16)
            back = normed_ref[r, :, lanes]
            sums[0] += back * normed
            sums[1] += back
            dn = back * gain
            mean_dn = jnp.sum(dn, axis=0, keepdims=True) * (1.0 / C)
            mean_dx = jnp.sum(dn * normed, axis=0, keepdims=True) * (1.0 / C)
            grad = inv_std * (dn - mean_dn - normed * mean_dx)
            if 128 * (tile + 1) > COLS:
                grad = jnp.where(lane_iota((C, 128)) < COLS - 128 * tile, grad, 0.0)
            grad = grad.astype(BF16).astype(F32)
            sums[2] += grad
            conv[r, :, lanes] = grad
        grad = pltpu.roll(conv[r], RADIUS, 1)
        rows.append(grad)
        grad_ref[r] = grad.astype(BF16)
    send_rows(rows, head_ref, tail_ref, up_ref, down_ref)
    lane = lane_iota((C, 128))
    total = jnp.zeros((C, 128), F32)
    for k in range(3):
        total = jnp.where(lane == 49 + k, jnp.sum(sums[k], axis=1, keepdims=True), total)
    sums_ref[...] = total


def taps_kernel(field_ref, grad_ref, normed_in_ref, hidden_ref, sums_ref, h_ref, order):
    row = lax.broadcasted_iota(jnp.int32, (CH, 256), 0)
    diagonal = lane_iota((CH, 256)) % CH == row
    row = lax.broadcasted_iota(jnp.int32, (128, 128), 0)
    pick = (TAPS * (row // CH) == lane_iota((128, 128))).astype(F32).astype(BF16)
    cells = (ROWS + 2 * RADIUS) * CH
    lane = lane_iota((CH, 128))

    def body(block, carry):
        chans = pl.ds(pl.multiple_of(block * CH, CH), CH)
        field = field_ref[:, chans, :].reshape(cells, LANES)
        grads = [grad_ref[i, chans, :] for i in range(ROWS)]
        moved = [
            pltpu.roll(grads[i], (q - RADIUS) % LANES, 1) if q != RADIUS else grads[i]
            for q in range(TAPS)
            for i in range(ROWS)
        ]
        product = nt_dot(jnp.concatenate(moved, axis=0), field)
        product = jnp.concatenate(
            [product, jnp.zeros((TAPS * ROWS * CH, 256 - cells), F32)], axis=1
        )
        totals = []
        for q in range(TAPS):
            total = None
            for i in range(ROWS):
                start = (q * ROWS + i) * CH
                value = jnp.where(diagonal, product[start : start + CH], 0.0)
                value = (pltpu.roll(value, 256 - CH * i, 1) if i else value)[:, :128]
                total = value if total is None else total + value
            totals.append(jnp.where(lane < TAPS * CH, total, 0.0))
        total = jnp.concatenate(totals, axis=0)
        high = total.astype(BF16)
        rest = (total - high.astype(F32)).astype(BF16)
        result = nn_dot(high, pick) + nn_dot(rest, pick)
        sums = jnp.zeros((CH, 128), F32)
        for q in range(TAPS):
            value = result[q * CH : (q + 1) * CH]
            value = pltpu.roll(value, q, 1) if q else value
            sums = jnp.where(lane % TAPS == q, value, sums)
        sums = jnp.where(lane < TAPS * TAPS, sums, 0.0)
        sums_ref[chans, :] = sums
        return carry

    lax.fori_loop(0, C // CH, body, 0, unroll=2)
    natural_order(order)
    h_sum = jnp.zeros((C, FF), F32)
    for r in range(ROWS):
        h_sum = h_sum + nt_dot(normed_in_ref[r], hidden_ref[r])
    h_ref[...] = reorder(h_sum, order)


def input_kernel(
    total_ref, above_ref, below_ref, taps_ref, grad_ref, out_ref, field, wide_taps, partial
):
    fill_halo(field, above_ref, 0, ROWS - RADIUS)
    fill_halo(field, below_ref, RADIUS, 0)

    def emit(chans, i, total):
        total = total + total_ref[i, chans, :]
        out_ref[i, chans, :] = (grad_ref[i, chans, :].astype(F32) + total).astype(BF16)

    def cell(r, chans, lanes):
        return field[r if r < RADIUS else r - ROWS, chans, lanes]

    stencil(cell, HALO, taps_ref, wide_taps, partial, emit, True)


def final_kernel(total_ref, chan_ref, w_out_ref, g_ref, h_ref, taps_ref, vectors_ref, *, factor):
    g_sum = total_ref[:, :FF].astype(F32) * factor
    h_ref[...] = total_ref[:, FF : 2 * FF].astype(F32) * factor
    sums = total_ref[:, 2 * FF :].astype(F32) * factor
    scale = chan_ref[:, 3:4]
    g_ref[...] = g_sum * scale
    total = jnp.sum(g_sum * w_out_ref[...].astype(F32), axis=1, keepdims=True)
    sum_grad = sums[:, 52:53]
    lane = lane_iota((C, 128))
    sums = jnp.where(lane == 53, total + chan_ref[:, 4:5] * sum_grad, sums)
    sums = jnp.where(lane == 52, sum_grad * scale, sums)
    flat = jnp.transpose(sums)
    for p in range(TAPS):
        taps_ref[p] = flat[TAPS * p : TAPS * (p + 1)]
    vectors_ref[...] = flat[48:56]


def ring(axis, count):
    ahead = [(i, (i + 1) % count) for i in range(count)]
    return functools.partial(lax.ppermute, axis_name=axis, perm=ahead), functools.partial(
        lax.ppermute, axis_name=axis, perm=[(b, a) for a, b in ahead]
    )


def add_rims(head, tail, up, down):
    ahead, behind = ring("lon", lax.axis_size("lon"))
    rims = ahead(tail) + behind(head)
    up = jnp.concatenate([up[:, : PACK - 128], up[:, PACK - 128 :] + rims], axis=1)
    down = jnp.concatenate([down[:, : PACK - 128], down[:, PACK - 128 :] + rims], axis=1)
    return rims, up, down


def lat_rows(up, down):
    count = lax.axis_size("lat")
    above = lax.ppermute(down, "lat", [(i, i + 1) for i in range(count - 1)])
    below = lax.ppermute(up, "lat", [(i + 1, i) for i in range(count - 1)])
    return above, below


def swap(value, bits):
    count = lax.axis_size("lat") * lax.axis_size("lon")
    return lax.ppermute(value, ("lat", "lon"), [(i, i ^ bits) for i in range(count)])


def rounded(value):
    return lax.reduce_precision(value, 8, 7)


def all_sum(value, hooks):
    me = lax.axis_index("lat") * lax.axis_size("lon") + lax.axis_index("lon")
    split = (1, 4, 8)
    step = 0
    for bit in split:
        value = hooks(step, value)
        step += 1
        half = value.shape[0] // 2
        upper = (me & bit) != 0
        low, high = value[:half], value[half:]
        send = jnp.where(upper, low, high)
        keep = jnp.where(upper, high, low)
        value = keep + swap(send.astype(BF16) if bit > 1 else send, bit).astype(F32)
    for first, second in ((32, 64), (2, 16)):
        value = hooks(step, value)
        step += 1
        mine = rounded(value)
        sent = mine.astype(BF16)
        near, far, both = (swap(sent, b).astype(F32) for b in (first, second, first | second))
        value = (mine + near) + (far + both)
    value = rounded(value).astype(BF16)
    for bit in reversed(split):
        value = hooks(step, value)
        step += 1
        upper = (me & bit) != 0
        other = swap(value, bit)
        value = jnp.concatenate(
            [jnp.where(upper, other, value), jnp.where(upper, value, other)], axis=0
        )
    return hooks(step, value)


def local(
    stash_input, input_low, input_high, stash_hidden, hidden_low, hidden_high, grad_out,
    kernel, conv_bias, norm_gain, norm_bias, w_in, w_out, out_bias, layer_scale,
):
    tie = lax.optimization_barrier

    def shape(*dims, dtype=F32):
        return jax.ShapeDtypeStruct(dims, dtype)

    field_shape = shape(ROWS, C, LANES, dtype=BF16)
    total_shape = shape(ROWS, C, LANES)
    rim_shape = shape(C, 128, dtype=BF16)
    pack_shape = shape(C, PACK, dtype=BF16)
    sums_shape = shape(C, 128)
    weight_shape = shape(C, FF)
    own, head, tail, up, down = resident(
        restore_kernel,
        "restore",
        (field_shape, rim_shape, rim_shape, pack_shape, pack_shape),
        stash_input,
        input_low,
        input_high,
        scratch=[
            pltpu.VMEM(stash_input.shape, jnp.int32),
            pltpu.VMEM(input_low.shape, BF16),
            pltpu.VMEM(input_high.shape, BF16),
            pltpu.VMEM((2, C // GROUP, ROWS, LANES), F32),
            pltpu.SemaphoreType.DMA((3,)),
        ],
        space=pl.ANY,
    )
    rims, up, down = add_rims(head, tail, up, down)
    above, below = lat_rows(up, down)

    taps = jnp.pad(kernel.reshape(C, TAPS * TAPS), ((0, 0), (0, 128 - TAPS * TAPS)))
    chan = jnp.stack([conv_bias, norm_gain, norm_bias, layer_scale, out_bias], axis=1)
    chan = jnp.pad(chan, ((0, 0), (0, 123)))
    w_out_t = jnp.transpose(w_out)
    stencil_scratch = [
        pltpu.VMEM((TAPS * TAPS, CH, 128), F32),
        pltpu.VMEM((TAPS, ROWS, CH, LANES), F32),
    ]
    hidden_back, normed_back, g_part, sums_a, grad_rows = resident(
        mlp_kernel,
        "mlp",
        (
            shape(ROWS, FF, LANES, dtype=BF16),
            total_shape,
            weight_shape,
            sums_shape,
            field_shape,
        ),
        stash_hidden,
        hidden_low,
        hidden_high,
        grad_out,
        chan,
        w_out_t,
        w_in,
        space=pl.ANY,
        scratch=[
            pltpu.VMEM(stash_hidden.shape, jnp.int32),
            pltpu.VMEM(hidden_low.shape, BF16),
            pltpu.VMEM(hidden_high.shape, BF16),
            pltpu.VMEM(grad_out.shape, BF16),
            pltpu.VMEM(chan.shape, F32),
            pltpu.VMEM((C, FF), BF16),
            pltpu.VMEM((C, FF), BF16),
            pltpu.SemaphoreType.DMA((7,)),
            pltpu.VMEM((FF, FF), BF16),
            pltpu.VMEM((FF, C), BF16),
            pltpu.VMEM((C, FF), BF16),
            pltpu.VMEM((FF, LANES), F32),
            pltpu.VMEM((FF, LANES), BF16),
            pltpu.VMEM((8, FF // GROUP, ROWS, LANES), F32),
            pltpu.VMEM(grad_out.shape, F32),
        ],
    )

    def over_own(own, rims, flip, name):
        return resident(
            functools.partial(own_kernel, flip=flip),
            name,
            (field_shape, total_shape),
            own,
            rims,
            taps,
            scratch=stencil_scratch,
        )

    filled, total = over_own(own, rims, False, "conv_own")
    field, grad_own, head, tail, up, down, normed_in, sums_b = resident(
        conv_kernel,
        "conv",
        (
            shape(ROWS + 2 * RADIUS, C, LANES, dtype=BF16),
            field_shape,
            rim_shape,
            rim_shape,
            pack_shape,
            pack_shape,
            field_shape,
            sums_shape,
        ),
        filled,
        total,
        above,
        below,
        taps,
        chan,
        normed_back,
        scratch=[pltpu.VMEM((ROWS, C, LANES), F32), pltpu.VMEM((3, C, 128), F32)]
        + stencil_scratch,
    )

    sums_c, h_part = resident(
        taps_kernel,
        "taps",
        (sums_shape, weight_shape),
        field,
        grad_own,
        normed_in,
        hidden_back,
        scratch=[pltpu.VMEM((FF, FF), BF16)],
    )
    rims, up, down = add_rims(head, tail, up, down)
    above, below = lat_rows(up, down)
    late = {"own": grad_own, "above": above, "below": below}

    def hooks(step, value):
        if step == 1:
            value, late["own"] = tie((value, late["own"]))
            late["total"] = over_own(late["own"], rims, True, "input_own")[1]
        elif step == 2:
            value, late["total"] = tie((value, late["total"]))
        elif step == 3:
            value, late["total"], late["above"], late["below"] = tie(
                (value, late["total"], late["above"], late["below"])
            )
        elif step == 5:
            value, late["total"] = tie((value, late["total"]))
            late["input"] = resident(
                input_kernel,
                "input",
                field_shape,
                late["total"],
                late["above"],
                late["below"],
                taps,
                grad_rows,
                scratch=[pltpu.VMEM((2 * RADIUS, C, LANES), BF16)] + stencil_scratch,
            )
        elif step == 6:
            value, late["input"] = tie((value, late["input"]))
            late["input"] = jnp.transpose(late["input"][:, :, :COLS], (1, 0, 2))
        elif step == 7:
            value, late["input"] = tie((value, late["input"]))
        return value

    summed = all_sum(jnp.concatenate([g_part, h_part, sums_a + sums_b + sums_c], axis=1), hooks)
    cells = ROWS * lax.axis_size("lat") * COLS * lax.axis_size("lon")
    g_sum, h_sum, grad_kernel, vectors = resident(
        functools.partial(final_kernel, factor=1.0 / math.sqrt(cells)),
        "final",
        (weight_shape, weight_shape, shape(TAPS, TAPS, C), shape(8, C)),
        summed,
        chan,
        w_out_t,
    )
    return (
        late["input"],
        jnp.transpose(grad_kernel, (2, 0, 1)),
        vectors[3],
        vectors[1],
        vectors[2],
        h_sum,
        jnp.transpose(g_sum),
        vectors[4],
        vectors[5],
    )


def solution(mesh):
    split = P(None, "lat", "lon")
    return jax.shard_map(
        local,
        mesh=mesh,
        in_specs=(split,) * 7 + (P(),) * 8,
        out_specs=(split,) + (P(),) * 8,
        check_vma=False,
    )
```

time: 144 us -> 130 us (0.903)
  waiting for transfers between devices: 43.4 us -> 30.3 us
  Pallas kernels: 36.2 us -> 46.5 us
  local copies, waits for them, and re-layouts: 14.2 us -> 9.45 us
  starting transfers between devices: 43.5 us -> 39.7 us
  other arithmetic: 4.46 us -> 2.57 us
    ppermute x18 -> x20, waiting for transfers between devices: 43.4 us -> 30.3 us  [the longest x12 14.9 us: swap(): lax.ppermute(value, ('lat', 'lon'), [(i, i ^ bits) for i in range(count)])]
    pallas_call x5 -> x8, Pallas kernels: 36.2 us -> 46.5 us  [resident(): pl.pallas_call(kernel, out_shape=out_shape, in_specs=[pl.BlockSpec(memory...]
    ppermute x18 -> x20, starting transfers between devices: 43.5 us -> 39.7 us  [the longest x12 21.2 us: swap(): lax.ppermute(value, ('lat', 'lon'), [(i, i ^ bits) for i in range(count)])]
    unnamed x46 -> x29, local copies, waits for them, and re-layouts: 9.06 us -> 6.04 us
    pad x4 -> x0, local copies, waits for them, and re-layouts: 2.94 us -> none  [by_row(): return jnp.pad(moved, ((0, 0), (0, 0), (0, LANES - moved.shape[2])))]
  transfers between devices with their start and end apart: 18 -> 20, of which waited for: 13 -> 11; matrix products, arithmetic and copies ran while one was open for 6% -> 4% of each run, Pallas kernels for 17% -> 27%
where the time goes in v2:
time: 130 us
  Pallas kernels  46.5 us (36%)
  starting transfers between devices  39.7 us (31%)
  waiting for transfers between devices  30.3 us (23%)
  local copies, waits for them, and re-layouts  9.45 us (7%)
  other arithmetic  2.57 us (2%)
    pallas_call x8, Pallas kernels, resident(): pl.pallas_call(kernel, out_shape=out_shape, in_specs=[pl.BlockSpec(memory...  46.5 us
    ppermute x12, starting transfers between devices, swap(): lax.ppermute(value, ('lat', 'lon'), [(i, i ^ bits) for i in range(count)])  21.2 us
    ppermute x12, waiting for transfers between devices, swap(): lax.ppermute(value, ('lat', 'lon'), [(i, i ^ bits) for i in range(count)])  14.9 us
    ppermute x2, waiting for transfers between devices, lat_rows(): above = lax.ppermute(down, 'lat', [(i, i + 1) for i in range(count - 1)])  11.7 us
    ppermute x2, starting transfers between devices, lat_rows(): above = lax.ppermute(down, 'lat', [(i, i + 1) for i in range(count - 1)])  10.7 us
    unnamed x29, local copies, waits for them, and re-layouts  6.04 us
    ppermute x4, starting transfers between devices, add_rims(): rims = ahead(tail) + behind(head)  5.08 us
    ppermute x4, waiting for transfers between devices, add_rims(): rims = ahead(tail) + behind(head)  3.74 us
  transfers between devices with their start and end apart: 20, of which 11 were waited for; matrix products, arithmetic and copies ran while one was open for 4% of the time, Pallas kernels for 27%

profile of v2, /device:TPU:1, one launch (start us, length us, event | category | flops | bytes accessed | tf_op | source)
XLA Modules:
  0.0 129.6 jit_solution(11089655832306773217)
XLA Ops:
  4.3 2.8 %collective-permute-start = (bf16[192,128]{1,0:T(8,128)(2,1)S(1)}, bf16[192,128]{1,0:T(8,128)(2,1)S(1)}, u32[]{:S(2)}, u32[]{:S(2)}) collective-permute-start(bf16[192,128]{1,0:T(8,128)(2,1)S(1)} %get-tuple-element.52), channel_id=1, source_target_pairs={{0,1},{1,2},{2,3},{3,4},{4,5},{5,6},{6,7},{7,8},{8,9},{9,10},{10,1... | collective-permute-start | bytes 147464 | tf_op jit(solution)/shard_map/ppermute | solution.py:445
  8.2 2.6 %collective-permute-done.1 = bf16[192,128]{1,0:T(8,128)(2,1)S(1)} collective-permute-done((bf16[192,128]{1,0:T(8,128)(2,1)S(1)}, bf16[192,128]{1,0:T(8,128)(2,1)S(1)}, u32[]{:S(2)}, u32[]{:S(2)}) %collective-permute-start.1) | collective-permute-done | bytes 49184 | tf_op jit(solution)/shard_map/ppermute | solution.py:445
  11.9 4.8 %collective-permute-start.2 = (bf16[192,1408]{1,0:T(8,128)(2,1)}, bf16[192,1408]{1,0:T(8,128)(2,1)S(1)}, u32[]{:S(2)}, u32[]{:S(2)}) collective-permute-start(bf16[192,1408]{1,0:T(8,128)(2,1)} %pad_maximum_fusion.2), channel_id=1, source_target_pairs={{0,16},{16,32},{32,48},{48,64},{64,80},{80,96},{96,112},{1,17},{17... | collective-permute-start | bytes 1622024 | tf_op jit(solution)/shard_map/ppermute | solution.py:453
  23.9 7.8 %mlp.1 = (bf16[4,768,512]{2,1,0:T(8,128)(2,1)S(1)}, f32[4,192,512]{2,1,0:T(8,128)S(1)}, f32[192,768]{1,0:T(8,128)S(1)}, f32[192,128]{1,0:T(8,128)S(1)}, bf16[4,192,512]{2,1,0:T(8,128)(2,1)S(1)}) custom-call(s32[192,4,450]{2,1,0:T(4,128)S(1)} %copy-done, bf16[12,4,450]{2,1,0:T(4,128)(2,1)S(1)} %copy-done.5, bf16[12,4,450]{2,1,0:T(4,128)(2,1)S(1)} %copy-done.6, ...), custom_call_target="tpu_custom_call" | custom-call | tf_op jit(solution)/shard_map/mlp/pallas_call | solution.py:37
  31.7 6.2 %conv_own.1 = (bf16[4,192,512]{2,1,0:T(8,128)(2,1)S(1)}, f32[4,192,512]{2,1,0:T(8,128)S(1)}) custom-call(bf16[4,192,512]{2,1,0:T(8,128)(2,1)S(1)} %get-tuple-element.51.own_ref, bf16[192,128]{1,0:T(8,128)(2,1)S(1)} %get-tuple-element.121.rims_ref, f32[192,128]{1,0:T(8,128)S(1)} %pad.9.taps_ref), custom_call_target="tpu_custom_call" | custom-call | tf_op jit(solution)/shard_map/conv_own/pallas_call | solution.py:37
  39.1 8.7 %conv.1 = (bf16[10,192,512]{2,1,0:T(8,128)(2,1)S(1)}, bf16[4,192,512]{2,1,0:T(8,128)(2,1)S(1)}, bf16[192,128]{1,0:T(8,128)(2,1)S(1)}, bf16[192,128]{1,0:T(8,128)...) custom-call(bf16[4,192,512]{2,1,0:T(8,128)(2,1)S(1)} %get-tuple-elem, ...), custom_call_target="tpu_custom_call" | custom-call | tf_op jit(solution)/shard_map/conv/pallas_call | solution.py:37
  47.9 2.2 %collective-permute-start.7 = (bf16[192,128]{1,0:T(8,128)(2,1)S(1)}, bf16[192,128]{1,0:T(8,128)(2,1)S(1)}, u32[]{:S(2)}, u32[]{:S(2)}) collective-permute-start(bf16[192,128]{1,0:T(8,128)(2,1)S(1)} %get-tuple-element.70), channel_id=1, source_target_pairs={{1,0},{2,1},{3,2},{4,3},{5,4},{6,5},{7,6},{8,7},{9,8},{10,9},{11,1... | collective-permute-start | bytes 147464 | tf_op jit(solution)/shard_map/ppermute | solution.py:445
  50.2 9.4 %taps.1 = (f32[192,128]{1,0:T(8,128)S(1)}, f32[192,768]{1,0:T(8,128)S(1)}) custom-call(bf16[10,192,512]{2,1,0:T(8,128)(2,1)S(1)} %get-tuple-element.59.field_ref, bf16[4,192,512]{2,1,0:T(8,128)(2,1)S(1)} %get-tuple-element.68.grad_ref.own_ref, bf16[4,192,512]{2,1,0:T(8,128)(2,1)S(1)} %get-tuple-element.61.normed_in_ref, ...), custom_call_target="tpu_custom_call" | custom-call | tf_op jit(solution)/shard_map/taps/pallas_call | solution.py:37
  59.8 3.6 %collective-permute-start.4 = (f32[96,1664]{1,0:T(8,128)S(1)}, f32[96,1664]{1,0:T(8,128)S(1)}, u32[]{:S(2)}, u32[]{:S(2)}) collective-permute-start(f32[96,1664]{1,0:T(8,128)S(1)} %slice_select_fusion), channel_id=1, source_target_pairs={{0,1},{1,0},{2,3},{3,2},{4,5},{5,4},{6,7},{7,6},{8,9},{9,8},{10,11... | collective-permute-start | bytes 1916936 | tf_op jit(solution)/shard_map/ppermute | solution.py:460
  65.6 5.9 %collective-permute-start.9 = (bf16[192,1408]{1,0:T(8,128)(2,1)S(1)}, bf16[192,1408]{1,0:T(8,128)(2,1)S(1)}, u32[]{:S(2)}, u32[]{:S(2)}) collective-permute-start(bf16[192,1408]{1,0:T(8,128)(2,1)S(1)} %pad_maximum_fusion.4), channel_id=1, source_target_pairs={{0,16},{16,32},{32,48},{48,64},{64,80},{80,96},{96,112},{1,17},{17... | collective-permute-start | bytes 1622024 | tf_op jit(solution)/shard_map/ppermute | solution.py:453
  71.4 6.6 %input_own.1 = (bf16[4,192,512]{2,1,0:T(8,128)(2,1)}, f32[4,192,512]{2,1,0:T(8,128)S(1)}) custom-call(bf16[4,192,512]{2,1,0:T(8,128)(2,1)S(1)} %get-tuple-element.68.grad_ref.own_ref, bf16[192,128]{1,0:T(8,128)(2,1)S(1)} %get-tuple-element.119.rims_ref, f32[192,128]{1,0:T(8,128)S(1)} %pad.9.taps_ref), custom_call_target="tpu_custom_call" | custom-call | tf_op jit(solution)/shard_map/input_own/pallas_call | solution.py:37
  78.1 3.1 %collective-permute-start.8 = (bf16[24,1664]{1,0:T(8,128)(2,1)S(1)}, bf16[24,1664]{1,0:T(8,128)(2,1)S(1)}, u32[]{:S(2)}, u32[]{:S(2)}) collective-permute-start(bf16[24,1664]{1,0:T(8,128)(2,1)S(1)} %select_convert_fusion.1), channel_id=1, source_target_pairs={{0,8},{1,9},{2,10},{3,11},{4,12},{5,13},{6,14},{7,15},{8,0},{9,1},... | collective-permute-start | bytes 239624 | tf_op jit(solution)/shard_map/ppermute | solution.py:460
  83.0 10.5 %collective-permute-done.9.above_ref = bf16[192,1408]{1,0:T(8,128)(2,1)S(1)} collective-permute-done((bf16[192,1408]{1,0:T(8,128)(2,1)S(1)}, bf16[192,1408]{1,0:T(8,128)(2,1)S(1)}, u32[]{:S(2)}, u32[]{:S(2)}) %collective-permute-start.9) | collective-permute-done | bytes 540704 | tf_op jit(solution)/shard_map/ppermute | solution.py:453
  93.5 2.0 %collective-permute-start.11 = (bf16[24,1664]{1,0:T(8,128)(2,1)S(1)}, bf16[24,1664]{1,0:T(8,128)(2,1)S(1)}, u32[]{:S(2)}, u32[]{:S(2)}) collective-permute-start(bf16[24,1664]{1,0:T(8,128)(2,1)S(1)} %reduce-precision_convert_fusion.1), channel_id=1, source_target_pairs={{0,32},{1,33},{2,34},{3,35},{4,36},{5,37},{6,38},{7,39},{8,40},{9,... | collective-permute-start | bytes 239624 | tf_op jit(solution)/shard_map/ppermute | solution.py:460
  95.5 2.5 %collective-permute-start.12 = (bf16[24,1664]{1,0:T(8,128)(2,1)S(1)}, bf16[24,1664]{1,0:T(8,128)(2,1)S(1)}, u32[]{:S(2)}, u32[]{:S(2)}) collective-permute-start(bf16[24,1664]{1,0:T(8,128)(2,1)S(1)} %reduce-precision_convert_fusion.1), channel_id=1, source_target_pairs={{0,64},{1,65},{2,66},{3,67},{4,68},{5,69},{6,70},{7,71},{8,72},{9,... | collective-permute-start | bytes 239624 | tf_op jit(solution)/shard_map/ppermute | solution.py:460
  98.0 3.0 %collective-permute-done.12 = bf16[24,1664]{1,0:T(8,128)(2,1)S(1)} collective-permute-done((bf16[24,1664]{1,0:T(8,128)(2,1)S(1)}, bf16[24,1664]{1,0:T(8,128)(2,1)S(1)}, u32[]{:S(2)}, u32[]{:S(2)}) %collective-permute-start.12) | collective-permute-done | bytes 79904 | tf_op jit(solution)/shard_map/ppermute | solution.py:460
  101.0 2.2 %collective-permute-done.13 = bf16[24,1664]{1,0:T(8,128)(2,1)S(1)} collective-permute-done((bf16[24,1664]{1,0:T(8,128)(2,1)S(1)}, bf16[24,1664]{1,0:T(8,128)(2,1)S(1)}, u32[]{:S(2)}, u32[]{:S(2)}) %collective-permute-start.13) | collective-permute-done | bytes 79904 | tf_op jit(solution)/shard_map/ppermute | solution.py:460
  103.3 2.9 %collective-permute-start.15 = (bf16[24,1664]{1,0:T(8,128)(2,1)S(1)}, bf16[24,1664]{1,0:T(8,128)(2,1)S(1)}, u32[]{:S(2)}, u32[]{:S(2)}) collective-permute-start(bf16[24,1664]{1,0:T(8,128)(2,1)S(1)} %fusion), channel_id=1, source_target_pairs={{0,16},{1,17},{2,18},{3,19},{4,20},{5,21},{6,22},{7,23},{8,24},{9,... | collective-permute-start | bytes 239624 | tf_op jit(solution)/shard_map/ppermute | solution.py:460
  107.2 2.2 %collective-permute-done.15 = bf16[24,1664]{1,0:T(8,128)(2,1)S(1)} collective-permute-done((bf16[24,1664]{1,0:T(8,128)(2,1)S(1)}, bf16[24,1664]{1,0:T(8,128)(2,1)S(1)}, u32[]{:S(2)}, u32[]{:S(2)}) %collective-permute-start.15) | collective-permute-done | bytes 79904 | tf_op jit(solution)/shard_map/ppermute | solution.py:460
  109.4 2.0 %collective-permute-done.16 = bf16[24,1664]{1,0:T(8,128)(2,1)S(1)} collective-permute-done((bf16[24,1664]{1,0:T(8,128)(2,1)S(1)}, bf16[24,1664]{1,0:T(8,128)(2,1)S(1)}, u32[]{:S(2)}, u32[]{:S(2)}) %collective-permute-start.16) | collective-permute-done | bytes 79904 | tf_op jit(solution)/shard_map/ppermute | solution.py:460
  111.5 1.9 %collective-permute-start.17 = (bf16[24,1664]{1,0:T(8,128)(2,1)S(1)}, bf16[24,1664]{1,0:T(8,128)(2,1)S(1)}, u32[]{:S(2)}, u32[]{:S(2)}) collective-permute-start(bf16[24,1664]{1,0:T(8,128)(2,1)S(1)} %reduce-precision_convert_fusion), channel_id=1, source_target_pairs={{0,8},{1,9},{2,10},{3,11},{4,12},{5,13},{6,14},{7,15},{8,0},{9,1},... | collective-permute-start | bytes 239624 | tf_op jit(solution)/shard_map/ppermute | solution.py:460
  113.4 5.3 %input.1 = bf16[4,192,512]{2,1,0:T(8,128)(2,1)S(1)} custom-call(f32[4,192,512]{2,1,0:T(8,128)S(1)} %get-tuple-element.79.total_ref, bf16[192,1408]{1,0:T(8,128)(2,1)S(1)} %collective-permute-done.9.above_ref, bf16[192,1408]{1,0:T(8,128)(2,1)S(1)} %collective-permute-done.10.below_ref, f32[192,128]{1,0:T(8,128)S(1)} %pad.9.taps_ref, ...), custom_call_target="tpu_custom_call" | custom-call | tf_op jit(solution)/shard_map/input/pallas_call | solution.py:37
  119.7 3.3 %collective-permute-done.18 = bf16[48,1664]{1,0:T(8,128)(2,1)S(1)} collective-permute-done((bf16[48,1664]{1,0:T(8,128)(2,1)S(1)}, bf16[48,1664]{1,0:T(8,128)(2,1)S(1)}, u32[]{:S(2)}, u32[]{:S(2)}) %collective-permute-start.18) | collective-permute-done | bytes 159776 | tf_op jit(solution)/shard_map/ppermute | solution.py:460
  123.1 3.1 %collective-permute-start.19 = (bf16[96,1664]{1,0:T(8,128)(2,1)S(1)}, bf16[96,1664]{1,0:T(8,128)(2,1)S(1)}, u32[]{:S(2)}, u32[]{:S(2)}) collective-permute-start(bf16[96,1664]{1,0:T(8,128)(2,1)S(1)} %pad_maximum_fusion.6), channel_id=1, source_target_pairs={{0,1},{1,0},{2,3},{3,2},{4,5},{5,4},{6,7},{7,6},{8,9},{9,8},{10,11... | collective-permute-start | bytes 958472 | tf_op jit(solution)/shard_map/ppermute | solution.py:460
  (90 shorter events, 23.8 us)
Async XLA Ops:
  4.3 3.9 %collective-permute-start = (bf16[192,128]{1,0:T(8,128)(2,1)S(1)}, bf16[192,128]{1,0:T(8,128)(2,1)S(1)}, u32[]{:S(2)}, u32[]{:S(2)}) collective-permute-start(bf16[192,128]{1,0:T(8,128)(2,1)S(1)} %get-tuple-element.52), channel_id=1, source_target_pairs={{0,1},{1,2},{2,3},{3,4},{4,5},{5,6},{6,7},{7,8},{8,9},{9,10},{10,1... | collective-permute-start | bytes 147464 | tf_op jit(solution)/shard_map/ppermute | solution.py:445
  7.1 3.8 %collective-permute-start.1 = (bf16[192,128]{1,0:T(8,128)(2,1)S(1)}, bf16[192,128]{1,0:T(8,128)(2,1)S(1)}, u32[]{:S(2)}, u32[]{:S(2)}) collective-permute-start(bf16[192,128]{1,0:T(8,128)(2,1)S(1)} %get-tuple-element.53), channel_id=1, source_target_pairs={{1,0},{2,1},{3,2},{4,3},{5,4},{6,5},{7,6},{8,7},{9,8},{10,9},{11,1... | collective-permute-start | bytes 147464 | tf_op jit(solution)/shard_map/ppermute | solution.py:445
  11.0 10.8 %copy-start = (s32[192,4,450]{2,1,0:T(4,128)S(1)}, s32[192,4,450]{2,1,0:T(4,128)}, u32[]{:S(2)}) copy-start(s32[192,4,450]{2,1,0:T(4,128)} %words_hbm.2) | copy-start | bytes 4147204
  11.0 10.8 %copy-start.1 = (bf16[768,192]{0,1:T(8,128)(2,1)S(1)}, bf16[768,192]{0,1:T(8,128)(2,1)}, u32[]{:S(2)}) copy-start(bf16[768,192]{0,1:T(8,128)(2,1)} %param.27) | copy-start | bytes 884740
  11.0 10.8 %copy-start.5 = (bf16[12,4,450]{2,1,0:T(4,128)(2,1)S(1)}, bf16[12,4,450]{2,1,0:T(4,128)(2,1)}, u32[]{:S(2)}) copy-start(bf16[12,4,450]{2,1,0:T(4,128)(2,1)} %low_hbm.2) | copy-start | bytes 129604
  11.0 10.8 %copy-start.6 = (bf16[12,4,450]{2,1,0:T(4,128)(2,1)S(1)}, bf16[12,4,450]{2,1,0:T(4,128)(2,1)}, u32[]{:S(2)}) copy-start(bf16[12,4,450]{2,1,0:T(4,128)(2,1)} %high_hbm.2) | copy-start | bytes 129604
  11.9 27.2 %collective-permute-start.2 = (bf16[192,1408]{1,0:T(8,128)(2,1)}, bf16[192,1408]{1,0:T(8,128)(2,1)S(1)}, u32[]{:S(2)}, u32[]{:S(2)}) collective-permute-start(bf16[192,1408]{1,0:T(8,128)(2,1)} %pad_maximum_fusion.2), channel_id=1, source_target_pairs={{0,16},{16,32},{32,48},{48,64},{64,80},{80,96},{96,112},{1,17},{17... | collective-permute-start | bytes 1622024 | tf_op jit(solution)/shard_map/ppermute | solution.py:453
  17.6 21.6 %collective-permute-start.3 = (bf16[192,1408]{1,0:T(8,128)(2,1)}, bf16[192,1408]{1,0:T(8,128)(2,1)}, u32[]{:S(2)}, u32[]{:S(2)}) collective-permute-start(bf16[192,1408]{1,0:T(8,128)(2,1)} %pad_maximum_fusion.3), channel_id=1, source_target_pairs={{16,0},{32,16},{48,32},{64,48},{80,64},{96,80},{112,96},{17,1},{33... | collective-permute-start | bytes 1622024 | tf_op jit(solution)/shard_map/ppermute | solution.py:454
  47.8 15.6 %collective-permute-start.6 = (bf16[192,128]{1,0:T(8,128)(2,1)S(1)}, bf16[192,128]{1,0:T(8,128)(2,1)S(1)}, u32[]{:S(2)}, u32[]{:S(2)}) collective-permute-start(bf16[192,128]{1,0:T(8,128)(2,1)S(1)} %get-tuple-element.69), channel_id=1, source_target_pairs={{0,1},{1,2},{2,3},{3,4},{4,5},{5,6},{6,7},{7,8},{8,9},{9,10},{10,1... | collective-permute-start | bytes 147464 | tf_op jit(solution)/shard_map/ppermute | solution.py:445
  47.9 15.6 %collective-permute-start.7 = (bf16[192,128]{1,0:T(8,128)(2,1)S(1)}, bf16[192,128]{1,0:T(8,128)(2,1)S(1)}, u32[]{:S(2)}, u32[]{:S(2)}) collective-permute-start(bf16[192,128]{1,0:T(8,128)(2,1)S(1)} %get-tuple-element.70), channel_id=1, source_target_pairs={{1,0},{2,1},{3,2},{4,3},{5,4},{6,5},{7,6},{8,7},{9,8},{10,9},{11,1... | collective-permute-start | bytes 147464 | tf_op jit(solution)/shard_map/ppermute | solution.py:445
  59.8 5.3 %collective-permute-start.4 = (f32[96,1664]{1,0:T(8,128)S(1)}, f32[96,1664]{1,0:T(8,128)S(1)}, u32[]{:S(2)}, u32[]{:S(2)}) collective-permute-start(f32[96,1664]{1,0:T(8,128)S(1)} %slice_select_fusion), channel_id=1, source_target_pairs={{0,1},{1,0},{2,3},{3,2},{4,5},{5,4},{6,7},{7,6},{8,9},{9,8},{10,11... | collective-permute-start | bytes 1916936 | tf_op jit(solution)/shard_map/ppermute | solution.py:460
  63.5 19.5 %collective-permute-start.10 = (bf16[192,1408]{1,0:T(8,128)(2,1)S(1)}, bf16[192,1408]{1,0:T(8,128)(2,1)S(1)}, u32[]{:S(2)}, u32[]{:S(2)}) collective-permute-start(bf16[192,1408]{1,0:T(8,128)(2,1)S(1)} %pad_maximum_fusion.5), channel_id=1, source_target_pairs={{16,0},{32,16},{48,32},{64,48},{80,64},{96,80},{112,96},{17,1},{33... | collective-permute-start | bytes 1622024 | tf_op jit(solution)/shard_map/ppermute | solution.py:454
  65.3 12.7 %collective-permute-start.5 = (bf16[48,1664]{1,0:T(8,128)(2,1)S(1)}, bf16[48,1664]{1,0:T(8,128)(2,1)S(1)}, u32[]{:S(2)}, u32[]{:S(2)}) collective-permute-start(bf16[48,1664]{1,0:T(8,128)(2,1)S(1)} %select_convert_fusion), channel_id=1, source_target_pairs={{0,4},{1,5},{2,6},{3,7},{4,0},{5,1},{6,2},{7,3},{8,12},{9,13},{10,... | collective-permute-start | bytes 479240 | tf_op jit(solution)/shard_map/ppermute | solution.py:460
  65.6 28.0 %collective-permute-start.9 = (bf16[192,1408]{1,0:T(8,128)(2,1)S(1)}, bf16[192,1408]{1,0:T(8,128)(2,1)S(1)}, u32[]{:S(2)}, u32[]{:S(2)}) collective-permute-start(bf16[192,1408]{1,0:T(8,128)(2,1)S(1)} %pad_maximum_fusion.4), channel_id=1, source_target_pairs={{0,16},{16,32},{32,48},{48,64},{64,80},{80,96},{96,112},{1,17},{17... | collective-permute-start | bytes 1622024 | tf_op jit(solution)/shard_map/ppermute | solution.py:453
  78.1 4.9 %collective-permute-start.8 = (bf16[24,1664]{1,0:T(8,128)(2,1)S(1)}, bf16[24,1664]{1,0:T(8,128)(2,1)S(1)}, u32[]{:S(2)}, u32[]{:S(2)}) collective-permute-start(bf16[24,1664]{1,0:T(8,128)(2,1)S(1)} %select_convert_fusion.1), channel_id=1, source_target_pairs={{0,8},{1,9},{2,10},{3,11},{4,12},{5,13},{6,14},{7,15},{8,0},{9,1},... | collective-permute-start | bytes 239624 | tf_op jit(solution)/shard_map/ppermute | solution.py:460
  93.5 4.4 %collective-permute-start.11 = (bf16[24,1664]{1,0:T(8,128)(2,1)S(1)}, bf16[24,1664]{1,0:T(8,128)(2,1)S(1)}, u32[]{:S(2)}, u32[]{:S(2)}) collective-permute-start(bf16[24,1664]{1,0:T(8,128)(2,1)S(1)} %reduce-precision_convert_fusion.1), channel_id=1, source_target_pairs={{0,32},{1,33},{2,34},{3,35},{4,36},{5,37},{6,38},{7,39},{8,40},{9,... | collective-permute-start | bytes 239624 | tf_op jit(solution)/shard_map/ppermute | solution.py:460
  95.5 5.5 %collective-permute-start.12 = (bf16[24,1664]{1,0:T(8,128)(2,1)S(1)}, bf16[24,1664]{1,0:T(8,128)(2,1)S(1)}, u32[]{:S(2)}, u32[]{:S(2)}) collective-permute-start(bf16[24,1664]{1,0:T(8,128)(2,1)S(1)} %reduce-precision_convert_fusion.1), channel_id=1, source_target_pairs={{0,64},{1,65},{2,66},{3,67},{4,68},{5,69},{6,70},{7,71},{8,72},{9,... | collective-permute-start | bytes 239624 | tf_op jit(solution)/shard_map/ppermute | solution.py:460
  98.0 5.2 %collective-permute-start.13 = (bf16[24,1664]{1,0:T(8,128)(2,1)S(1)}, bf16[24,1664]{1,0:T(8,128)(2,1)S(1)}, u32[]{:S(2)}, u32[]{:S(2)}) collective-permute-start(bf16[24,1664]{1,0:T(8,128)(2,1)S(1)} %reduce-precision_convert_fusion.1), channel_id=1, source_target_pairs={{0,96},{1,97},{2,98},{3,99},{4,100},{5,101},{6,102},{7,103},{8,104... | collective-permute-start | bytes 239624 | tf_op jit(solution)/shard_map/ppermute | solution.py:460
  103.2 3.9 %collective-permute-start.14 = (bf16[24,1664]{1,0:T(8,128)(2,1)S(1)}, bf16[24,1664]{1,0:T(8,128)(2,1)S(1)}, u32[]{:S(2)}, u32[]{:S(2)}) collective-permute-start(bf16[24,1664]{1,0:T(8,128)(2,1)S(1)} %fusion), channel_id=1, source_target_pairs={{0,2},{1,3},{2,0},{3,1},{4,6},{5,7},{6,4},{7,5},{8,10},{9,11},{10,... | collective-permute-start | bytes 239624 | tf_op jit(solution)/shard_map/ppermute | solution.py:460
  103.3 6.1 %collective-permute-start.15 = (bf16[24,1664]{1,0:T(8,128)(2,1)S(1)}, bf16[24,1664]{1,0:T(8,128)(2,1)S(1)}, u32[]{:S(2)}, u32[]{:S(2)}) collective-permute-start(bf16[24,1664]{1,0:T(8,128)(2,1)S(1)} %fusion), channel_id=1, source_target_pairs={{0,16},{1,17},{2,18},{3,19},{4,20},{5,21},{6,22},{7,23},{8,24},{9,... | collective-permute-start | bytes 239624 | tf_op jit(solution)/shard_map/ppermute | solution.py:460
  106.2 5.1 %collective-permute-start.16 = (bf16[24,1664]{1,0:T(8,128)(2,1)S(1)}, bf16[24,1664]{1,0:T(8,128)(2,1)S(1)}, u32[]{:S(2)}, u32[]{:S(2)}) collective-permute-start(bf16[24,1664]{1,0:T(8,128)(2,1)S(1)} %fusion), channel_id=1, source_target_pairs={{0,18},{1,19},{2,16},{3,17},{4,22},{5,23},{6,20},{7,21},{8,26},{9,... | collective-permute-start | bytes 239624 | tf_op jit(solution)/shard_map/ppermute | solution.py:460
  111.5 7.3 %collective-permute-start.17 = (bf16[24,1664]{1,0:T(8,128)(2,1)S(1)}, bf16[24,1664]{1,0:T(8,128)(2,1)S(1)}, u32[]{:S(2)}, u32[]{:S(2)}) collective-permute-start(bf16[24,1664]{1,0:T(8,128)(2,1)S(1)} %reduce-precision_convert_fusion), channel_id=1, source_target_pairs={{0,8},{1,9},{2,10},{3,11},{4,12},{5,13},{6,14},{7,15},{8,0},{9,1},... | collective-permute-start | bytes 239624 | tf_op jit(solution)/shard_map/ppermute | solution.py:460
  118.8 4.2 %collective-permute-start.18 = (bf16[48,1664]{1,0:T(8,128)(2,1)S(1)}, bf16[48,1664]{1,0:T(8,128)(2,1)S(1)}, u32[]{:S(2)}, u32[]{:S(2)}) collective-permute-start(bf16[48,1664]{1,0:T(8,128)(2,1)S(1)} %pad_maximum_fusion.7), channel_id=1, source_target_pairs={{0,4},{1,5},{2,6},{3,7},{4,0},{5,1},{6,2},{7,3},{8,12},{9,13},{10,... | collective-permute-start | bytes 479240 | tf_op jit(solution)/shard_map/ppermute | solution.py:460
  123.1 4.6 %collective-permute-start.19 = (bf16[96,1664]{1,0:T(8,128)(2,1)S(1)}, bf16[96,1664]{1,0:T(8,128)(2,1)S(1)}, u32[]{:S(2)}, u32[]{:S(2)}) collective-permute-start(bf16[96,1664]{1,0:T(8,128)(2,1)S(1)} %pad_maximum_fusion.6), channel_id=1, source_target_pairs={{0,1},{1,0},{2,3},{3,2},{4,5},{5,4},{6,7},{7,6},{8,9},{9,8},{10,11... | collective-permute-start | bytes 958472 | tf_op jit(solution)/shard_map/ppermute | solution.py:460
  (10 other events, 49.8 us)

commit v3 on v2

--- a/solution.py
+++ b/solution.py
@@ -32,7 +32,7 @@
     return pltpu.CompilerParams(vmem_limit_bytes=VMEM_LIMIT)
 
 
-def resident(kernel, name, out_shape, *args, scratch=(), space=pltpu.VMEM, aliases=()):
+def resident(kernel, name, out_shape, *args, scratch=(), space=pltpu.VMEM, cost=0):
     spec = pl.BlockSpec(memory_space=pltpu.VMEM)
     return pl.pallas_call(
         kernel,
@@ -40,8 +40,7 @@
         in_specs=[pl.BlockSpec(memory_space=space)] * len(args),
         out_specs=jax.tree.map(lambda _: spec, out_shape),
         scratch_shapes=list(scratch),
-        input_output_aliases=dict(aliases),
-        cost_estimate=pl.CostEstimate(flops=0, bytes_accessed=0, transcendentals=0),
+        cost_estimate=pl.CostEstimate(flops=0, bytes_accessed=cost, transcendentals=0),
         compiler_params=params(),
         name=name,
     )(*args)
@@ -349,7 +348,15 @@
     sums_ref[...] = total
 
 
-def taps_kernel(field_ref, grad_ref, normed_in_ref, hidden_ref, sums_ref, h_ref, order):
+def weight_kernel(normed_in_ref, hidden_ref, h_ref, order):
+    natural_order(order)
+    h_sum = jnp.zeros((C, FF), F32)
+    for r in range(ROWS):
+        h_sum = h_sum + nt_dot(normed_in_ref[r], hidden_ref[r])
+    h_ref[...] = reorder(h_sum, order)
+
+
+def taps_kernel(field_ref, grad_ref, sums_ref):
     row = lax.broadcasted_iota(jnp.int32, (CH, 256), 0)
     diagonal = lane_iota((CH, 256)) % CH == row
     row = lax.broadcasted_iota(jnp.int32, (128, 128), 0)
@@ -393,18 +400,14 @@
         return carry
 
     lax.fori_loop(0, C // CH, body, 0, unroll=2)
-    natural_order(order)
-    h_sum = jnp.zeros((C, FF), F32)
-    for r in range(ROWS):
-        h_sum = h_sum + nt_dot(normed_in_ref[r], hidden_ref[r])
-    h_ref[...] = reorder(h_sum, order)
-
-
-def input_kernel(
-    total_ref, above_ref, below_ref, taps_ref, grad_ref, out_ref, field, wide_taps, partial
-):
-    fill_halo(field, above_ref, 0, ROWS - RADIUS)
-    fill_halo(field, below_ref, RADIUS, 0)
+
+
+def halo_kernel(above_ref, below_ref, field_ref):
+    fill_halo(field_ref, above_ref, 0, ROWS - RADIUS)
+    fill_halo(field_ref, below_ref, RADIUS, 0)
+
+
+def input_kernel(total_ref, field, taps_ref, grad_ref, out_ref, wide_taps, partial):
 
     def emit(chans, i, total):
         total = total + total_ref[i, chans, :]
@@ -416,10 +419,10 @@
     stencil(cell, HALO, taps_ref, wide_taps, partial, emit, True)
 
 
-def final_kernel(total_ref, chan_ref, w_out_ref, g_ref, h_ref, taps_ref, vectors_ref, *, factor):
+def final_kernel(total_ref, extra_ref, chan_ref, w_out_ref, g_ref, h_ref, taps_ref, vectors_ref, *, factor):
     g_sum = total_ref[:, :FF].astype(F32) * factor
     h_ref[...] = total_ref[:, FF : 2 * FF].astype(F32) * factor
-    sums = total_ref[:, 2 * FF :].astype(F32) * factor
+    sums = (total_ref[:, 2 * FF :].astype(F32) + extra_ref[...]) * factor
     scale = chan_ref[:, 3:4]
     g_ref[...] = g_sum * scale
     total = jnp.sum(g_sum * w_out_ref[...].astype(F32), axis=1, keepdims=True)
@@ -464,19 +467,31 @@
     return lax.reduce_precision(value, 8, 7)
 
 
+def by_index(index, parts):
+    low = jnp.where((index & 1) != 0, parts[1], parts[0])
+    high = jnp.where((index & 1) != 0, parts[3], parts[2])
+    return jnp.where((index & 2) != 0, high, low)
+
+
+def halved(value):
+    core = lax.axis_index("lon") & 1
+    half = value.shape[0] // 2
+    low, high = value[:half], value[half:]
+    sent = jnp.where(core != 0, low, high)
+    return jnp.where(core != 0, high, low) + swap(sent, 1)
+
+
 def all_sum(value, hooks):
     me = lax.axis_index("lat") * lax.axis_size("lon") + lax.axis_index("lon")
-    split = (1, 4, 8)
-    step = 0
-    for bit in split:
-        value = hooks(step, value)
-        step += 1
-        half = value.shape[0] // 2
-        upper = (me & bit) != 0
-        low, high = value[:half], value[half:]
-        send = jnp.where(upper, low, high)
-        keep = jnp.where(upper, high, low)
-        value = keep + swap(send.astype(BF16) if bit > 1 else send, bit).astype(F32)
+    core, z = me & 1, (me >> 2) & 3
+    value = hooks(1, halved(hooks(0, value)))
+    size = value.shape[0] // 4
+    quarters = [value[size * k : size * (k + 1)] for k in range(4)]
+    total = by_index(z, quarters)
+    for k in range(1, 4):
+        total = total + swap(by_index(z ^ k, quarters).astype(BF16), 4 * k).astype(F32)
+    value = total
+    step = 2
     for first, second in ((32, 64), (2, 16)):
         value = hooks(step, value)
         step += 1
@@ -484,16 +499,18 @@
         sent = mine.astype(BF16)
         near, far, both = (swap(sent, b).astype(F32) for b in (first, second, first | second))
         value = (mine + near) + (far + both)
-    value = rounded(value).astype(BF16)
-    for bit in reversed(split):
-        value = hooks(step, value)
-        step += 1
-        upper = (me & bit) != 0
-        other = swap(value, bit)
-        value = jnp.concatenate(
-            [jnp.where(upper, other, value), jnp.where(upper, value, other)], axis=0
-        )
-    return hooks(step, value)
+    value = hooks(4, rounded(value).astype(BF16))
+    parts = [value] + [swap(value, 4 * k) for k in range(1, 4)]
+    value = jnp.concatenate([by_index(z ^ k, parts) for k in range(4)], axis=0)
+    value = hooks(5, value)
+    other = swap(value, 1)
+    width = value.shape[1] - 256
+    taps = value[:, width:].astype(F32) + other[:, width:].astype(F32)
+    taps = taps.reshape(4, C // 8, 2, 128)
+    taps = jnp.transpose(taps, (0, 2, 1, 3)).reshape(C, 128)
+    value, other = value[:, :width], other[:, :width]
+    low, high = jnp.where(core != 0, other, value), jnp.where(core != 0, value, other)
+    return jnp.concatenate([low, high], axis=0), taps
 
 
 def local(
@@ -525,7 +542,7 @@
             pltpu.VMEM((2, C // GROUP, ROWS, LANES), F32),
             pltpu.SemaphoreType.DMA((3,)),
         ],
-        space=pl.ANY,
+        space=pltpu.HBM,
     )
     rims, up, down = add_rims(head, tail, up, down)
     above, below = lat_rows(up, down)
@@ -555,7 +572,7 @@
         chan,
         w_out_t,
         w_in,
-        space=pl.ANY,
+        space=pltpu.HBM,
         scratch=[
             pltpu.VMEM(stash_hidden.shape, jnp.int32),
             pltpu.VMEM(hidden_low.shape, BF16),
@@ -611,12 +628,10 @@
         + stencil_scratch,
     )
 
-    sums_c, h_part = resident(
-        taps_kernel,
-        "taps",
-        (sums_shape, weight_shape),
-        field,
-        grad_own,
+    h_part = resident(
+        weight_kernel,
+        "weight",
+        weight_shape,
         normed_in,
         hidden_back,
         scratch=[pltpu.VMEM((FF, FF), BF16)],
@@ -627,41 +642,51 @@
 
     def hooks(step, value):
         if step == 1:
+            value, late["grad"], _ = tie((value, grad_own, up))
+            late["taps"] = resident(taps_kernel, "taps", sums_shape, field, late["grad"])
+            parts = late["taps"].reshape(4, 2, C // 8, 128)
+            parts = [parts[:, k].reshape(C // 2, 128) for k in range(2)]
+            value = jnp.concatenate([value, *parts], axis=1)
             value, late["own"] = tie((value, late["own"]))
             late["total"] = over_own(late["own"], rims, True, "input_own")[1]
         elif step == 2:
-            value, late["total"] = tie((value, late["total"]))
+            above, below, late["total"] = tie((late["above"], late["below"], late["total"]))
+            halo = resident(
+                halo_kernel,
+                "halo",
+                shape(2 * RADIUS, C, LANES, dtype=BF16),
+                above,
+                below,
+                cost=0,
+            )
+            value, late["total"], late["halo"] = tie((value, late["total"], halo))
         elif step == 3:
-            value, late["total"], late["above"], late["below"] = tie(
-                (value, late["total"], late["above"], late["below"])
-            )
-        elif step == 5:
             value, late["total"] = tie((value, late["total"]))
             late["input"] = resident(
                 input_kernel,
                 "input",
                 field_shape,
                 late["total"],
-                late["above"],
-                late["below"],
+                late["halo"],
                 taps,
                 grad_rows,
-                scratch=[pltpu.VMEM((2 * RADIUS, C, LANES), BF16)] + stencil_scratch,
+                scratch=stencil_scratch,
             )
-        elif step == 6:
+        elif step == 4:
             value, late["input"] = tie((value, late["input"]))
             late["input"] = jnp.transpose(late["input"][:, :, :COLS], (1, 0, 2))
-        elif step == 7:
+        elif step == 5:
             value, late["input"] = tie((value, late["input"]))
         return value
 
-    summed = all_sum(jnp.concatenate([g_part, h_part, sums_a + sums_b + sums_c], axis=1), hooks)
+    summed, summed_taps = all_sum(jnp.concatenate([g_part, h_part, sums_a + sums_b], axis=1), hooks)
     cells = ROWS * lax.axis_size("lat") * COLS * lax.axis_size("lon")
     g_sum, h_sum, grad_kernel, vectors = resident(
         functools.partial(final_kernel, factor=1.0 / math.sqrt(cells)),
         "final",
         (weight_shape, weight_shape, shape(TAPS, TAPS, C), shape(8, C)),
         summed,
+        summed_taps,
         chan,
         w_out_t,
     )

time: 130 us -> 123 us (0.946)
  waiting for transfers between devices: 30.3 us -> 18.7 us
  starting transfers between devices: 39.7 us -> 42.8 us
    ppermute x2, waiting for transfers between devices: 11.7 us -> 4.34 us  [lat_rows(): above = lax.ppermute(down, 'lat', [(i, i + 1) for i in range(count - 1)])]
    ppermute x12 -> x14, waiting for transfers between devices: 14.9 us -> 10.6 us  [swap(): lax.ppermute(value, ('lat', 'lon'), [(i, i ^ bits) for i in range(count)])]
    ppermute x12 -> x14, starting transfers between devices: 21.2 us -> 24.7 us  [swap(): lax.ppermute(value, ('lat', 'lon'), [(i, i ^ bits) for i in range(count)])]
    unnamed x29 -> x39, local copies, waits for them, and re-layouts: 6.04 us -> 6.93 us
    pallas_call x8 -> x10, Pallas kernels: 46.5 us -> 46.6 us  [resident(): pl.pallas_call(kernel, out_shape=out_shape, in_specs=[pl.BlockSpec(memory...]
  transfers between devices with their start and end apart: 20 -> 22, of which waited for: 11 -> 9; matrix products, arithmetic and copies ran while one was open for 4% -> 5% of each run, Pallas kernels for 27% -> 29%
where the time goes in v3:
time: 123 us; the launch traced here: 122 us
  Pallas kernels  46.6 us (38%)
  starting transfers between devices  42.8 us (35%)
  waiting for transfers between devices  18.7 us (15%)
  local copies, waits for them, and re-layouts  9.59 us (8%)
  other arithmetic  3.42 us (3%)
  between operations  1.26 us (1%)
    pallas_call x10, Pallas kernels, resident(): pl.pallas_call(kernel, out_shape=out_shape, in_specs=[pl.BlockSpec(memory...  46.6 us
    ppermute x14, starting transfers between devices, swap(): lax.ppermute(value, ('lat', 'lon'), [(i, i ^ bits) for i in range(count)])  24.7 us
    ppermute x14, waiting for transfers between devices, swap(): lax.ppermute(value, ('lat', 'lon'), [(i, i ^ bits) for i in range(count)])  10.6 us
    ppermute x2, starting transfers between devices, lat_rows(): above = lax.ppermute(down, 'lat', [(i, i + 1) for i in range(count - 1)])  10.4 us
    unnamed x39, local copies, waits for them, and re-layouts  6.93 us
    ppermute x4, starting transfers between devices, add_rims(): rims = ahead(tail) + behind(head)  5.08 us
    ppermute x2, waiting for transfers between devices, lat_rows(): above = lax.ppermute(down, 'lat', [(i, i + 1) for i in range(count - 1)])  4.34 us
    ppermute x4, waiting for transfers between devices, add_rims(): rims = ahead(tail) + behind(head)  3.73 us
  transfers between devices with their start and end apart: 22, of which 9 were waited for; matrix products, arithmetic and copies ran while one was open for 5% of the time, Pallas kernels for 29%

profile of v3, /device:TPU:1, one launch (start us, length us, event | category | flops | bytes accessed | tf_op | source)
XLA Modules:
  0.0 122.4 jit_solution(5181103198215901230)
XLA Ops:
  4.3 2.8 %collective-permute-start = (bf16[192,128]{1,0:T(8,128)(2,1)S(1)}, bf16[192,128]{1,0:T(8,128)(2,1)S(1)}, u32[]{:S(2)}, u32[]{:S(2)}) collective-permute-start(bf16[192,128]{1,0:T(8,128)(2,1)S(1)} %get-tuple-element.52), channel_id=1, source_target_pairs={{0,1},{1,2},{2,3},{3,4},{4,5},{5,6},{6,7},{7,8},{8,9},{9,10},{10,1... | collective-permute-start | bytes 147464 | tf_op jit(solution)/shard_map/ppermute | solution.py:448
  8.2 2.6 %collective-permute-done.1 = bf16[192,128]{1,0:T(8,128)(2,1)S(1)} collective-permute-done((bf16[192,128]{1,0:T(8,128)(2,1)S(1)}, bf16[192,128]{1,0:T(8,128)(2,1)S(1)}, u32[]{:S(2)}, u32[]{:S(2)}) %collective-permute-start.1) | collective-permute-done | bytes 49184 | tf_op jit(solution)/shard_map/ppermute | solution.py:448
  11.9 4.8 %collective-permute-start.2 = (bf16[192,1408]{1,0:T(8,128)(2,1)}, bf16[192,1408]{1,0:T(8,128)(2,1)S(1)}, u32[]{:S(2)}, u32[]{:S(2)}) collective-permute-start(bf16[192,1408]{1,0:T(8,128)(2,1)} %pad_maximum_fusion.3), channel_id=1, source_target_pairs={{0,16},{16,32},{32,48},{48,64},{64,80},{80,96},{96,112},{1,17},{17... | collective-permute-start | bytes 1622024 | tf_op jit(solution)/shard_map/ppermute | solution.py:456
  23.1 7.8 %mlp.1 = (bf16[4,768,512]{2,1,0:T(8,128)(2,1)S(1)}, f32[4,192,512]{2,1,0:T(8,128)S(1)}, f32[192,768]{1,0:T(8,128)S(1)}, f32[192,128]{1,0:T(8,128)S(1)}, bf16[4,192,512]{2,1,0:T(8,128)(2,1)S(1)}) custom-call(s32[192,4,450]{2,1,0:T(4,128)S(1)} %copy-done, bf16[12,4,450]{2,1,0:T(4,128)(2,1)S(1)} %copy-done.7, bf16[12,4,450]{2,1,0:T(4,128)(2,1)S(1)} %copy-done.8, ...), custom_call_target="tpu_custom_call" | custom-call | tf_op jit(solution)/shard_map/mlp/pallas_call | solution.py:37
  30.9 6.2 %conv_own.1 = (bf16[4,192,512]{2,1,0:T(8,128)(2,1)S(1)}, f32[4,192,512]{2,1,0:T(8,128)S(1)}) custom-call(bf16[4,192,512]{2,1,0:T(8,128)(2,1)S(1)} %get-tuple-element.51.own_ref, bf16[192,128]{1,0:T(8,128)(2,1)S(1)} %get-tuple-element.121.rims_ref, f32[192,128]{1,0:T(8,128)S(1)} %pad.9.taps_ref), custom_call_target="tpu_custom_call" | custom-call | tf_op jit(solution)/shard_map/conv_own/pallas_call | solution.py:37
  37.2 1.9 %collective-permute-done.2.above_ref = bf16[192,1408]{1,0:T(8,128)(2,1)S(1)} collective-permute-done((bf16[192,1408]{1,0:T(8,128)(2,1)}, bf16[192,1408]{1,0:T(8,128)(2,1)S(1)}, u32[]{:S(2)}, u32[]{:S(2)}) %collective-permute-start.2) | collective-permute-done | bytes 540704 | tf_op jit(solution)/shard_map/ppermute | solution.py:456
  39.1 8.7 %conv.1 = (bf16[10,192,512]{2,1,0:T(8,128)(2,1)S(1)}, bf16[4,192,512]{2,1,0:T(8,128)(2,1)S(1)}, bf16[192,128]{1,0:T(8,128)(2,1)S(1)}, bf16[192,128]{1,0:T(8,128)...) custom-call(bf16[4,192,512]{2,1,0:T(8,128)(2,1)S(1)} %get-tuple-elem, ...), custom_call_target="tpu_custom_call" | custom-call | tf_op jit(solution)/shard_map/conv/pallas_call | solution.py:37
  47.9 2.2 %collective-permute-start.6 = (bf16[192,128]{1,0:T(8,128)(2,1)S(1)}, bf16[192,128]{1,0:T(8,128)(2,1)S(1)}, u32[]{:S(2)}, u32[]{:S(2)}) collective-permute-start(bf16[192,128]{1,0:T(8,128)(2,1)S(1)} %get-tuple-element.66), channel_id=1, source_target_pairs={{1,0},{2,1},{3,2},{4,3},{5,4},{6,5},{7,6},{8,7},{9,8},{10,9},{11,1... | collective-permute-start | bytes 147464 | tf_op jit(solution)/shard_map/ppermute | solution.py:448
  50.2 2.4 %weight.1 = f32[192,768]{1,0:T(8,128)S(1)} custom-call(bf16[4,192,512]{2,1,0:T(8,128)(2,1)S(1)} %get-tuple-element.59.normed_in_ref, bf16[4,768,512]{2,1,0:T(8,128)(2,1)S(1)} %get-tuple-element.60.hidden_ref), custom_call_target="tpu_custom_call" | custom-call | tf_op jit(solution)/shard_map/weight/pallas_call | solution.py:37
  52.8 3.6 %collective-permute-start.4 = (f32[96,1664]{1,0:T(8,128)S(1)}, f32[96,1664]{1,0:T(8,128)S(1)}, u32[]{:S(2)}, u32[]{:S(2)}) collective-permute-start(f32[96,1664]{1,0:T(8,128)S(1)} %slice_select_fusion), channel_id=1, source_target_pairs={{0,1},{1,0},{2,3},{3,2},{4,5},{5,4},{6,7},{7,6},{8,9},{9,8},{10,11... | collective-permute-start | bytes 1916936 | tf_op jit(solution)/shard_map/ppermute | solution.py:463
  56.6 5.5 %collective-permute-start.10 = (bf16[192,1408]{1,0:T(8,128)(2,1)S(1)}, bf16[192,1408]{1,0:T(8,128)(2,1)S(1)}, u32[]{:S(2)}, u32[]{:S(2)}) collective-permute-start(bf16[192,1408]{1,0:T(8,128)(2,1)S(1)} %pad_maximum_fusion.6), channel_id=1, source_target_pairs={{0,16},{16,32},{32,48},{48,64},{64,80},{80,96},{96,112},{1,17},{17... | collective-permute-start | bytes 1622024 | tf_op jit(solution)/shard_map/ppermute | solution.py:456
  64.4 7.0 %taps.1 = f32[192,128]{1,0:T(8,128)S(1)} custom-call(bf16[10,192,512]{2,1,0:T(8,128)(2,1)S(1)} %get-tuple-element.68.field_ref, bf16[4,192,512]{2,1,0:T(8,128)(2,1)S(1)} %get-tuple-element.72.grad_ref.own_ref), custom_call_target="tpu_custom_call" | custom-call | tf_op jit(solution)/shard_map/taps/pallas_call | solution.py:37
  72.7 3.0 %collective-permute-start.8 = (bf16[24,1920]{1,0:T(8,128)(2,1)S(1)}, bf16[24,1920]{1,0:T(8,128)(2,1)S(1)}, u32[]{:S(2)}, u32[]{:S(2)}) collective-permute-start(bf16[24,1920]{1,0:T(8,128)(2,1)S(1)} %get-tuple-element.125), channel_id=1, source_target_pairs={{0,8},{1,9},{2,10},{3,11},{4,12},{5,13},{6,14},{7,15},{8,0},{9,1},... | collective-permute-start | bytes 276488 | tf_op jit(solution)/shard_map/ppermute | solution.py:463
  76.4 6.6 %input_own.1 = (bf16[4,192,512]{2,1,0:T(8,128)(2,1)}, f32[4,192,512]{2,1,0:T(8,128)S(1)}) custom-call(bf16[4,192,512]{2,1,0:T(8,128)(2,1)S(1)} %get-tuple-element.72.grad_ref.own_ref, bf16[192,128]{1,0:T(8,128)(2,1)S(1)} %get-tuple-element.119.rims_ref, f32[192,128]{1,0:T(8,128)S(1)} %pad.9.taps_ref), custom_call_target="tpu_custom_call" | custom-call | tf_op jit(solution)/shard_map/input_own/pallas_call | solution.py:37
  83.0 2.4 %collective-permute-done.10.above_ref = bf16[192,1408]{1,0:T(8,128)(2,1)S(1)} collective-permute-done((bf16[192,1408]{1,0:T(8,128)(2,1)S(1)}, bf16[192,1408]{1,0:T(8,128)(2,1)S(1)}, u32[]{:S(2)}, u32[]{:S(2)}) %collective-permute-start.10) | collective-permute-done | bytes 540704 | tf_op jit(solution)/shard_map/ppermute | solution.py:456
  85.9 4.4 %collective-permute-start.12 = (bf16[24,1920]{1,0:T(8,128)(2,1)S(1)}, bf16[24,1920]{1,0:T(8,128)(2,1)S(1)}, u32[]{:S(2)}, u32[]{:S(2)}) collective-permute-start(bf16[24,1920]{1,0:T(8,128)(2,1)S(1)} %reduce-precision_convert_fusion.2), channel_id=1, source_target_pairs={{0,32},{1,33},{2,34},{3,35},{4,36},{5,37},{6,38},{7,39},{8,40},{9,... | collective-permute-start | bytes 276488 | tf_op jit(solution)/shard_map/ppermute | solution.py:463
  90.3 2.4 %collective-permute-start.13 = (bf16[24,1920]{1,0:T(8,128)(2,1)S(1)}, bf16[24,1920]{1,0:T(8,128)(2,1)S(1)}, u32[]{:S(2)}, u32[]{:S(2)}) collective-permute-start(bf16[24,1920]{1,0:T(8,128)(2,1)S(1)} %reduce-precision_convert_fusion.2), channel_id=1, source_target_pairs={{0,64},{1,65},{2,66},{3,67},{4,68},{5,69},{6,70},{7,71},{8,72},{9,... | collective-permute-start | bytes 276488 | tf_op jit(solution)/shard_map/ppermute | solution.py:463
  92.9 4.1 %collective-permute-done.13 = bf16[24,1920]{1,0:T(8,128)(2,1)S(1)} collective-permute-done((bf16[24,1920]{1,0:T(8,128)(2,1)S(1)}, bf16[24,1920]{1,0:T(8,128)(2,1)S(1)}, u32[]{:S(2)}, u32[]{:S(2)}) %collective-permute-start.13) | collective-permute-done | bytes 92192 | tf_op jit(solution)/shard_map/ppermute | solution.py:463
  97.0 2.5 %collective-permute-done.14 = bf16[24,1920]{1,0:T(8,128)(2,1)S(1)} collective-permute-done((bf16[24,1920]{1,0:T(8,128)(2,1)S(1)}, bf16[24,1920]{1,0:T(8,128)(2,1)S(1)}, u32[]{:S(2)}, u32[]{:S(2)}) %collective-permute-start.14) | collective-permute-done | bytes 92192 | tf_op jit(solution)/shard_map/ppermute | solution.py:463
  99.7 3.8 %collective-permute-start.17 = (bf16[24,1920]{1,0:T(8,128)(2,1)S(1)}, bf16[24,1920]{1,0:T(8,128)(2,1)S(1)}, u32[]{:S(2)}, u32[]{:S(2)}) collective-permute-start(bf16[24,1920]{1,0:T(8,128)(2,1)S(1)} %reduce-precision_convert_fusion.1), channel_id=1, source_target_pairs={{0,18},{1,19},{2,16},{3,17},{4,22},{5,23},{6,20},{7,21},{8,26},{9,... | collective-permute-start | bytes 276488 | tf_op jit(solution)/shard_map/ppermute | solution.py:463
  103.5 5.0 %input.1 = bf16[4,192,512]{2,1,0:T(8,128)(2,1)S(1)} custom-call(f32[4,192,512]{2,1,0:T(8,128)S(1)} %get-tuple-element.80.total_ref, bf16[6,192,512]{2,1,0:T(8,128)(2,1)S(1)} %halo.1.field, f32[192,128]{1,0:T(8,128)S(1)} %pad.9.taps_ref, bf16[4,192,512]{2,1,0:T(8,128)(2,1)S(1)} %copy-done.4), custom_call_target="tpu_custom_call" | custom-call | tf_op jit(solution)/shard_map/input/pallas_call | solution.py:37
  108.6 2.3 %collective-permute-start.18 = (bf16[24,1920]{1,0:T(8,128)(2,1)S(1)}, bf16[24,1920]{1,0:T(8,128)(2,1)S(1)}, u32[]{:S(2)}, u32[]{:S(2)}) collective-permute-start(bf16[24,1920]{1,0:T(8,128)(2,1)S(1)} %reduce-precision_convert_fusion), channel_id=1, source_target_pairs={{0,12},{1,13},{2,14},{3,15},{4,8},{5,9},{6,10},{7,11},{8,4},{9,5},... | collective-permute-start | bytes 276488 | tf_op jit(solution)/shard_map/ppermute | solution.py:463
  113.3 2.6 %collective-permute-done.19 = bf16[24,1920]{1,0:T(8,128)(2,1)S(1)} collective-permute-done((bf16[24,1920]{1,0:T(8,128)(2,1)S(1)}, bf16[24,1920]{1,0:T(8,128)(2,1)S(1)}, u32[]{:S(2)}, u32[]{:S(2)}) %collective-permute-start.19) | collective-permute-done | bytes 92192 | tf_op jit(solution)/shard_map/ppermute | solution.py:463
  116.0 2.9 %collective-permute-start.21 = (bf16[96,1920]{1,0:T(8,128)(2,1)S(1)}, bf16[96,1920]{1,0:T(8,128)(2,1)S(1)}, u32[]{:S(2)}, u32[]{:S(2)}) collective-permute-start(bf16[96,1920]{1,0:T(8,128)(2,1)S(1)} %pad_maximum_fusion.7), channel_id=1, source_target_pairs={{0,1},{1,0},{2,3},{3,2},{4,5},{5,4},{6,7},{7,6},{8,9},{9,8},{10,11... | collective-permute-start | bytes 1105928 | tf_op jit(solution)/shard_map/ppermute | solution.py:463
  (108 shorter events, 23.4 us)
Async XLA Ops:
  4.3 3.9 %collective-permute-start = (bf16[192,128]{1,0:T(8,128)(2,1)S(1)}, bf16[192,128]{1,0:T(8,128)(2,1)S(1)}, u32[]{:S(2)}, u32[]{:S(2)}) collective-permute-start(bf16[192,128]{1,0:T(8,128)(2,1)S(1)} %get-tuple-element.52), channel_id=1, source_target_pairs={{0,1},{1,2},{2,3},{3,4},{4,5},{5,6},{6,7},{7,8},{8,9},{9,10},{10,1... | collective-permute-start | bytes 147464 | tf_op jit(solution)/shard_map/ppermute | solution.py:448
  7.1 3.8 %collective-permute-start.1 = (bf16[192,128]{1,0:T(8,128)(2,1)S(1)}, bf16[192,128]{1,0:T(8,128)(2,1)S(1)}, u32[]{:S(2)}, u32[]{:S(2)}) collective-permute-start(bf16[192,128]{1,0:T(8,128)(2,1)S(1)} %get-tuple-element.53), channel_id=1, source_target_pairs={{1,0},{2,1},{3,2},{4,3},{5,4},{6,5},{7,6},{8,7},{9,8},{10,9},{11,1... | collective-permute-start | bytes 147464 | tf_op jit(solution)/shard_map/ppermute | solution.py:448
  7.1 11.9 %copy-start.13 = (f32[192,7,7]{0,2,1:T(8,128)S(1)}, f32[192,7,7]{0,2,1:T(8,128)}, u32[]{:S(2)}) copy-start(f32[192,7,7]{0,2,1:T(8,128)} %param.22) | copy-start | bytes 112900
  11.9 27.2 %collective-permute-start.2 = (bf16[192,1408]{1,0:T(8,128)(2,1)}, bf16[192,1408]{1,0:T(8,128)(2,1)S(1)}, u32[]{:S(2)}, u32[]{:S(2)}) collective-permute-start(bf16[192,1408]{1,0:T(8,128)(2,1)} %pad_maximum_fusion.3), channel_id=1, source_target_pairs={{0,16},{16,32},{32,48},{48,64},{64,80},{80,96},{96,112},{1,17},{17... | collective-permute-start | bytes 1622024 | tf_op jit(solution)/shard_map/ppermute | solution.py:456
  17.6 21.6 %collective-permute-start.3 = (bf16[192,1408]{1,0:T(8,128)(2,1)}, bf16[192,1408]{1,0:T(8,128)(2,1)}, u32[]{:S(2)}, u32[]{:S(2)}) collective-permute-start(bf16[192,1408]{1,0:T(8,128)(2,1)} %pad_maximum_fusion.4), channel_id=1, source_target_pairs={{16,0},{32,16},{48,32},{64,48},{80,64},{96,80},{112,96},{17,1},{33... | collective-permute-start | bytes 1622024 | tf_op jit(solution)/shard_map/ppermute | solution.py:457
  47.8 8.7 %collective-permute-start.5 = (bf16[192,128]{1,0:T(8,128)(2,1)S(1)}, bf16[192,128]{1,0:T(8,128)(2,1)S(1)}, u32[]{:S(2)}, u32[]{:S(2)}) collective-permute-start(bf16[192,128]{1,0:T(8,128)(2,1)S(1)} %get-tuple-element.65), channel_id=1, source_target_pairs={{0,1},{1,2},{2,3},{3,4},{4,5},{5,6},{6,7},{7,8},{8,9},{9,10},{10,1... | collective-permute-start | bytes 147464 | tf_op jit(solution)/shard_map/ppermute | solution.py:448
  47.9 8.6 %collective-permute-start.6 = (bf16[192,128]{1,0:T(8,128)(2,1)S(1)}, bf16[192,128]{1,0:T(8,128)(2,1)S(1)}, u32[]{:S(2)}, u32[]{:S(2)}) collective-permute-start(bf16[192,128]{1,0:T(8,128)(2,1)S(1)} %get-tuple-element.66), channel_id=1, source_target_pairs={{1,0},{2,1},{3,2},{4,3},{5,4},{6,5},{7,6},{8,7},{9,8},{10,9},{11,1... | collective-permute-start | bytes 147464 | tf_op jit(solution)/shard_map/ppermute | solution.py:448
  52.8 11.5 %collective-permute-start.4 = (f32[96,1664]{1,0:T(8,128)S(1)}, f32[96,1664]{1,0:T(8,128)S(1)}, u32[]{:S(2)}, u32[]{:S(2)}) collective-permute-start(f32[96,1664]{1,0:T(8,128)S(1)} %slice_select_fusion), channel_id=1, source_target_pairs={{0,1},{1,0},{2,3},{3,2},{4,5},{5,4},{6,7},{7,6},{8,9},{9,8},{10,11... | collective-permute-start | bytes 1916936 | tf_op jit(solution)/shard_map/ppermute | solution.py:463
  56.6 28.8 %collective-permute-start.10 = (bf16[192,1408]{1,0:T(8,128)(2,1)S(1)}, bf16[192,1408]{1,0:T(8,128)(2,1)S(1)}, u32[]{:S(2)}, u32[]{:S(2)}) collective-permute-start(bf16[192,1408]{1,0:T(8,128)(2,1)S(1)} %pad_maximum_fusion.6), channel_id=1, source_target_pairs={{0,16},{16,32},{32,48},{48,64},{64,80},{80,96},{96,112},{1,17},{17... | collective-permute-start | bytes 1622024 | tf_op jit(solution)/shard_map/ppermute | solution.py:456
  63.0 22.4 %collective-permute-start.11 = (bf16[192,1408]{1,0:T(8,128)(2,1)}, bf16[192,1408]{1,0:T(8,128)(2,1)S(1)}, u32[]{:S(2)}, u32[]{:S(2)}) collective-permute-start(bf16[192,1408]{1,0:T(8,128)(2,1)} %pad_maximum_fusion.5), channel_id=1, source_target_pairs={{16,0},{32,16},{48,32},{64,48},{80,64},{96,80},{112,96},{17,1},{33... | collective-permute-start | bytes 1622024 | tf_op jit(solution)/shard_map/ppermute | solution.py:457
  72.4 13.3 %collective-permute-start.7 = (bf16[24,1920]{1,0:T(8,128)(2,1)S(1)}, bf16[24,1920]{1,0:T(8,128)(2,1)S(1)}, u32[]{:S(2)}, u32[]{:S(2)}) collective-permute-start(bf16[24,1920]{1,0:T(8,128)(2,1)S(1)} %get-tuple-element.124), channel_id=1, source_target_pairs={{0,4},{1,5},{2,6},{3,7},{4,0},{5,1},{6,2},{7,3},{8,12},{9,13},{10,... | collective-permute-start | bytes 276488 | tf_op jit(solution)/shard_map/ppermute | solution.py:463
  72.7 13.1 %collective-permute-start.8 = (bf16[24,1920]{1,0:T(8,128)(2,1)S(1)}, bf16[24,1920]{1,0:T(8,128)(2,1)S(1)}, u32[]{:S(2)}, u32[]{:S(2)}) collective-permute-start(bf16[24,1920]{1,0:T(8,128)(2,1)S(1)} %get-tuple-element.125), channel_id=1, source_target_pairs={{0,8},{1,9},{2,10},{3,11},{4,12},{5,13},{6,14},{7,15},{8,0},{9,1},... | collective-permute-start | bytes 276488 | tf_op jit(solution)/shard_map/ppermute | solution.py:463
  75.7 10.1 %collective-permute-start.9 = (bf16[24,1920]{1,0:T(8,128)(2,1)S(1)}, bf16[24,1920]{1,0:T(8,128)(2,1)S(1)}, u32[]{:S(2)}, u32[]{:S(2)}) collective-permute-start(bf16[24,1920]{1,0:T(8,128)(2,1)S(1)} %get-tuple-element.126), channel_id=1, source_target_pairs={{0,12},{1,13},{2,14},{3,15},{4,8},{5,9},{6,10},{7,11},{8,4},{9,5},... | collective-permute-start | bytes 276488 | tf_op jit(solution)/shard_map/ppermute | solution.py:463
  85.7 17.8 %copy-start.4 = (bf16[4,192,512]{2,1,0:T(8,128)(2,1)S(1)}, bf16[4,192,512]{2,1,0:T(8,128)(2,1)}, u32[]{:S(2)}) copy-start(bf16[4,192,512]{2,1,0:T(8,128)(2,1)} %copy-done.3) | copy-start | bytes 2359300
  85.9 7.1 %collective-permute-start.12 = (bf16[24,1920]{1,0:T(8,128)(2,1)S(1)}, bf16[24,1920]{1,0:T(8,128)(2,1)S(1)}, u32[]{:S(2)}, u32[]{:S(2)}) collective-permute-start(bf16[24,1920]{1,0:T(8,128)(2,1)S(1)} %reduce-precision_convert_fusion.2), channel_id=1, source_target_pairs={{0,32},{1,33},{2,34},{3,35},{4,36},{5,37},{6,38},{7,39},{8,40},{9,... | collective-permute-start | bytes 276488 | tf_op jit(solution)/shard_map/ppermute | solution.py:463
  90.3 6.7 %collective-permute-start.13 = (bf16[24,1920]{1,0:T(8,128)(2,1)S(1)}, bf16[24,1920]{1,0:T(8,128)(2,1)S(1)}, u32[]{:S(2)}, u32[]{:S(2)}) collective-permute-start(bf16[24,1920]{1,0:T(8,128)(2,1)S(1)} %reduce-precision_convert_fusion.2), channel_id=1, source_target_pairs={{0,64},{1,65},{2,66},{3,67},{4,68},{5,69},{6,70},{7,71},{8,72},{9,... | collective-permute-start | bytes 276488 | tf_op jit(solution)/shard_map/ppermute | solution.py:463
  92.7 6.7 %collective-permute-start.14 = (bf16[24,1920]{1,0:T(8,128)(2,1)S(1)}, bf16[24,1920]{1,0:T(8,128)(2,1)S(1)}, u32[]{:S(2)}, u32[]{:S(2)}) collective-permute-start(bf16[24,1920]{1,0:T(8,128)(2,1)S(1)} %reduce-precision_convert_fusion.2), channel_id=1, source_target_pairs={{0,96},{1,97},{2,98},{3,99},{4,100},{5,101},{6,102},{7,103},{8,104... | collective-permute-start | bytes 276488 | tf_op jit(solution)/shard_map/ppermute | solution.py:463
  99.6 8.9 %collective-permute-start.15 = (bf16[24,1920]{1,0:T(8,128)(2,1)S(1)}, bf16[24,1920]{1,0:T(8,128)(2,1)S(1)}, u32[]{:S(2)}, u32[]{:S(2)}) collective-permute-start(bf16[24,1920]{1,0:T(8,128)(2,1)S(1)} %reduce-precision_convert_fusion.1), channel_id=1, source_target_pairs={{0,2},{1,3},{2,0},{3,1},{4,6},{5,7},{6,4},{7,5},{8,10},{9,11},{10,... | collective-permute-start | bytes 276488 | tf_op jit(solution)/shard_map/ppermute | solution.py:463
  99.7 8.9 %collective-permute-start.16 = (bf16[24,1920]{1,0:T(8,128)(2,1)S(1)}, bf16[24,1920]{1,0:T(8,128)(2,1)S(1)}, u32[]{:S(2)}, u32[]{:S(2)}) collective-permute-start(bf16[24,1920]{1,0:T(8,128)(2,1)S(1)} %reduce-precision_convert_fusion.1), channel_id=1, source_target_pairs={{0,16},{1,17},{2,18},{3,19},{4,20},{5,21},{6,22},{7,23},{8,24},{9,... | collective-permute-start | bytes 276488 | tf_op jit(solution)/shard_map/ppermute | solution.py:463
  99.7 8.8 %collective-permute-start.17 = (bf16[24,1920]{1,0:T(8,128)(2,1)S(1)}, bf16[24,1920]{1,0:T(8,128)(2,1)S(1)}, u32[]{:S(2)}, u32[]{:S(2)}) collective-permute-start(bf16[24,1920]{1,0:T(8,128)(2,1)S(1)} %reduce-precision_convert_fusion.1), channel_id=1, source_target_pairs={{0,18},{1,19},{2,16},{3,17},{4,22},{5,23},{6,20},{7,21},{8,26},{9,... | collective-permute-start | bytes 276488 | tf_op jit(solution)/shard_map/ppermute | solution.py:463
  108.6 4.7 %collective-permute-start.18 = (bf16[24,1920]{1,0:T(8,128)(2,1)S(1)}, bf16[24,1920]{1,0:T(8,128)(2,1)S(1)}, u32[]{:S(2)}, u32[]{:S(2)}) collective-permute-start(bf16[24,1920]{1,0:T(8,128)(2,1)S(1)} %reduce-precision_convert_fusion), channel_id=1, source_target_pairs={{0,12},{1,13},{2,14},{3,15},{4,8},{5,9},{6,10},{7,11},{8,4},{9,5},... | collective-permute-start | bytes 276488 | tf_op jit(solution)/shard_map/ppermute | solution.py:463
  110.9 5.0 %collective-permute-start.19 = (bf16[24,1920]{1,0:T(8,128)(2,1)S(1)}, bf16[24,1920]{1,0:T(8,128)(2,1)S(1)}, u32[]{:S(2)}, u32[]{:S(2)}) collective-permute-start(bf16[24,1920]{1,0:T(8,128)(2,1)S(1)} %reduce-precision_convert_fusion), channel_id=1, source_target_pairs={{0,8},{1,9},{2,10},{3,11},{4,12},{5,13},{6,14},{7,15},{8,0},{9,1},... | collective-permute-start | bytes 276488 | tf_op jit(solution)/shard_map/ppermute | solution.py:463
  110.9 5.0 %collective-permute-start.20 = (bf16[24,1920]{1,0:T(8,128)(2,1)S(1)}, bf16[24,1920]{1,0:T(8,128)(2,1)S(1)}, u32[]{:S(2)}, u32[]{:S(2)}) collective-permute-start(bf16[24,1920]{1,0:T(8,128)(2,1)S(1)} %reduce-precision_convert_fusion), channel_id=1, source_target_pairs={{0,4},{1,5},{2,6},{3,7},{4,0},{5,1},{6,2},{7,3},{8,12},{9,13},{10,... | collective-permute-start | bytes 276488 | tf_op jit(solution)/shard_map/ppermute | solution.py:463
  116.0 4.4 %collective-permute-start.21 = (bf16[96,1920]{1,0:T(8,128)(2,1)S(1)}, bf16[96,1920]{1,0:T(8,128)(2,1)S(1)}, u32[]{:S(2)}, u32[]{:S(2)}) collective-permute-start(bf16[96,1920]{1,0:T(8,128)(2,1)S(1)} %pad_maximum_fusion.7), channel_id=1, source_target_pairs={{0,1},{1,0},{2,3},{3,2},{4,5},{5,4},{6,7},{7,6},{8,9},{9,8},{10,11... | collective-permute-start | bytes 1105928 | tf_op jit(solution)/shard_map/ppermute | solution.py:463
  (17 other events, 97.5 us)

commit v4 on v3

--- a/solution.py
+++ b/solution.py
@@ -274,7 +274,7 @@
             emit(chans, i, total)
         return carry
 
-    lax.fori_loop(0, C // CH, body, 0)
+    lax.fori_loop(0, C // CH, body, 0, unroll=2)
 
 
 def own_kernel(own_ref, rims_ref, taps_ref, filled_ref, total_ref, wide_taps, partial, *, flip):
@@ -399,7 +399,7 @@
         sums_ref[chans, :] = sums
         return carry
 
-    lax.fori_loop(0, C // CH, body, 0, unroll=2)
+    lax.fori_loop(0, C // CH, body, 0, unroll=4)
 
 
 def halo_kernel(above_ref, below_ref, field_ref):
@@ -649,7 +649,7 @@
             value = jnp.concatenate([value, *parts], axis=1)
             value, late["own"] = tie((value, late["own"]))
             late["total"] = over_own(late["own"], rims, True, "input_own")[1]
-        elif step == 2:
+        elif step == 3:
             above, below, late["total"] = tie((late["above"], late["below"], late["total"]))
             halo = resident(
                 halo_kernel,
@@ -660,7 +660,7 @@
                 cost=0,
             )
             value, late["total"], late["halo"] = tie((value, late["total"], halo))
-        elif step == 3:
+        elif step == 4:
             value, late["total"] = tie((value, late["total"]))
             late["input"] = resident(
                 input_kernel,
@@ -672,11 +672,9 @@
                 grad_rows,
                 scratch=stencil_scratch,
             )
-        elif step == 4:
+        elif step == 5:
             value, late["input"] = tie((value, late["input"]))
             late["input"] = jnp.transpose(late["input"][:, :, :COLS], (1, 0, 2))
-        elif step == 5:
-            value, late["input"] = tie((value, late["input"]))
         return value
 
     summed, summed_taps = all_sum(jnp.concatenate([g_part, h_part, sums_a + sums_b], axis=1), hooks)

time: 123 us -> 118 us (0.959)
  waiting for transfers between devices: 18.7 us -> 12.3 us
  starting transfers between devices: 42.8 us -> 48.9 us
  Pallas kernels: 46.6 us -> 43.2 us
    ppermute x14, starting transfers between devices: 24.7 us -> 30.3 us  [swap(): lax.ppermute(value, ('lat', 'lon'), [(i, i ^ bits) for i in range(count)])]
    ppermute x14, waiting for transfers between devices: 10.6 us -> 6.94 us  [swap(): lax.ppermute(value, ('lat', 'lon'), [(i, i ^ bits) for i in range(count)])]
    pallas_call x10, Pallas kernels: 46.6 us -> 43.2 us  [resident(): pl.pallas_call(kernel, out_shape=out_shape, in_specs=[pl.BlockSpec(memory...]
    ppermute x2, waiting for transfers between devices: 4.34 us -> 1.63 us  [lat_rows(): above = lax.ppermute(down, 'lat', [(i, i + 1) for i in range(count - 1)])]
    unnamed x39 -> x29, local copies, waits for them, and re-layouts: 6.93 us -> 6.04 us
  transfers between devices with their start and end apart: 22 -> 22, of which waited for: 9 -> 8; matrix products, arithmetic and copies ran while one was open for 5% -> 5% of each run, Pallas kernels for 29% -> 27%
where the time goes in v4:
time: 118 us
  starting transfers between devices  48.9 us (41%)
  Pallas kernels  43.2 us (37%)
  waiting for transfers between devices  12.3 us (10%)
  local copies, waits for them, and re-layouts  9.52 us (8%)
  other arithmetic  2.61 us (2%)
  between operations  1.23 us (1%)
    pallas_call x10, Pallas kernels, resident(): pl.pallas_call(kernel, out_shape=out_shape, in_specs=[pl.BlockSpec(memory...  43.2 us
    ppermute x14, starting transfers between devices, swap(): lax.ppermute(value, ('lat', 'lon'), [(i, i ^ bits) for i in range(count)])  30.3 us
    ppermute x2, starting transfers between devices, lat_rows(): above = lax.ppermute(down, 'lat', [(i, i + 1) for i in range(count - 1)])  10.8 us
    ppermute x14, waiting for transfers between devices, swap(): lax.ppermute(value, ('lat', 'lon'), [(i, i ^ bits) for i in range(count)])  6.94 us
    unnamed x29, local copies, waits for them, and re-layouts  6.04 us
    ppermute x4, starting transfers between devices, add_rims(): rims = ahead(tail) + behind(head)  5.08 us
    ppermute x4, waiting for transfers between devices, add_rims(): rims = ahead(tail) + behind(head)  3.74 us
    ppermute x2, starting transfers between devices, lat_rows(): below = lax.ppermute(up, 'lat', [(i + 1, i) for i in range(count - 1)])  2.75 us
  transfers between devices with their start and end apart: 22, of which 8 were waited for; matrix products, arithmetic and copies ran while one was open for 5% of the time, Pallas kernels for 27%

profile of v4, /device:TPU:1, one launch (start us, length us, event | category | flops | bytes accessed | tf_op | source)
XLA Modules:
  0.0 117.8 jit_solution(271946986156677803)
XLA Ops:
  4.3 2.8 %collective-permute-start = (bf16[192,128]{1,0:T(8,128)(2,1)S(1)}, bf16[192,128]{1,0:T(8,128)(2,1)S(1)}, u32[]{:S(2)}, u32[]{:S(2)}) collective-permute-start(bf16[192,128]{1,0:T(8,128)(2,1)S(1)} %get-tuple-element.50), channel_id=1, source_target_pairs={{0,1},{1,2},{2,3},{3,4},{4,5},{5,6},{6,7},{7,8},{8,9},{9,10},{10,1... | collective-permute-start | bytes 147464 | tf_op jit(solution)/shard_map/ppermute | solution.py:448
  8.2 2.6 %collective-permute-done.1 = bf16[192,128]{1,0:T(8,128)(2,1)S(1)} collective-permute-done((bf16[192,128]{1,0:T(8,128)(2,1)S(1)}, bf16[192,128]{1,0:T(8,128)(2,1)S(1)}, u32[]{:S(2)}, u32[]{:S(2)}) %collective-permute-start.1) | collective-permute-done | bytes 49184 | tf_op jit(solution)/shard_map/ppermute | solution.py:448
  11.9 4.8 %collective-permute-start.2 = (bf16[192,1408]{1,0:T(8,128)(2,1)}, bf16[192,1408]{1,0:T(8,128)(2,1)S(1)}, u32[]{:S(2)}, u32[]{:S(2)}) collective-permute-start(bf16[192,1408]{1,0:T(8,128)(2,1)} %pad_maximum_fusion.3), channel_id=1, source_target_pairs={{0,16},{16,32},{32,48},{48,64},{64,80},{80,96},{96,112},{1,17},{17... | collective-permute-start | bytes 1622024 | tf_op jit(solution)/shard_map/ppermute | solution.py:456
  17.6 1.5 %collective-permute-start.3 = (bf16[192,1408]{1,0:T(8,128)(2,1)}, bf16[192,1408]{1,0:T(8,128)(2,1)}, u32[]{:S(2)}, u32[]{:S(2)}) collective-permute-start(bf16[192,1408]{1,0:T(8,128)(2,1)} %pad_maximum_fusion.4), channel_id=1, source_target_pairs={{16,0},{32,16},{48,32},{64,48},{80,64},{96,80},{112,96},{17,1},{33... | collective-permute-start | bytes 1622024 | tf_op jit(solution)/shard_map/ppermute | solution.py:457
  23.9 7.8 %mlp.1 = (bf16[4,768,512]{2,1,0:T(8,128)(2,1)S(1)}, f32[4,192,512]{2,1,0:T(8,128)S(1)}, f32[192,768]{1,0:T(8,128)S(1)}, f32[192,128]{1,0:T(8,128)S(1)}, bf16[4,192,512]{2,1,0:T(8,128)(2,1)S(1)}) custom-call(s32[192,4,450]{2,1,0:T(4,128)S(1)} %copy-done, bf16[12,4,450]{2,1,0:T(4,128)(2,1)S(1)} %copy-done.5, bf16[12,4,450]{2,1,0:T(4,128)(2,1)S(1)} %copy-done.6, ...), custom_call_target="tpu_custom_call" | custom-call | tf_op jit(solution)/shard_map/mlp/pallas_call | solution.py:37
  31.8 5.7 %conv_own.1 = (bf16[4,192,512]{2,1,0:T(8,128)(2,1)S(1)}, f32[4,192,512]{2,1,0:T(8,128)S(1)}) custom-call(bf16[4,192,512]{2,1,0:T(8,128)(2,1)S(1)} %get-tuple-element.49.own_ref, bf16[192,128]{1,0:T(8,128)(2,1)S(1)} %get-tuple-element.119.rims_ref, f32[192,128]{1,0:T(8,128)S(1)} %pad.9.taps_ref), custom_call_target="tpu_custom_call" | custom-call | tf_op jit(solution)/shard_map/conv_own/pallas_call | solution.py:37
  37.5 1.6 %collective-permute-done.2.above_ref = bf16[192,1408]{1,0:T(8,128)(2,1)S(1)} collective-permute-done((bf16[192,1408]{1,0:T(8,128)(2,1)}, bf16[192,1408]{1,0:T(8,128)(2,1)S(1)}, u32[]{:S(2)}, u32[]{:S(2)}) %collective-permute-start.2) | collective-permute-done | bytes 540704 | tf_op jit(solution)/shard_map/ppermute | solution.py:456
  39.1 8.5 %conv.1 = (bf16[10,192,512]{2,1,0:T(8,128)(2,1)S(1)}, bf16[4,192,512]{2,1,0:T(8,128)(2,1)S(1)}, bf16[192,128]{1,0:T(8,128)(2,1)S(1)}, bf16[192,128]{1,0:T(8,128)...) custom-call(bf16[4,192,512]{2,1,0:T(8,128)(2,1)S(1)} %get-tuple-elem, ...), custom_call_target="tpu_custom_call" | custom-call | tf_op jit(solution)/shard_map/conv/pallas_call | solution.py:37
  47.9 2.0 %collective-permute-start.6 = (bf16[192,128]{1,0:T(8,128)(2,1)S(1)}, bf16[192,128]{1,0:T(8,128)(2,1)S(1)}, u32[]{:S(2)}, u32[]{:S(2)}) collective-permute-start(bf16[192,128]{1,0:T(8,128)(2,1)S(1)} %get-tuple-element.64), channel_id=1, source_target_pairs={{1,0},{2,1},{3,2},{4,3},{5,4},{6,5},{7,6},{8,7},{9,8},{10,9},{11,1... | collective-permute-start | bytes 147464 | tf_op jit(solution)/shard_map/ppermute | solution.py:448
  50.0 2.4 %weight.1 = f32[192,768]{1,0:T(8,128)S(1)} custom-call(bf16[4,192,512]{2,1,0:T(8,128)(2,1)S(1)} %get-tuple-element.57.normed_in_ref, bf16[4,768,512]{2,1,0:T(8,128)(2,1)S(1)} %get-tuple-element.58.hidden_ref), custom_call_target="tpu_custom_call" | custom-call | tf_op jit(solution)/shard_map/weight/pallas_call | solution.py:37
  52.6 3.9 %collective-permute-start.4 = (f32[96,1664]{1,0:T(8,128)S(1)}, f32[96,1664]{1,0:T(8,128)S(1)}, u32[]{:S(2)}, u32[]{:S(2)}) collective-permute-start(f32[96,1664]{1,0:T(8,128)S(1)} %slice_select_fusion), channel_id=1, source_target_pairs={{0,1},{1,0},{2,3},{3,2},{4,5},{5,4},{6,7},{7,6},{8,9},{9,8},{10,11... | collective-permute-start | bytes 1916936 | tf_op jit(solution)/shard_map/ppermute | solution.py:463
  58.3 5.6 %taps.1 = f32[192,128]{1,0:T(8,128)S(1)} custom-call(bf16[10,192,512]{2,1,0:T(8,128)(2,1)S(1)} %get-tuple-element.66.field_ref, bf16[4,192,512]{2,1,0:T(8,128)(2,1)S(1)} %get-tuple-element.70.grad_ref.own_ref), custom_call_target="tpu_custom_call" | custom-call | tf_op jit(solution)/shard_map/taps/pallas_call | solution.py:37
  64.2 3.0 %collective-permute-start.8 = (bf16[24,1920]{1,0:T(8,128)(2,1)S(1)}, bf16[24,1920]{1,0:T(8,128)(2,1)S(1)}, u32[]{:S(2)}, u32[]{:S(2)}) collective-permute-start(bf16[24,1920]{1,0:T(8,128)(2,1)S(1)} %get-tuple-element.123), channel_id=1, source_target_pairs={{0,8},{1,9},{2,10},{3,11},{4,12},{5,13},{6,14},{7,15},{8,0},{9,1},... | collective-permute-start | bytes 276488 | tf_op jit(solution)/shard_map/ppermute | solution.py:463
  68.0 5.9 %collective-permute-start.13 = (bf16[192,1408]{1,0:T(8,128)(2,1)S(1)}, bf16[192,1408]{1,0:T(8,128)(2,1)S(1)}, u32[]{:S(2)}, u32[]{:S(2)}) collective-permute-start(bf16[192,1408]{1,0:T(8,128)(2,1)S(1)} %pad_maximum_fusion.6), channel_id=1, source_target_pairs={{0,16},{16,32},{32,48},{48,64},{64,80},{80,96},{96,112},{1,17},{17... | collective-permute-start | bytes 1622024 | tf_op jit(solution)/shard_map/ppermute | solution.py:456
  74.2 5.3 %collective-permute-start.10 = (bf16[24,1920]{1,0:T(8,128)(2,1)S(1)}, bf16[24,1920]{1,0:T(8,128)(2,1)S(1)}, u32[]{:S(2)}, u32[]{:S(2)}) collective-permute-start(bf16[24,1920]{1,0:T(8,128)(2,1)S(1)} %get-tuple-element.116), channel_id=1, source_target_pairs={{0,32},{1,33},{2,34},{3,35},{4,36},{5,37},{6,38},{7,39},{8,40},{9,... | collective-permute-start | bytes 276488 | tf_op jit(solution)/shard_map/ppermute | solution.py:463
  79.6 2.7 %collective-permute-start.11 = (bf16[24,1920]{1,0:T(8,128)(2,1)S(1)}, bf16[24,1920]{1,0:T(8,128)(2,1)S(1)}, u32[]{:S(2)}, u32[]{:S(2)}) collective-permute-start(bf16[24,1920]{1,0:T(8,128)(2,1)S(1)} %get-tuple-element.116), channel_id=1, source_target_pairs={{0,64},{1,65},{2,66},{3,67},{4,68},{5,69},{6,70},{7,71},{8,72},{9,... | collective-permute-start | bytes 276488 | tf_op jit(solution)/shard_map/ppermute | solution.py:463
  82.3 5.7 %input_own.1 = (bf16[4,192,512]{2,1,0:T(8,128)(2,1)}, f32[4,192,512]{2,1,0:T(8,128)S(1)}) custom-call(bf16[4,192,512]{2,1,0:T(8,128)(2,1)S(1)} %get-tuple-element.70.grad_ref.own_ref, bf16[192,128]{1,0:T(8,128)(2,1)S(1)} %get-tuple-element.115.rims_ref, f32[192,128]{1,0:T(8,128)S(1)} %pad.9.taps_ref), custom_call_target="tpu_custom_call" | custom-call | tf_op jit(solution)/shard_map/input_own/pallas_call | solution.py:37
  89.1 8.0 %collective-permute-start.16 = (bf16[24,1920]{1,0:T(8,128)(2,1)S(1)}, bf16[24,1920]{1,0:T(8,128)(2,1)S(1)}, u32[]{:S(2)}, u32[]{:S(2)}) collective-permute-start(bf16[24,1920]{1,0:T(8,128)(2,1)S(1)} %reduce-precision_convert_fusion.1), channel_id=1, source_target_pairs={{0,16},{1,17},{2,18},{3,19},{4,20},{5,21},{6,22},{7,23},{8,24},{9,... | collective-permute-start | bytes 276488 | tf_op jit(solution)/shard_map/ppermute | solution.py:463
  97.1 3.6 %collective-permute-done.16 = bf16[24,1920]{1,0:T(8,128)(2,1)S(1)} collective-permute-done((bf16[24,1920]{1,0:T(8,128)(2,1)S(1)}, bf16[24,1920]{1,0:T(8,128)(2,1)S(1)}, u32[]{:S(2)}, u32[]{:S(2)}) %collective-permute-start.16) | collective-permute-done | bytes 92192 | tf_op jit(solution)/shard_map/ppermute | solution.py:463
  100.7 2.4 %collective-permute-done.17 = bf16[24,1920]{1,0:T(8,128)(2,1)S(1)} collective-permute-done((bf16[24,1920]{1,0:T(8,128)(2,1)S(1)}, bf16[24,1920]{1,0:T(8,128)(2,1)S(1)}, u32[]{:S(2)}, u32[]{:S(2)}) %collective-permute-start.17) | collective-permute-done | bytes 92192 | tf_op jit(solution)/shard_map/ppermute | solution.py:463
  103.1 3.3 %collective-permute-start.18 = (bf16[24,1920]{1,0:T(8,128)(2,1)S(1)}, bf16[24,1920]{1,0:T(8,128)(2,1)S(1)}, u32[]{:S(2)}, u32[]{:S(2)}) collective-permute-start(bf16[24,1920]{1,0:T(8,128)(2,1)S(1)} %reduce-precision_convert_fusion), channel_id=1, source_target_pairs={{0,12},{1,13},{2,14},{3,15},{4,8},{5,9},{6,10},{7,11},{8,4},{9,5},... | collective-permute-start | bytes 276488 | tf_op jit(solution)/shard_map/ppermute | solution.py:463
  107.1 4.6 %input.1 = bf16[4,192,512]{2,1,0:T(8,128)(2,1)S(1)} custom-call(f32[4,192,512]{2,1,0:T(8,128)S(1)} %get-tuple-element.78.total_ref, bf16[6,192,512]{2,1,0:T(8,128)(2,1)S(1)} %halo.1.field, f32[192,128]{1,0:T(8,128)S(1)} %pad.9.taps_ref, bf16[4,192,512]{2,1,0:T(8,128)(2,1)S(1)} %get-tuple-element.80.grad_ref), custom_call_target="tpu_custom_call" | custom-call | tf_op jit(solution)/shard_map/input/pallas_call | solution.py:37
  111.9 2.3 %collective-permute-start.21 = (bf16[96,1920]{1,0:T(8,128)(2,1)S(1)}, bf16[96,1920]{1,0:T(8,128)(2,1)S(1)}, u32[]{:S(2)}, u32[]{:S(2)}) collective-permute-start(bf16[96,1920]{1,0:T(8,128)(2,1)S(1)} %pad_maximum_fusion.7), channel_id=1, source_target_pairs={{0,1},{1,0},{2,3},{3,2},{4,5},{5,4},{6,7},{7,6},{8,9},{9,8},{10,11... | collective-permute-start | bytes 1105928 | tf_op jit(solution)/shard_map/ppermute | solution.py:463
  114.3 1.5 %copy.44 = bf16[192,4,450]{2,1,0:T(4,128)(2,1)} copy(bf16[192,4,450]{2,0,1:T(8,128)(2,1)S(1)} %slice_bitcast_fusion) | data formatting | bytes 1382400
  (97 shorter events, 18.8 us)
Async XLA Ops:
  4.3 3.9 %collective-permute-start = (bf16[192,128]{1,0:T(8,128)(2,1)S(1)}, bf16[192,128]{1,0:T(8,128)(2,1)S(1)}, u32[]{:S(2)}, u32[]{:S(2)}) collective-permute-start(bf16[192,128]{1,0:T(8,128)(2,1)S(1)} %get-tuple-element.50), channel_id=1, source_target_pairs={{0,1},{1,2},{2,3},{3,4},{4,5},{5,6},{6,7},{7,8},{8,9},{9,10},{10,1... | collective-permute-start | bytes 147464 | tf_op jit(solution)/shard_map/ppermute | solution.py:448
  7.1 3.8 %collective-permute-start.1 = (bf16[192,128]{1,0:T(8,128)(2,1)S(1)}, bf16[192,128]{1,0:T(8,128)(2,1)S(1)}, u32[]{:S(2)}, u32[]{:S(2)}) collective-permute-start(bf16[192,128]{1,0:T(8,128)(2,1)S(1)} %get-tuple-element.51), channel_id=1, source_target_pairs={{1,0},{2,1},{3,2},{4,3},{5,4},{6,5},{7,6},{8,7},{9,8},{10,9},{11,1... | collective-permute-start | bytes 147464 | tf_op jit(solution)/shard_map/ppermute | solution.py:448
  11.0 10.8 %copy-start = (s32[192,4,450]{2,1,0:T(4,128)S(1)}, s32[192,4,450]{2,1,0:T(4,128)}, u32[]{:S(2)}) copy-start(s32[192,4,450]{2,1,0:T(4,128)} %words_hbm.2) | copy-start | bytes 4147204
  11.0 10.8 %copy-start.1 = (bf16[768,192]{0,1:T(8,128)(2,1)S(1)}, bf16[768,192]{0,1:T(8,128)(2,1)}, u32[]{:S(2)}) copy-start(bf16[768,192]{0,1:T(8,128)(2,1)} %param.27) | copy-start | bytes 884740
  11.9 27.2 %collective-permute-start.2 = (bf16[192,1408]{1,0:T(8,128)(2,1)}, bf16[192,1408]{1,0:T(8,128)(2,1)S(1)}, u32[]{:S(2)}, u32[]{:S(2)}) collective-permute-start(bf16[192,1408]{1,0:T(8,128)(2,1)} %pad_maximum_fusion.3), channel_id=1, source_target_pairs={{0,16},{16,32},{32,48},{48,64},{64,80},{80,96},{96,112},{1,17},{17... | collective-permute-start | bytes 1622024 | tf_op jit(solution)/shard_map/ppermute | solution.py:456
  17.6 21.6 %collective-permute-start.3 = (bf16[192,1408]{1,0:T(8,128)(2,1)}, bf16[192,1408]{1,0:T(8,128)(2,1)}, u32[]{:S(2)}, u32[]{:S(2)}) collective-permute-start(bf16[192,1408]{1,0:T(8,128)(2,1)} %pad_maximum_fusion.4), channel_id=1, source_target_pairs={{16,0},{32,16},{48,32},{64,48},{80,64},{96,80},{112,96},{17,1},{33... | collective-permute-start | bytes 1622024 | tf_op jit(solution)/shard_map/ppermute | solution.py:457
  47.6 8.9 %collective-permute-start.5 = (bf16[192,128]{1,0:T(8,128)(2,1)S(1)}, bf16[192,128]{1,0:T(8,128)(2,1)S(1)}, u32[]{:S(2)}, u32[]{:S(2)}) collective-permute-start(bf16[192,128]{1,0:T(8,128)(2,1)S(1)} %get-tuple-element.63), channel_id=1, source_target_pairs={{0,1},{1,2},{2,3},{3,4},{4,5},{5,6},{6,7},{7,8},{8,9},{9,10},{10,1... | collective-permute-start | bytes 147464 | tf_op jit(solution)/shard_map/ppermute | solution.py:448
  47.9 8.6 %collective-permute-start.6 = (bf16[192,128]{1,0:T(8,128)(2,1)S(1)}, bf16[192,128]{1,0:T(8,128)(2,1)S(1)}, u32[]{:S(2)}, u32[]{:S(2)}) collective-permute-start(bf16[192,128]{1,0:T(8,128)(2,1)S(1)} %get-tuple-element.64), channel_id=1, source_target_pairs={{1,0},{2,1},{3,2},{4,3},{5,4},{6,5},{7,6},{8,7},{9,8},{10,9},{11,1... | collective-permute-start | bytes 147464 | tf_op jit(solution)/shard_map/ppermute | solution.py:448
  52.6 5.6 %collective-permute-start.4 = (f32[96,1664]{1,0:T(8,128)S(1)}, f32[96,1664]{1,0:T(8,128)S(1)}, u32[]{:S(2)}, u32[]{:S(2)}) collective-permute-start(f32[96,1664]{1,0:T(8,128)S(1)} %slice_select_fusion), channel_id=1, source_target_pairs={{0,1},{1,0},{2,3},{3,2},{4,5},{5,4},{6,7},{7,6},{8,9},{9,8},{10,11... | collective-permute-start | bytes 1916936 | tf_op jit(solution)/shard_map/ppermute | solution.py:463
  56.6 31.4 %collective-permute-start.14 = (bf16[192,1408]{1,0:T(8,128)(2,1)S(1)}, bf16[192,1408]{1,0:T(8,128)(2,1)S(1)}, u32[]{:S(2)}, u32[]{:S(2)}) collective-permute-start(bf16[192,1408]{1,0:T(8,128)(2,1)S(1)} %pad_maximum_fusion.5), channel_id=1, source_target_pairs={{16,0},{32,16},{48,32},{64,48},{80,64},{96,80},{112,96},{17,1},{33... | collective-permute-start | bytes 1622024 | tf_op jit(solution)/shard_map/ppermute | solution.py:457
  64.0 9.9 %collective-permute-start.7 = (bf16[24,1920]{1,0:T(8,128)(2,1)S(1)}, bf16[24,1920]{1,0:T(8,128)(2,1)S(1)}, u32[]{:S(2)}, u32[]{:S(2)}) collective-permute-start(bf16[24,1920]{1,0:T(8,128)(2,1)S(1)} %get-tuple-element.122), channel_id=1, source_target_pairs={{0,4},{1,5},{2,6},{3,7},{4,0},{5,1},{6,2},{7,3},{8,12},{9,13},{10,... | collective-permute-start | bytes 276488 | tf_op jit(solution)/shard_map/ppermute | solution.py:463
  64.2 9.7 %collective-permute-start.8 = (bf16[24,1920]{1,0:T(8,128)(2,1)S(1)}, bf16[24,1920]{1,0:T(8,128)(2,1)S(1)}, u32[]{:S(2)}, u32[]{:S(2)}) collective-permute-start(bf16[24,1920]{1,0:T(8,128)(2,1)S(1)} %get-tuple-element.123), channel_id=1, source_target_pairs={{0,8},{1,9},{2,10},{3,11},{4,12},{5,13},{6,14},{7,15},{8,0},{9,1},... | collective-permute-start | bytes 276488 | tf_op jit(solution)/shard_map/ppermute | solution.py:463
  67.2 6.9 %collective-permute-start.9 = (bf16[24,1920]{1,0:T(8,128)(2,1)S(1)}, bf16[24,1920]{1,0:T(8,128)(2,1)S(1)}, u32[]{:S(2)}, u32[]{:S(2)}) collective-permute-start(bf16[24,1920]{1,0:T(8,128)(2,1)S(1)} %get-tuple-element.124), channel_id=1, source_target_pairs={{0,12},{1,13},{2,14},{3,15},{4,8},{5,9},{6,10},{7,11},{8,4},{9,5},... | collective-permute-start | bytes 276488 | tf_op jit(solution)/shard_map/ppermute | solution.py:463
  68.0 20.1 %collective-permute-start.13 = (bf16[192,1408]{1,0:T(8,128)(2,1)S(1)}, bf16[192,1408]{1,0:T(8,128)(2,1)S(1)}, u32[]{:S(2)}, u32[]{:S(2)}) collective-permute-start(bf16[192,1408]{1,0:T(8,128)(2,1)S(1)} %pad_maximum_fusion.6), channel_id=1, source_target_pairs={{0,16},{16,32},{32,48},{48,64},{64,80},{80,96},{96,112},{1,17},{17... | collective-permute-start | bytes 1622024 | tf_op jit(solution)/shard_map/ppermute | solution.py:456
  74.2 14.2 %collective-permute-start.10 = (bf16[24,1920]{1,0:T(8,128)(2,1)S(1)}, bf16[24,1920]{1,0:T(8,128)(2,1)S(1)}, u32[]{:S(2)}, u32[]{:S(2)}) collective-permute-start(bf16[24,1920]{1,0:T(8,128)(2,1)S(1)} %get-tuple-element.116), channel_id=1, source_target_pairs={{0,32},{1,33},{2,34},{3,35},{4,36},{5,37},{6,38},{7,39},{8,40},{9,... | collective-permute-start | bytes 276488 | tf_op jit(solution)/shard_map/ppermute | solution.py:463
  79.6 8.8 %collective-permute-start.11 = (bf16[24,1920]{1,0:T(8,128)(2,1)S(1)}, bf16[24,1920]{1,0:T(8,128)(2,1)S(1)}, u32[]{:S(2)}, u32[]{:S(2)}) collective-permute-start(bf16[24,1920]{1,0:T(8,128)(2,1)S(1)} %get-tuple-element.116), channel_id=1, source_target_pairs={{0,64},{1,65},{2,66},{3,67},{4,68},{5,69},{6,70},{7,71},{8,72},{9,... | collective-permute-start | bytes 276488 | tf_op jit(solution)/shard_map/ppermute | solution.py:463
  82.3 6.6 %collective-permute-start.12 = (bf16[24,1920]{1,0:T(8,128)(2,1)S(1)}, bf16[24,1920]{1,0:T(8,128)(2,1)S(1)}, u32[]{:S(2)}, u32[]{:S(2)}) collective-permute-start(bf16[24,1920]{1,0:T(8,128)(2,1)S(1)} %get-tuple-element.116), channel_id=1, source_target_pairs={{0,96},{1,97},{2,98},{3,99},{4,100},{5,101},{6,102},{7,103},{8,104... | collective-permute-start | bytes 276488 | tf_op jit(solution)/shard_map/ppermute | solution.py:463
  89.0 8.1 %collective-permute-start.15 = (bf16[24,1920]{1,0:T(8,128)(2,1)S(1)}, bf16[24,1920]{1,0:T(8,128)(2,1)S(1)}, u32[]{:S(2)}, u32[]{:S(2)}) collective-permute-start(bf16[24,1920]{1,0:T(8,128)(2,1)S(1)} %reduce-precision_convert_fusion.1), channel_id=1, source_target_pairs={{0,2},{1,3},{2,0},{3,1},{4,6},{5,7},{6,4},{7,5},{8,10},{9,11},{10,... | collective-permute-start | bytes 276488 | tf_op jit(solution)/shard_map/ppermute | solution.py:463
  89.1 11.6 %collective-permute-start.16 = (bf16[24,1920]{1,0:T(8,128)(2,1)S(1)}, bf16[24,1920]{1,0:T(8,128)(2,1)S(1)}, u32[]{:S(2)}, u32[]{:S(2)}) collective-permute-start(bf16[24,1920]{1,0:T(8,128)(2,1)S(1)} %reduce-precision_convert_fusion.1), channel_id=1, source_target_pairs={{0,16},{1,17},{2,18},{3,19},{4,20},{5,21},{6,22},{7,23},{8,24},{9,... | collective-permute-start | bytes 276488 | tf_op jit(solution)/shard_map/ppermute | solution.py:463
  97.1 6.0 %collective-permute-start.17 = (bf16[24,1920]{1,0:T(8,128)(2,1)S(1)}, bf16[24,1920]{1,0:T(8,128)(2,1)S(1)}, u32[]{:S(2)}, u32[]{:S(2)}) collective-permute-start(bf16[24,1920]{1,0:T(8,128)(2,1)S(1)} %reduce-precision_convert_fusion.1), channel_id=1, source_target_pairs={{0,18},{1,19},{2,16},{3,17},{4,22},{5,23},{6,20},{7,21},{8,26},{9,... | collective-permute-start | bytes 276488 | tf_op jit(solution)/shard_map/ppermute | solution.py:463
  103.1 8.6 %collective-permute-start.18 = (bf16[24,1920]{1,0:T(8,128)(2,1)S(1)}, bf16[24,1920]{1,0:T(8,128)(2,1)S(1)}, u32[]{:S(2)}, u32[]{:S(2)}) collective-permute-start(bf16[24,1920]{1,0:T(8,128)(2,1)S(1)} %reduce-precision_convert_fusion), channel_id=1, source_target_pairs={{0,12},{1,13},{2,14},{3,15},{4,8},{5,9},{6,10},{7,11},{8,4},{9,5},... | collective-permute-start | bytes 276488 | tf_op jit(solution)/shard_map/ppermute | solution.py:463
  106.5 5.3 %collective-permute-start.19 = (bf16[24,1920]{1,0:T(8,128)(2,1)S(1)}, bf16[24,1920]{1,0:T(8,128)(2,1)S(1)}, u32[]{:S(2)}, u32[]{:S(2)}) collective-permute-start(bf16[24,1920]{1,0:T(8,128)(2,1)S(1)} %reduce-precision_convert_fusion), channel_id=1, source_target_pairs={{0,8},{1,9},{2,10},{3,11},{4,12},{5,13},{6,14},{7,15},{8,0},{9,1},... | collective-permute-start | bytes 276488 | tf_op jit(solution)/shard_map/ppermute | solution.py:463
  106.5 5.3 %collective-permute-start.20 = (bf16[24,1920]{1,0:T(8,128)(2,1)S(1)}, bf16[24,1920]{1,0:T(8,128)(2,1)S(1)}, u32[]{:S(2)}, u32[]{:S(2)}) collective-permute-start(bf16[24,1920]{1,0:T(8,128)(2,1)S(1)} %reduce-precision_convert_fusion), channel_id=1, source_target_pairs={{0,4},{1,5},{2,6},{3,7},{4,0},{5,1},{6,2},{7,3},{8,12},{9,13},{10,... | collective-permute-start | bytes 276488 | tf_op jit(solution)/shard_map/ppermute | solution.py:463
  111.9 3.9 %collective-permute-start.21 = (bf16[96,1920]{1,0:T(8,128)(2,1)S(1)}, bf16[96,1920]{1,0:T(8,128)(2,1)S(1)}, u32[]{:S(2)}, u32[]{:S(2)}) collective-permute-start(bf16[96,1920]{1,0:T(8,128)(2,1)S(1)} %pad_maximum_fusion.7), channel_id=1, source_target_pairs={{0,1},{1,0},{2,3},{3,2},{4,5},{5,4},{6,7},{7,6},{8,9},{9,8},{10,11... | collective-permute-start | bytes 1105928 | tf_op jit(solution)/shard_map/ppermute | solution.py:463
  (12 other events, 71.4 us)
